TPU v7x, 32 devices: a whole 2x2x4 slice. The times are simulated.
32 devices in a mesh: rep: 4 (over y, x), shard: 8 (over z, core).
Axes of the slice: x: 2, y: 2, z: 4, core: 2. Of those that a mesh axis runs over, the one named last changes fastest.
Arguments:
- streams: bfloat16 [5120, 4, 2048], P(('rep', 'shard')), may hold values from -6 to 6
- cotangent: bfloat16 [5120, 4, 2048], P(('rep', 'shard')), may hold values from -6 to 6
- lengths: int32 [4, 2], P('rep'), may hold values from 1 to 1024, 1280 in all within a row
- packed_at: int32 [4, 1280], P('rep'), may hold values from 0 to 1279, each once within a row
- query_weight: bfloat16 [2048, 2048], P('shard'), may hold values from -0.125 to 0.125
- key_weight: bfloat16 [2048, 2048], P('shard'), may hold values from -0.125 to 0.125
- value_weight: bfloat16 [2048, 2048], P('shard'), may hold values from -0.125 to 0.125
- output_weight: bfloat16 [2048, 2048], P('shard'), may hold values from -0.5 to 0.5
- gate_weight: bfloat16 [2048, 8192], P('shard'), may hold values from -0.125 to 0.125
- up_weight: bfloat16 [2048, 8192], P('shard'), may hold values from -0.125 to 0.125
- down_weight: bfloat16 [8192, 2048], P('shard'), may hold values from -0.0625 to 0.0625
- mixing_weight: bfloat16 [2, 2048, 6], P(None, 'shard'), may hold values from -0.125 to 0.125
- mixing_static: float32 [2, 4, 6], replicated, may hold values from -0.5 to 0.5
Outputs:
- streams_out: bfloat16 [5120, 4, 2048], P(('rep', 'shard'))
- grad_streams: float32 [5120, 4, 2048], P(('rep', 'shard'))
- grad_query: float32 [2048, 2048], P('shard')
- grad_key: float32 [2048, 2048], P('shard')
- grad_value: float32 [2048, 2048], P('shard')
- grad_output: float32 [2048, 2048], P('shard')
- grad_gate: float32 [2048, 8192], P('shard')
- grad_up: float32 [2048, 8192], P('shard')
- grad_down: float32 [8192, 2048], P('shard')
- grad_mixing: float32 [2, 2048, 6], P(None, 'shard')
- grad_static: float32 [2, 4, 6], replicated
Inputs may be any that keep to these rules, and one draw needn't show every extreme that they name: `lengths`: each row sums to 1280. `packed_at`: each row is a permutation of 0 to 1279.
All inputs are finite; a program needn't handle non-finite values.
Results may differ from a plain program's by a relative error of at most 0.024.
Values may be sent and summed in bfloat16 or wider, within the bound.
No kernel may reach another device: no remote copies, remote signals or barrier semaphores. Data moves between devices by JAX's collectives and lax.ppermute only.
A program may use at most 576 MiB of HBM per device.

v0:
```python
import math

import jax
import jax.numpy as jnp
from jax import lax
from jax.sharding import PartitionSpec as P

HEADS = 16


EPSILON = 1e-05
NEGATIVE = -1e30
HIGHEST = lax.Precision.HIGHEST


def layer_norm(values):
    centred = values - jnp.mean(values, axis=-1, keepdims=True)
    spread = jnp.mean(centred * centred, axis=-1, keepdims=True)
    return centred * lax.rsqrt(spread + EPSILON)


def mixing(stream_values, weight, static):
    normed = layer_norm(stream_values)
    coefficients = static + jnp.tanh(jnp.einsum("tnd,dc->tnc", normed, weight, precision=HIGHEST))
    entering = jnp.einsum("tn,tnd->td", coefficients[:, :, 0], stream_values, precision=HIGHEST)
    carried = jnp.einsum("tnj,tnd->tjd", coefficients[:, :, 1:-1], stream_values, precision=HIGHEST)
    return (layer_norm(entering), carried, coefficients[:, :, -1])


def sequence_meta(ordering, lengths):
    ending = jnp.cumsum(lengths)
    segment = jnp.sum((ordering[:, None] >= ending[None, :]).astype(jnp.int32), axis=1)
    opening = ending - lengths
    chosen = segment[:, None] == jnp.arange(lengths.shape[0], dtype=jnp.int32)[None, :]
    first_place = jnp.sum(jnp.where(chosen, opening[None, :], 0), axis=1)
    return (segment, ordering - first_place)


def rope_tables(position, head_width):
    middle = head_width // 2
    frequency = jnp.exp(
        jnp.arange(middle, dtype=jnp.float32) * (-2.0 * math.log(10000.0) / head_width)
    )
    angles = position.astype(jnp.float32)[:, None] * frequency[None, :]
    angles = jnp.concatenate([angles, angles], axis=1)
    return (jnp.cos(angles), jnp.sin(angles))


def rotate(values, cosine, sine_part):
    middle = values.shape[-1] // 2
    turned = jnp.concatenate([-values[..., middle:], values[..., :middle]], axis=-1)
    return values * cosine + turned * sine_part


def rotate_back(gradient, cosine, sine_part):
    middle = gradient.shape[-1] // 2
    scaled = gradient * sine_part
    turned = jnp.concatenate([scaled[..., middle:], -scaled[..., :middle]], axis=-1)
    return gradient * cosine + turned


def block_scores(
    query_block,
    key_rot,
    segment,
    ordering,
    query_segment,
    query_order,
    key_start,
    block_rows,
    score_scale,
):
    key_block = lax.dynamic_slice_in_dim(key_rot, key_start, block_rows, 0)
    key_segment = lax.dynamic_slice_in_dim(segment, key_start, block_rows, 0)
    key_order = lax.dynamic_slice_in_dim(ordering, key_start, block_rows, 0)
    raw_scores = (
        jnp.einsum("qhd,khd->hqk", query_block, key_block, preferred_element_type=jnp.float32)
        * score_scale
    )
    allowed = (query_segment[:, None] == key_segment[None, :]) & (
        key_order[None, :] <= query_order[:, None]
    )
    return jnp.where(allowed[None, :, :], raw_scores, NEGATIVE)


def head_forward(
    query_rot, key_rot, value_rows, segment, ordering, lower_bounds, upper_bounds, block_rows
):
    score_scale = query_rot.shape[-1] ** (-0.5)
    heads_here = query_rot.shape[1]
    block_total = query_rot.shape[0] // block_rows

    def one_block(block_index):
        row_start = block_index * block_rows
        query_block = lax.dynamic_slice_in_dim(query_rot, row_start, block_rows, 0)
        query_segment = lax.dynamic_slice_in_dim(segment, row_start, block_rows, 0)
        query_order = lax.dynamic_slice_in_dim(ordering, row_start, block_rows, 0)

        def scores_of(key_index):
            return block_scores(
                query_block,
                key_rot,
                segment,
                ordering,
                query_segment,
                query_order,
                key_index * block_rows,
                block_rows,
                score_scale,
            )

        def top_step(key_index, running):
            running_top, running_total = running
            scores = scores_of(key_index)
            new_top = jnp.maximum(running_top, jnp.max(scores, axis=-1))
            running_total = running_total * jnp.exp(running_top - new_top) + jnp.sum(
                jnp.exp(scores - new_top[:, :, None]), axis=-1
            )
            return (new_top, running_total)

        starting = (
            jnp.full((heads_here, block_rows), NEGATIVE, jnp.float32),
            jnp.zeros((heads_here, block_rows), jnp.float32),
        )
        running_top, running_total = lax.fori_loop(
            lower_bounds[block_index], upper_bounds[block_index], top_step, starting
        )
        log_total = running_top + jnp.log(running_total)

        def value_step(key_index, gathered):
            weights = jnp.exp(scores_of(key_index) - log_total[:, :, None]).astype(jnp.bfloat16)
            value_block = lax.dynamic_slice_in_dim(
                value_rows, key_index * block_rows, block_rows, 0
            )
            return gathered + jnp.einsum(
                "hqk,khd->qhd", weights, value_block, preferred_element_type=jnp.float32
            )

        empty = jnp.zeros((block_rows, heads_here, query_rot.shape[-1]), jnp.float32)
        attended = lax.fori_loop(
            lower_bounds[block_index], upper_bounds[block_index], value_step, empty
        )
        return (attended, log_total)

    attended, log_totals = lax.map(one_block, jnp.arange(block_total, dtype=jnp.int32))
    return (attended.reshape(query_rot.shape), log_totals)


def head_backward(
    query_rot,
    key_rot,
    value_rows,
    grad_attended,
    log_totals,
    segment,
    ordering,
    lower_bounds,
    upper_bounds,
    block_rows,
):
    score_scale = query_rot.shape[-1] ** (-0.5)
    heads_here = query_rot.shape[1]
    block_total = query_rot.shape[0] // block_rows

    def block_step(block_index, totals):
        grad_query, grad_key, grad_value = totals
        row_start = block_index * block_rows
        query_block = lax.dynamic_slice_in_dim(query_rot, row_start, block_rows, 0)
        query_segment = lax.dynamic_slice_in_dim(segment, row_start, block_rows, 0)
        query_order = lax.dynamic_slice_in_dim(ordering, row_start, block_rows, 0)
        grad_block = lax.dynamic_slice_in_dim(grad_attended, row_start, block_rows, 0)
        log_total = log_totals[block_index]

        def pieces_of(key_index):
            key_start = key_index * block_rows
            scores = block_scores(
                query_block,
                key_rot,
                segment,
                ordering,
                query_segment,
                query_order,
                key_start,
                block_rows,
                score_scale,
            )
            weights = jnp.exp(scores - log_total[:, :, None])
            value_block = lax.dynamic_slice_in_dim(value_rows, key_start, block_rows, 0)
            grad_weights = jnp.einsum(
                "qhd,khd->hqk", grad_block, value_block, preferred_element_type=jnp.float32
            )
            return (weights, grad_weights, key_start)

        def centre_step(key_index, centre):
            weights, grad_weights, key_start = pieces_of(key_index)
            return centre + jnp.sum(weights * grad_weights, axis=-1)

        centre = lax.fori_loop(
            lower_bounds[block_index],
            upper_bounds[block_index],
            centre_step,
            jnp.zeros((heads_here, block_rows), jnp.float32),
        )

        def grad_step(key_index, inner):
            query_part, key_all, value_all = inner
            weights, grad_weights, key_start = pieces_of(key_index)
            grad_scores = (weights * (grad_weights - centre[:, :, None])).astype(jnp.bfloat16)
            key_block = lax.dynamic_slice_in_dim(key_rot, key_start, block_rows, 0)
            query_part = (
                query_part
                + jnp.einsum(
                    "hqk,khd->qhd", grad_scores, key_block, preferred_element_type=jnp.float32
                )
                * score_scale
            )
            key_piece = (
                jnp.einsum(
                    "hqk,qhd->khd", grad_scores, query_block, preferred_element_type=jnp.float32
                )
                * score_scale
            )
            value_piece = jnp.einsum(
                "hqk,qhd->khd",
                weights.astype(jnp.bfloat16),
                grad_block,
                preferred_element_type=jnp.float32,
            )
            key_all = lax.dynamic_update_slice_in_dim(
                key_all,
                lax.dynamic_slice_in_dim(key_all, key_start, block_rows, 0) + key_piece,
                key_start,
                0,
            )
            value_all = lax.dynamic_update_slice_in_dim(
                value_all,
                lax.dynamic_slice_in_dim(value_all, key_start, block_rows, 0) + value_piece,
                key_start,
                0,
            )
            return (query_part, key_all, value_all)

        empty = jnp.zeros((block_rows, heads_here, query_rot.shape[-1]), jnp.float32)
        query_part, grad_key, grad_value = lax.fori_loop(
            lower_bounds[block_index],
            upper_bounds[block_index],
            grad_step,
            (empty, grad_key, grad_value),
        )
        grad_query = lax.dynamic_update_slice_in_dim(grad_query, query_part, row_start, 0)
        return (grad_query, grad_key, grad_value)

    zero_rows = jnp.zeros(query_rot.shape, jnp.float32)
    return lax.fori_loop(0, block_total, block_step, (zero_rows, zero_rows, zero_rows))


def reduce_gradient(operand_pairs):
    columns = []
    for left_side, right_side in operand_pairs:
        columns.append(
            jnp.einsum("tr,tc->rc", left_side, right_side, preferred_element_type=jnp.float32)
        )
    group_sum = lax.psum_scatter(
        jnp.concatenate(columns, axis=1).astype(jnp.bfloat16),
        "shard",
        scatter_dimension=0,
        tiled=True,
    )
    return lax.psum(group_sum, "rep").astype(jnp.float32)


def per_device(
    streams,
    cotangent,
    lengths,
    packed_at,
    query_weight,
    key_weight,
    value_weight,
    output_weight,
    gate_weight,
    up_weight,
    down_weight,
    mixing_weight,
    mixing_static,
):
    query_full, key_full, value_full, output_full, mixing_full = (
        lax.all_gather(query_weight, "shard", axis=0, tiled=True),
        lax.all_gather(key_weight, "shard", axis=0, tiled=True),
        lax.all_gather(value_weight, "shard", axis=0, tiled=True),
        lax.all_gather(output_weight, "shard", axis=0, tiled=True),
        lax.all_gather(mixing_weight, "shard", axis=1, tiled=True),
    )
    gate_full, up_full, down_full = (
        lax.all_gather(gate_weight, "shard", axis=0, tiled=True),
        lax.all_gather(up_weight, "shard", axis=0, tiled=True),
        lax.all_gather(down_weight, "shard", axis=0, tiled=True),
    )
    token_rows, stream_count, width = streams.shape
    heads_all = HEADS
    head_width = width // heads_all
    ordering = packed_at[0]
    group_rows = ordering.shape[0]
    block_total = lengths.shape[1]
    block_rows = group_rows // block_total
    segment, position = sequence_meta(ordering, lengths[0])
    lower_bounds = jnp.zeros((block_total,), jnp.int32)
    upper_bounds = jnp.full((block_total,), block_total, jnp.int32)
    cosine, sine_part = rope_tables(position, head_width)
    cosine = cosine[:, None, :]
    sine_part = sine_part[:, None, :]
    streams_float = streams.astype(jnp.float32)
    mixing_float = mixing_full.astype(jnp.float32)
    (normed, carried, beta_first), pull_first = jax.vjp(
        mixing, streams_float, mixing_float[0], mixing_static[0]
    )
    attention_in = normed.astype(jnp.bfloat16)
    projected = jnp.stack(
        [
            jnp.dot(attention_in, weight_full, preferred_element_type=jnp.float32).astype(
                jnp.bfloat16
            )
            for weight_full in (query_full, key_full, value_full)
        ],
        axis=1,
    )
    projected = projected.reshape(token_rows, 3, heads_all, head_width)
    head_rows = lax.all_to_all(projected, "shard", split_axis=2, concat_axis=0, tiled=True)
    query_rot = rotate(head_rows[:, 0].astype(jnp.float32), cosine, sine_part).astype(jnp.bfloat16)
    key_rot = rotate(head_rows[:, 1].astype(jnp.float32), cosine, sine_part).astype(jnp.bfloat16)
    value_rows = head_rows[:, 2]
    attended, log_totals = head_forward(
        query_rot, key_rot, value_rows, segment, ordering, lower_bounds, upper_bounds, block_rows
    )
    attended = attended.astype(jnp.bfloat16)
    token_attended = lax.all_to_all(
        attended, "shard", split_axis=0, concat_axis=1, tiled=True
    ).reshape(token_rows, width)
    branch = jnp.dot(token_attended, output_full, preferred_element_type=jnp.float32)
    middle = carried + beta_first[:, :, None] * branch[:, None, :]
    (normed_second, carried_second, beta_second), pull_second = jax.vjp(
        mixing, middle, mixing_float[1], mixing_static[1]
    )
    ffn_in = normed_second.astype(jnp.bfloat16)
    gate_pre = jnp.dot(ffn_in, gate_full, preferred_element_type=jnp.float32)
    up_pre = jnp.dot(ffn_in, up_full, preferred_element_type=jnp.float32)
    sigmoid_gate = jax.nn.sigmoid(gate_pre)
    activated = (gate_pre * sigmoid_gate * up_pre).astype(jnp.bfloat16)
    ffn_out = jnp.dot(activated, down_full, preferred_element_type=jnp.float32)
    result = carried_second + beta_second[:, :, None] * ffn_out[:, None, :]
    grad_result = cotangent.astype(jnp.float32)
    grad_beta_second = jnp.sum(grad_result * ffn_out[:, None, :], axis=-1)
    grad_down_in = jnp.sum(grad_result * beta_second[:, :, None], axis=1).astype(jnp.bfloat16)
    grad_activated = jnp.einsum(
        "tc,fc->tf", grad_down_in, down_full, preferred_element_type=jnp.float32
    )
    grad_gate = (
        grad_activated * up_pre * sigmoid_gate * (1.0 + gate_pre * (1.0 - sigmoid_gate))
    ).astype(jnp.bfloat16)
    grad_up = (grad_activated * gate_pre * sigmoid_gate).astype(jnp.bfloat16)
    grad_ffn_in = jnp.einsum(
        "tf,df->td", grad_gate, gate_full, preferred_element_type=jnp.float32
    ) + jnp.einsum("tf,df->td", grad_up, up_full, preferred_element_type=jnp.float32)
    grad_middle, grad_mixing_second, grad_static_second = pull_second(
        (grad_ffn_in, grad_result, grad_beta_second)
    )
    grad_beta_first = jnp.sum(grad_middle * branch[:, None, :], axis=-1)
    grad_branch = jnp.sum(grad_middle * beta_first[:, :, None], axis=1).astype(jnp.bfloat16)
    grad_token_attended = jnp.einsum(
        "tc,dc->td", grad_branch, output_full, preferred_element_type=jnp.float32
    ).astype(jnp.bfloat16)
    grad_heads = lax.all_to_all(
        grad_token_attended.reshape(token_rows, heads_all, head_width),
        "shard",
        split_axis=1,
        concat_axis=0,
        tiled=True,
    )
    grad_query_rot, grad_key_rot, grad_value_rows = head_backward(
        query_rot,
        key_rot,
        value_rows,
        grad_heads,
        log_totals,
        segment,
        ordering,
        lower_bounds,
        upper_bounds,
        block_rows,
    )
    grad_projected = jnp.stack(
        [
            rotate_back(grad_query_rot, cosine, sine_part),
            rotate_back(grad_key_rot, cosine, sine_part),
            grad_value_rows,
        ],
        axis=1,
    ).astype(jnp.bfloat16)
    grad_tokens = lax.all_to_all(
        grad_projected, "shard", split_axis=0, concat_axis=2, tiled=True
    ).reshape(token_rows, 3, width)
    grad_attention_in = jnp.einsum(
        "tc,dc->td", grad_tokens[:, 0], query_full, preferred_element_type=jnp.float32
    )
    grad_attention_in = grad_attention_in + jnp.einsum(
        "tc,dc->td", grad_tokens[:, 1], key_full, preferred_element_type=jnp.float32
    )
    grad_attention_in = grad_attention_in + jnp.einsum(
        "tc,dc->td", grad_tokens[:, 2], value_full, preferred_element_type=jnp.float32
    )
    grad_streams, grad_mixing_first, grad_static_first = pull_first(
        (grad_attention_in, grad_middle, grad_beta_first)
    )
    down_rows = reduce_gradient(((activated, grad_down_in),))
    gate_up_rows = reduce_gradient(((ffn_in, jnp.concatenate([grad_gate, grad_up], axis=1)),))
    attention_rows = reduce_gradient(
        ((attention_in, grad_tokens.reshape(token_rows, 3 * width)), (token_attended, grad_branch))
    )
    mixing_sums, static_sums = lax.psum(
        (
            jnp.stack([grad_mixing_first, grad_mixing_second]),
            jnp.stack([grad_static_first, grad_static_second]),
        ),
        ("rep", "shard"),
    )
    shard_rows = width // lax.axis_size("shard")
    own_mixing = lax.dynamic_slice_in_dim(
        mixing_sums, lax.axis_index("shard") * shard_rows, shard_rows, 1
    )
    ffn_width = gate_full.shape[1]
    return (
        result.astype(jnp.bfloat16),
        grad_streams,
        attention_rows[:, :width],
        attention_rows[:, width : 2 * width],
        attention_rows[:, 2 * width : 3 * width],
        attention_rows[:, 3 * width :],
        gate_up_rows[:, :ffn_width],
        gate_up_rows[:, ffn_width:],
        down_rows,
        own_mixing,
        static_sums,
    )


def solution(mesh):
    return jax.shard_map(
        per_device,
        mesh=mesh,
        in_specs=(
            P(("rep", "shard"), None, None),
            P(("rep", "shard"), None, None),
            P("rep", None),
            P("rep", None),
            P("shard", None),
            P("shard", None),
            P("shard", None),
            P("shard", None),
            P("shard", None),
            P("shard", None),
            P("shard", None),
            P(None, "shard", None),
            P(),
        ),
        out_specs=(
            P(("rep", "shard"), None, None),
            P(("rep", "shard"), None, None),
            P("shard", None),
            P("shard", None),
            P("shard", None),
            P("shard", None),
            P("shard", None),
            P("shard", None),
            P("shard", None),
            P(None, "shard", None),
            P(),
        ),
        check_vma=False,
    )
```

profile of v0, /device:TPU:0, one launch (start us, length us, event | category | flops | bytes accessed | tf_op | source)
XLA Modules:
  0.0 3133.4 jit_solution(13109241112346863319)
XLA Ops:
  46.3 48.4 %all-gather.8.cloned.1.call-done = bf16[2048,2048]{1,0:T(8,128)(2,1)} async-done(((bf16[256,2048]{1,0:T(8,128)(2,1)}), bf16[2048,2048]{1,0:T(8,128)(2,1)}) %all-gather.8.cloned.1.call-update) | async-done | bytes 8388624 | tf_op jit(solution)/shard_map/all_gather | solution.py:288
  100.6 76.4 %all-gather.10.cloned.1.call-done = bf16[2048,2048]{1,0:T(8,128)(2,1)} async-done(((bf16[256,2048]{1,0:T(8,128)(2,1)}), bf16[2048,2048]{1,0:T(8,128)(2,1)}) %all-gather.10.cloned.1.call-update) | async-done | bytes 8388624 | tf_op jit(solution)/shard_map/all_gather | solution.py:289
  182.5 76.7 %all-gather.12.cloned.1.call-done = bf16[2048,2048]{1,0:T(8,128)(2,1)} async-done(((bf16[256,2048]{1,0:T(8,128)(2,1)}), bf16[2048,2048]{1,0:T(8,128)(2,1)}) %all-gather.12.cloned.1.call-update) | async-done | bytes 8388624 | tf_op jit(solution)/shard_map/all_gather | solution.py:290
  284.9 89.9 %all-to-all-done = bf16[160,3,16,128]{3,0,1,2:T(8,128)(2,1)S(1)} async-done(((bf16[160,3,16,128]{3,0,1,2:T(8,128)(2,1)}), bf16[160,3,16,128]{3,0,1,2:T(8,128)(2,1)S(1)}, u32[]{:S(2)}, u32[]{:S(2)}) %all-to-all-start) | async-done | bytes 1966112 | tf_op jit(solution)/shard_map/all_to_all | solution.py:328
  389.1 42.0 %while.109 = (s32[]{:T(128)}, bf16[2,640,2,128]{3,1,0,2:T(8,128)(2,1)}, f32[2,2,640]{2,1,0:T(2,128)S(1)}, s32[2]{0:T(128)S(1)}, bf16[1280,2,128]{2,0,1:T(8,128)(...) while((s32[]{:T(128)}, ...), condition=%wide.region_14.15_spmd, body=%wide.region_7.14_spmd.sunk | while | flops 640949760 | bytes 20871628 | solution.py:145
  442.3 34.4 %all-to-all-done.1 = bf16[1280,2,128]{2,1,0:T(2,128)(2,1)S(1)} async-done(((bf16[1280,2,128]{2,1,0:T(2,128)(2,1)}), bf16[1280,2,128]{2,1,0:T(2,128)(2,1)S(1)}, u32[]{:S(2)}, u32[]{:S(2)}) %all-to-all-start.1) | async-done | bytes 655392 | tf_op jit(solution)/shard_map/all_to_all | solution.py:336
  516.8 168.8 %all-gather.16.cloned.1.call-done = bf16[2048,8192]{1,0:T(8,128)(2,1)} async-done(((bf16[256,8192]{1,0:T(8,128)(2,1)}), bf16[2048,8192]{1,0:T(8,128)(2,1)}) %all-gather.16.cloned.1.call-update) | async-done | bytes 33554448 | tf_op jit(solution)/shard_map/all_gather | solution.py:295
  704.3 269.5 %all-gather.18.cloned.1.call-done = bf16[2048,8192]{1,0:T(8,128)(2,1)} async-done(((bf16[256,8192]{1,0:T(8,128)(2,1)}), bf16[2048,8192]{1,0:T(8,128)(2,1)}) %all-gather.18.cloned.1.call-update) | async-done | bytes 33554448 | tf_op jit(solution)/shard_map/all_gather | solution.py:296
  973.8 22.7 multiply_convert_fusion.2
  996.6 265.7 %all-gather.20.cloned.1.call-done = bf16[8192,2048]{1,0:T(8,128)(2,1)} async-done(((bf16[1024,2048]{1,0:T(8,128)(2,1)}), bf16[8192,2048]{1,0:T(8,128)(2,1)}) %all-gather.20.cloned.1.call-update) | async-done | bytes 33554448 | tf_op jit(solution)/shard_map/all_gather | solution.py:297
  1312.5 21.6 multiply_convert_fusion
  1370.8 24.0 fusion.88
  1448.9 28.0 all-to-all-done.2
  1481.3 66.3 %while.112 = (s32[]{:T(128)}, f32[1280,2,128]{2,1,0:T(2,128)}, f32[1280,2,128]{2,0,1:T(8,128)}, f32[1280,2,128]{2,0,1:T(8,128)}, bf16[1280,2,128]{2,0,1:T(8,128)...) while((s32[]{:T(128)}, f32[1280,2,128]{2,1,0:T(2,128)}, ...), condition=%wide.region_32.33_spmd, body=%wide.region_26.32_spmd.sunk | while | flops 1483736320 | bytes 65393816 | solution.py:254
  1490.1 22.8 while.116
  1523.3 22.6 while.116
  1583.3 72.6 %all-to-all-done.3 = bf16[1280,3,2,128]{3,2,1,0:T(2,128)(2,1)S(1)} async-done(((bf16[1280,3,2,128]{3,2,1,0:T(2,128)(2,1)}), bf16[1280,3,2,128]{3,2,1,0:T(2,128)(2,1)S(1)}, u32[]{:S(2)}, u32[]{:S(2)}) %all-to-all-start.3) | async-done | bytes 1966112 | tf_op jit(solution)/shard_map/all_to_all | solution.py:399
  1676.7 22.8 pad_maximum_fusion
  1700.9 28.2 convolution_convert_fusion
  1797.6 226.3 %reduce-scatter.4.cloned.1.call-done = bf16[256,8192]{1,0:T(8,128)(2,1)} async-done(((bf16[2048,8192]{1,0:T(8,128)(2,1)}), bf16[256,8192]{1,0:T(8,128)(2,1)}) %reduce-scatter.4.cloned.1.call-update) | async-done | bytes 4194320 | tf_op jit(solution)/shard_map/reduce_scatter | solution.py:263
  2023.9 640.7 %reduce-scatter.6.cloned.1.call-done = bf16[256,16384]{1,0:T(8,128)(2,1)} async-done(((bf16[2048,16384]{1,0:T(8,128)(2,1)}), bf16[256,16384]{1,0:T(8,128)(2,1)}) %reduce-scatter.6.cloned.1.call-update) | async-done | bytes 8388624 | tf_op jit(solution)/shard_map/reduce_scatter | solution.py:263
  2689.5 38.1 %psum.39 = f32[2,4,6]{2,1,0:T(4,128)} all-reduce(f32[2,4,6]{2,1,0:T(4,128)S(1)} %pad_maximum_fusion.5), channel_id=1, replica_groups=mesh['rep'=4,'shard'=8] {'rep','shard'}, use_global_device_ids=true, to_apply=%region_47.48 | all-reduce | flops 48 | bytes 384 | tf_op jit(solution)/shard_map/psum | solution.py:419
  2756.4 36.1 %all-reduce.10.cloned.1.call-done = f32[2,2048,6]{1,2,0:T(8,128)} async-done(((f32[2,2048,6]{1,2,0:T(8,128)}), f32[2,2048,6]{1,2,0:T(8,128)}) %all-reduce.10.cloned.1.call-update) | async-done | bytes 98320 | tf_op jit(solution)/shard_map/psum | solution.py:419
  2793.8 311.2 %all-reduce.12.cloned.1.call-done = (bf16[256,8192]{1,0:T(8,128)(2,1)}, bf16[256,16384]{1,0:T(8,128)(2,1)}, bf16[1024,2048]{1,0:T(8,128)(2,1)}) async-done(((bf16[256,8192]{1,0:T(8,128)(2,1)}, bf16[256,16384]{1,0:T(8,128)(2,1)}, bf16[1024,2048]{1,0:T(8,128)(2,1)}), (bf16[256,8192]{1,0:T(8,128)(2,1)}, bf16[256,16384]{1,0:T(8,128)(2,1)}, bf16[1024,2048]{1,0:T(8,128)(2,1)})) %all-reduce.12.cloned.1.call-update) | async-done | bytes 16777232 | tf_op jit(solution)/shard_map/psum | solution.py:269
  (557 shorter events, 659.8 us)
Async XLA Ops:
  7.2 87.5 %all-gather.8.cloned.1.call-start = ((), (), s32[]{:S(2)}) async-start(), calls=%async_computation.7 | async-start | bytes 9437184 | tf_op jit(solution)/shard_map/all_gather | solution.py:288
  7.9 169.1 %all-gather.10.cloned.1.call-start = ((), (), s32[]{:S(2)}) async-start(), calls=%async_computation.8 | async-start | bytes 9437184 | tf_op jit(solution)/shard_map/all_gather | solution.py:289
  8.7 250.6 %all-gather.12.cloned.1.call-start = ((), (), s32[]{:S(2)}) async-start(), calls=%async_computation.9 | async-start | bytes 9437184 | tf_op jit(solution)/shard_map/all_gather | solution.py:290
  9.4 468.3 %all-gather.14.cloned.1.call-start = ((), (), s32[]{:S(2)}) async-start(), calls=%async_computation.10 | async-start | bytes 9437184 | tf_op jit(solution)/shard_map/all_gather | solution.py:291
  10.0 675.6 %all-gather.16.cloned.1.call-start = ((), (), s32[]{:S(2)}) async-start(), calls=%async_computation.11 | async-start | bytes 37748736 | tf_op jit(solution)/shard_map/all_gather | solution.py:295
  10.6 963.3 %all-gather.18.cloned.1.call-start = ((), (), s32[]{:S(2)}) async-start(), calls=%async_computation.12 | async-start | bytes 37748736 | tf_op jit(solution)/shard_map/all_gather | solution.py:296
  11.1 1251.1 %all-gather.20.cloned.1.call-start = ((), (), s32[]{:S(2)}) async-start(), calls=%async_computation.13 | async-start | bytes 37748736 | tf_op jit(solution)/shard_map/all_gather | solution.py:297
  45.8 213.5 %copy-start.82 = (f32[160]{0:T(256)}, f32[160]{0:T(256)S(1)}, u32[]{:S(2)}) copy-start(f32[160]{0:T(256)S(1)} %broadcast_multiply_fusion.5) | copy-start | bytes 1924
  46.3 213.0 %copy-start.86 = (f32[160]{0:T(256)}, f32[160]{0:T(256)S(1)}, u32[]{:S(2)}) copy-start(f32[160]{0:T(256)S(1)} %fusion.123) | copy-start | bytes 1924
  266.2 108.5 %all-to-all-start = ((bf16[160,3,16,128]{3,0,1,2:T(8,128)(2,1)}), bf16[160,3,16,128]{3,0,1,2:T(8,128)(2,1)S(1)}, u32[]{:S(2)}, u32[]{:S(2)}) async-start(bf16[160,3,16,128]{3,0,1,2:T(8,128)(2,1)} %pad_maximum_fusion.1), calls=%async_computation | async-start | bytes 3932160 | tf_op jit(solution)/shard_map/all_to_all | solution.py:328
  437.6 39.1 %all-to-all-start.1 = ((bf16[1280,2,128]{2,1,0:T(2,128)(2,1)}), bf16[1280,2,128]{2,1,0:T(2,128)(2,1)S(1)}, u32[]{:S(2)}, u32[]{:S(2)}) async-start(bf16[1280,2,128]{2,1,0:T(2,128)(2,1)} %copy.276), calls=%async_computation.1 | async-start | bytes 1310720 | tf_op jit(solution)/shard_map/all_to_all | solution.py:336
  441.2 1356.4 %reduce-scatter.8.cloned.1.call-start = ((), (), s32[]{:S(2)}) async-start(), calls=%async_computation.16 | async-start | bytes 37748736 | tf_op jit(solution)/shard_map/reduce_scatter | solution.py:263
  504.1 890.9 %copy-start.69 = (f32[160,4,6]{0,2,1:T(8,128)}, f32[160,4,6]{0,2,1:T(8,128)S(1)}, u32[]{:S(2)}) copy-start(f32[160,4,6]{0,2,1:T(8,128)S(1)} %get-tuple-element.1016) | copy-start | bytes 46084
  504.3 772.3 %copy-start.53 = (f32[160,4,1]{1,0,2:T(8,128)}, f32[160,4,1]{1,0,2:T(8,128)S(1)}, u32[]{:S(2)}) copy-start(f32[160,4,1]{1,0,2:T(8,128)S(1)} %copy.338) | copy-start | bytes 7684
  515.8 854.1 %copy-start.11 = (f32[160,1,2048]{2,1,0:T(1,128)}, f32[160,1,2048]{2,1,0:T(1,128)S(1)}, u32[]{:S(2)}) copy-start(f32[160,1,2048]{2,1,0:T(1,128)S(1)} %fusion.148) | copy-start | bytes 3932164
  516.3 853.7 %copy-start.62 = (f32[160]{0:T(256)}, f32[160]{0:T(256)S(1)}, u32[]{:S(2)}) copy-start(f32[160]{0:T(256)S(1)} %broadcast_multiply_fusion.4) | copy-start | bytes 1924
  516.8 853.2 %copy-start.64 = (f32[160]{0:T(256)}, f32[160]{0:T(256)S(1)}, u32[]{:S(2)}) copy-start(f32[160]{0:T(256)S(1)} %fusion.124) | copy-start | bytes 1924
  1312.5 104.7 %copy-start.47 = (f32[160,4,4]{2,1,0:T(4,128)}, f32[160,4,4]{2,1,0:T(4,128)S(1)}, u32[]{:S(2)}) copy-start(f32[160,4,4]{2,1,0:T(4,128)S(1)} %copy.285) | copy-start | bytes 30724
  1444.2 32.7 %all-to-all-start.2 = ((bf16[160,16,128]{2,0,1:T(8,128)(2,1)}), bf16[160,16,128]{2,0,1:T(8,128)(2,1)S(1)}, u32[]{:S(2)}, u32[]{:S(2)}) async-start(bf16[160,16,128]{2,0,1:T(8,128)(2,1)} %bitcast.294), calls=%async_computation.2 | async-start | bytes 1310720 | tf_op jit(solution)/shard_map/all_to_all | solution.py:372
  1573.7 82.2 %all-to-all-start.3 = ((bf16[1280,3,2,128]{3,2,1,0:T(2,128)(2,1)}), bf16[1280,3,2,128]{3,2,1,0:T(2,128)(2,1)S(1)}, u32[]{:S(2)}, u32[]{:S(2)}) async-start(bf16[1280,3,2,128]{3,2,1,0:T(2,128)(2,1)} %pad_maximum_fusion.2), calls=%async_computation.3 | async-start | bytes 3932160 | tf_op jit(solution)/shard_map/all_to_all | solution.py:399
  1577.4 446.5 %reduce-scatter.4.cloned.1.call-start = ((), (), s32[]{:S(2)}) async-start(), calls=%async_computation.14 | async-start | bytes 37748736 | tf_op jit(solution)/shard_map/reduce_scatter | solution.py:263
  1699.6 965.1 %reduce-scatter.6.cloned.1.call-start = ((), (), s32[]{:S(2)}) async-start(), calls=%async_computation.15 | async-start | bytes 75497472 | tf_op jit(solution)/shard_map/reduce_scatter | solution.py:263
  1729.1 1063.5 %all-reduce.10.cloned.1.call-start = ((), (), s32[]{:S(2)}) async-start(), calls=%async_computation.17 | async-start | bytes 262144 | tf_op jit(solution)/shard_map/psum | solution.py:419
  1797.6 1307.5 %all-reduce.12.cloned.1.call-start = ((), (), s32[]{:S(2)}) async-start(), calls=%async_computation.18 | async-start | bytes 33554432 | tf_op jit(solution)/shard_map/psum | solution.py:269
  (107 other events, 1100.6 us)
Sparse Core Ops, SparseCore 0:
  9.6 85.0 all-gather.7
  96.3 80.6 all-gather.9
  178.6 80.5 all-gather.11
  260.7 122.3 all-gather.13
  384.5 301.0 all-gather.15
  687.0 286.7 all-gather.17
  975.4 286.8 all-gather.19
  1297.8 366.6 reduce-scatter.7
  1699.7 324.1 reduce-scatter.3
  2026.1 638.4 reduce-scatter.5
  2671.7 120.7 all-reduce.9
  2796.9 308.1 all-reduce.11
where the time goes:
time: 3140 us; the launch traced here: 3130 us
  waiting for transfers between devices  2350 us (75%)
  matrix products  455 us (14%)
  other arithmetic  124 us (4%)
  local copies, waits for them, and re-layouts  106 us (3%)
  blocking collectives  54 us (2%)
    reduce_scatter x3, waiting for transfers between devices, reduce_gradient(): lax.psum_scatter(jnp.concatenate(columns, axis=1).astype(jnp.bfloat16), '...  867 us
    psum x1, waiting for transfers between devices, reduce_gradient(): return lax.psum(group_sum, 'rep').astype(jnp.float32)  311 us
    all_gather x1, waiting for transfers between devices, per_device(): lax.all_gather(up_weight, 'shard', axis=0, tiled=True)  270 us
    all_gather x1, waiting for transfers between devices, per_device(): lax.all_gather(down_weight, 'shard', axis=0, tiled=True)  266 us
    all_gather x1, waiting for transfers between devices, per_device(): lax.all_gather(gate_weight, 'shard', axis=0, tiled=True)  169 us
    all_to_all x1, waiting for transfers between devices, per_device(): lax.all_to_all(projected, 'shard', split_axis=2, concat_axis=0, tiled=True)  89.9 us
    dot_general x6, matrix products, mixing(): jnp.einsum('tnj,tnd->tjd', coefficients[:, :, 1:-1], stream_values, preci...  86.3 us
    all_gather x1, waiting for transfers between devices, per_device(): lax.all_gather(value_weight, 'shard', axis=0, tiled=True)  76.7 us
  transfers between devices with their start and end apart: 16, of which 14 were waited for; matrix products, arithmetic and copies ran while one was open for 19% of the time, Pallas kernels for 0%

commit v1 on v0

v1 whole, which is shorter than its diff:
```python
import functools
import math

import jax
import jax.numpy as jnp
from jax import lax
from jax.experimental import pallas as pl
from jax.experimental.pallas import tpu as pltpu
from jax.sharding import PartitionSpec as P

HEADS = 16
EPSILON = 1e-05
NEGATIVE = -1e30
LANES = 128
LOG2E = 1.4426950408889634
F32 = jnp.float32
BF16 = jnp.bfloat16
NO_COST = pl.CostEstimate(flops=0, bytes_accessed=0, transcendentals=0)
NN = (((1,), (0,)), ((), ()))
NT = (((1,), (1,)), ((), ()))
TN = (((0,), (0,)), ((), ()))


def dot(a, b, dims=NN):
    return lax.dot_general(a, b, dims, preferred_element_type=F32)


def params(mib):
    return pltpu.CompilerParams(vmem_limit_bytes=mib << 20)


def after(value, *events):
    return lax.optimization_barrier((value, *events))[0] if events else value


def assemble_kernel(line, x_ref, *refs):
    rights, lefts, out_ref = refs[: line - 1], refs[line - 1 : -1], refs[-1]
    out_ref[0] = x_ref[...]
    for k in range(1, line):
        out_ref[k] = lefts[k - 1][...] + rights[line - k - 1][...]


class Task:
    def __init__(self, steps):
        self.steps, self.value, self.over, self.arrived = steps, None, False, []
        self.advance(None)

    def advance(self, arrived):
        self.arrived += arrived or []
        try:
            self.sends = list(self.steps.send(arrived))
            self.left = list(range(len(self.sends)))
            self.got = [None] * len(self.sends)
        except StopIteration as stop:
            self.value, self.over, self.left = stop.value, True, []


class Rounds:
    def __init__(self):
        self.base, self.fence, self.last = (), (), ()

    def hold(self, *values):
        self.fence += values

    def tie(self, value):
        return after(value, *self.fence)

    def run(self, *jobs):
        self.base, self.fence = self.fence, ()
        self.last = self.base
        self.send(jobs, self.base)

    def also(self, *jobs):
        self.last = self.send(jobs, self.base)

    def then(self, *jobs):
        self.last = self.send(jobs, self.last)

    def send(self, jobs, events):
        sends = []
        for job in jobs:
            task, pairs = job if isinstance(job, tuple) else (job, len(job.left))
            sends += [(task, i) for i in task.left[: 2 * pairs]]
        out = tuple(t.sends[i][0](after(t.sends[i][1], *events)) for t, i in sends)
        self.fence += out
        for (t, i), v in zip(sends, out):
            t.got[i] = v
            t.left.remove(i)
        for t in {id(t): t for t, _ in sends}.values():
            if not t.left:
                t.advance(t.got)
        return out

    def finish(self, *tasks):
        while any(not t.over for t in tasks):
            self.run(*tasks)


def sender(axis, pairs):
    return lambda x: lax.ppermute(x, axis, pairs)


def assemble_kernel(line, x_ref, *refs):
    rights, lefts, out_ref = refs[: line - 1], refs[line - 1 : -1], refs[-1]
    out_ref[0] = x_ref[...]
    for k in range(1, line):
        out_ref[k] = lefts[k - 1][...] + rights[line - k - 1][...]


def line_gather(x):
    line = lax.axis_size("shard") // 2
    right = left = x
    rights, lefts = [], []
    for step in range(line - 1):
        right, left = yield [
            (sender("shard", [(2 * p + c, 2 * p + 2 + c) for p in range(step, line - 1) for c in range(2)]), right),
            (sender("shard", [(2 * p + c, 2 * p - 2 + c) for p in range(1, line - step) for c in range(2)]), left),
        ]
        rights.append(right)
        lefts.append(left)
    rows, width = x.shape
    (mine,) = token_call(
        functools.partial(assemble_kernel, line), rows, [x, *rights, *lefts],
        [jax.ShapeDtypeStruct((line, rows, width), x.dtype)],
    )
    return mine.reshape(line * rows, width)


def other_core(x):
    size = lax.axis_size("shard")
    (other,) = yield [(sender("shard", [(i, i ^ 1) for i in range(size)]), x)]
    return other


def line_shift(k):
    line = lax.axis_size("shard") // 2
    return sender("shard", [(2 * p + c, 2 * ((p + k) % line) + c) for p in range(line) for c in range(2)])


def stack_kernel(*refs):
    for k, ref in enumerate(refs[:-1]):
        refs[-1][k] = ref[...]


def shifts(line, steps):
    return [list(range(1, line))] if steps == 1 else [list(range(1, line, 2)), list(range(2, line, 2))]


def direct_gather(x, steps=1):
    line = lax.axis_size("shard") // 2
    came = {}
    for step in shifts(line, steps):
        came |= dict(zip(step, (yield [(line_shift(k), x) for k in step])))
    rows, width = x.shape
    (mine,) = token_call(
        stack_kernel, rows, [x] + [came[line - q] for q in range(1, line)],
        [jax.ShapeDtypeStruct((line, rows, width), x.dtype)],
    )
    return mine.reshape(line * rows, width)


def direct_scatter(rows, steps=1):
    line = lax.axis_size("shard") // 2
    parts = list(rows.reshape(line, rows.shape[0] // line, -1))
    came = [parts[0]]
    for step in shifts(line, steps):
        came += yield [(line_shift(k), parts[k]) for k in step]
    return came


def rep_sender(bit):
    return sender("rep", [(i, i ^ (1 << bit)) for i in range(lax.axis_size("rep"))])


def rep_orders(units):
    bits = list(range(lax.axis_size("rep").bit_length() - 1))
    return [bits] * (units // 2) + [bits[::-1]] * (units - units // 2)


def paired(sends):
    middle = len(sends) // 2
    return [v for pair in zip(sends[:middle], sends[middle:]) for v in pair]


def rep_scatter(units, merge=False):
    orders = rep_orders(len(units))
    units = [dict(enumerate(u)) for u in units]
    for i in range(len(orders[0])):
        bits = [1 << o[i] for o in orders]
        keys = [[m for m in unit if m & bit] for unit, bit in zip(units, bits)]
        came = yield from exchange_blocks(units, keys, [o[i] for o in orders], merge)
        units = [
            {m ^ bit: unit[m ^ bit] + v for m, v in zip(key, new)}
            for unit, bit, key, new in zip(units, bits, keys, came)
        ]
    return [u[0] for u in units]


def rep_gather(units, merge=False):
    orders = [o[::-1] for o in rep_orders(len(units))]
    units = [{0: u} for u in units]
    for i in range(len(orders[0])):
        keys = [list(unit) for unit in units]
        came = yield from exchange_blocks(units, keys, [o[i] for o in orders], merge)
        for unit, o, key, new in zip(units, orders, keys, came):
            unit |= {m ^ (1 << o[i]): v for m, v in zip(key, new)}
    return [[u[m] for m in range(len(u))] for u in units]


def rep_flip(m):
    return sender("rep", [(i, i ^ m) for i in range(lax.axis_size("rep"))])


def rep_scatter_direct(blocks):
    came = yield [(rep_flip(m), blocks[m]) for m in range(1, len(blocks))]
    return sum(v.astype(F32) for v in [blocks[0], *came]).astype(blocks[0].dtype)


def rep_gather_direct(block):
    came = yield [(rep_flip(m), block) for m in range(1, lax.axis_size("rep"))]
    return [block, *came]


def exchange_blocks(units, keys, bits, merge):
    if merge:
        came = yield [
            (rep_sender(bit), jnp.concatenate([unit[m] for m in key]) if len(key) > 1 else unit[key[0]])
            for unit, key, bit in paired(list(zip(units, keys, bits)))
        ]
        order = paired(list(range(len(units))))
        return [cut_units(came[order.index(u)], len(keys[u])) for u in range(len(units))]
    flat = paired([(u, m) for u, key in enumerate(keys) for m in key])
    came = yield [(rep_sender(bits[u]), units[u][m]) for u, m in flat]
    came = dict(zip(flat, came))
    return [[came[u, m] for m in key] for u, key in enumerate(keys)]


def shard_exchange(x, counts=()):
    shards = lax.axis_size("shard")
    me = lax.axis_index("shard")
    take = lambda k: lax.dynamic_index_in_dim(x, me ^ k, 0, keepdims=False)
    out, counts = [take(0)], list(counts)
    while len(out) < shards:
        step = range(len(out), min(shards, len(out) + (counts.pop(0) if counts else shards)))
        out += yield [(sender("shard", [(i, i ^ k) for i in range(shards)]), take(k)) for k in step]
    return out


def chip_exchange(x, counts=(), out=None):
    shards = lax.axis_size("shard")
    me = lax.axis_index("shard")
    pick = lambda k: lax.dynamic_index_in_dim(x, me ^ k, 0, keepdims=False)
    (came,) = yield [
        (sender("shard", [(i, i ^ 1) for i in range(shards)]), jnp.stack([pick(k) for k in range(1, shards, 2)]))
    ]
    held = [jnp.stack([pick(2 * q), came[q]]) for q in range(shards // 2)]
    out, counts = [] if out is None else out, list(counts)
    out += [held[0][0], held[0][1]]
    while len(out) < shards:
        q = len(out) // 2
        step = range(q, min(shards // 2, q + (counts.pop(0) if counts else shards)))
        came = yield [(sender("shard", [(i, i ^ (2 * q)) for i in range(shards)]), held[q]) for q in step]
        out += [v[f] for v in came for f in range(2)]
    return out


def stack_units(blocks, count):
    size = len(blocks) // count
    return [jnp.stack(blocks[i * size : (i + 1) * size]) for i in range(count)]


def to_tokens(x):
    shards = lax.axis_size("shard")
    line = shards // 2
    (came,) = yield [(sender("shard", [(i, i ^ 1) for i in range(shards)]), x[1])]
    held = jnp.stack([x[0], came], axis=1)
    came = yield [
        (sender("shard", [(2 * p + c, 2 * ((p + k) % line) + c) for p in range(line) for c in range(2)]), held[k])
        for k in range(1, line)
    ]
    came = [held[0], *came]
    return [jnp.concatenate([came[(line - q) % line][f] for q in range(line)], axis=1) for f in range(2)]


def cut_units(x, count):
    size = x.shape[0] // count
    return [x[i * size : (i + 1) * size] for i in range(count)]


def recut_piece(weights):
    shards, reps = lax.axis_size("shard"), lax.axis_size("rep")
    part = weights[0].shape[0] // reps
    start = lax.axis_index("rep") * part
    pieces = [
        lax.dynamic_slice_in_dim(w, start, part, 0).reshape(part, shards, -1).transpose(1, 0, 2) for w in weights
    ]
    return jnp.concatenate(pieces, axis=2)


def halves(x):
    return cut_units(x, 2)


def unit_specs(units):
    size = units[0][0].shape[0]
    return [
        pl.BlockSpec((1,) + v.shape[1:], lambda k, me, g=g: (jnp.clip(k - g * size, 0, size - 1), 0, 0))
        for g, u in enumerate(units) for v in u
    ]


def columns_kernel(units, reps, parts, me_ref, *refs):
    outs = refs[-parts:]
    size = pl.num_programs(0) // units
    part = refs[0].shape[1]
    for g in range(units):
        @pl.when(pl.program_id(0) // size == g)
        def _(chosen=refs[g * reps : (g + 1) * reps]):
            for m in range(reps):
                row = pl.multiple_of((me_ref[0] ^ m) * part, part)
                for i, out_ref in enumerate(outs):
                    width = out_ref.shape[1]
                    out_ref[pl.ds(row, part), :] = chosen[m][0, :, i * width : (i + 1) * width].astype(out_ref.dtype)


def join(units, parts, spec, shapes, filled=(), mib=32):
    reps = lax.axis_size("rep")
    operands = [v for u in units for v in u]
    return pl.pallas_call(
        functools.partial(columns_kernel, len(units), reps, parts),
        grid_spec=pltpu.PrefetchScalarGridSpec(
            num_scalar_prefetch=1,
            grid=(len(units) * units[0][0].shape[0],),
            in_specs=unit_specs(units) + [pl.BlockSpec(memory_space=pl.ANY)] * len(filled),
            out_specs=[spec] * parts,
        ),
        out_shape=shapes,
        input_output_aliases={1 + len(operands) + i: i for i in range(len(filled))},
        compiler_params=params(mib),
        cost_estimate=NO_COST,
    )(jnp.stack([lax.axis_index("rep"), lax.axis_index("shard")]).astype(jnp.int32), *operands, *filled)


def recut_join(units, first=0, filled=()):
    shards, reps = lax.axis_size("shard"), lax.axis_size("rep")
    _, part, columns = units[0][0].shape
    rows = part * reps
    return join(
        units, 1, pl.BlockSpec((rows, columns), lambda k, me: ((k + first) ^ me[1], 0)),
        [jax.ShapeDtypeStruct((shards * rows, columns), BF16)], filled,
    )[0]


def rows_in_order(units):
    blocks, part, columns = units[0][0].shape
    rows = part * lax.axis_size("rep")
    return join(
        units, 1, pl.BlockSpec((rows, columns), lambda k, me: (k, 0)),
        [jax.ShapeDtypeStruct((len(units) * blocks * rows, columns), BF16)],
    )[0]


def columns_join(units, parts):
    shards, reps = lax.axis_size("shard"), lax.axis_size("rep")
    _, part, columns = units[0][0].shape
    rows, width = part * reps, columns // parts
    return join(
        units, parts, pl.BlockSpec((rows, width), lambda k, me: (0, k ^ me[1])),
        [jax.ShapeDtypeStruct((rows, shards * width), F32)] * parts, mib=56 if parts == 2 else 32,
    )


def rows_kernel(units, reps, me_ref, *refs):
    out_ref = refs[-1]
    part = refs[0].shape[0]
    for u in range(units):
        for m in range(reps):
            row = pl.multiple_of((me_ref[0] ^ m) * (units * part) + u * part, part)
            out_ref[pl.ds(row, part), :] = refs[u * reps + m][...].astype(F32)


def rows_join(units):
    reps = lax.axis_size("rep")
    operands = [v for u in units for v in u]
    part, columns = operands[0].shape
    block = 512 if columns % 512 == 0 else columns
    return pl.pallas_call(
        functools.partial(rows_kernel, len(units), reps),
        grid_spec=pltpu.PrefetchScalarGridSpec(
            num_scalar_prefetch=1,
            grid=(columns // block,),
            in_specs=[pl.BlockSpec((part, block), lambda j, me: (0, j))] * len(operands),
            out_specs=pl.BlockSpec((part * len(operands), block), lambda j, me: (0, j)),
        ),
        out_shape=jax.ShapeDtypeStruct((part * len(operands), columns), F32),
        compiler_params=params(32),
        cost_estimate=NO_COST,
    )(lax.axis_index("rep").astype(jnp.int32)[None], *operands)


def mixing_kernel(me_ref, *refs):
    out_ref = refs[-1]
    out_ref[...] = jnp.zeros_like(out_ref)
    width = refs[0].shape[2]
    for k, ref in enumerate(refs[:-1]):
        start = pl.multiple_of((me_ref[0] ^ k) * width, width)
        out_ref[:, : ref.shape[1], pl.ds(start, width)] = ref[...]


def mixing_gather(weight):
    shards = lax.axis_size("shard")
    piece = jnp.pad(jnp.swapaxes(weight, 1, 2), ((0, 0), (0, 2), (0, 0)))
    piece = jnp.concatenate([piece, piece], axis=1)
    (came,) = yield [(sender("shard", [(i, i ^ 1) for i in range(shards)]), piece)]
    held = jnp.stack([piece, came])
    came = yield [
        (sender("shard", [(i, i ^ (2 * q)) for i in range(shards)]), held) for q in range(1, shards // 2)
    ]
    came = [v[f] for v in [held, *came] for f in range(2)]
    return pl.pallas_call(
        mixing_kernel,
        grid_spec=pltpu.PrefetchScalarGridSpec(
            num_scalar_prefetch=1,
            grid=(1,),
            in_specs=[pl.BlockSpec(piece.shape, lambda i, me: (0, 0, 0))] * shards,
            out_specs=pl.BlockSpec((2, LANES, shards * piece.shape[2]), lambda i, me: (0, 0, 0)),
        ),
        out_shape=jax.ShapeDtypeStruct((2, LANES, shards * piece.shape[2]), BF16),
        compiler_params=params(32),
    )(lax.axis_index("shard").astype(jnp.int32)[None], *came)


def sum_small(blocks):
    shards, reps = lax.axis_size("shard"), lax.axis_size("rep")
    me = lax.axis_index("shard")
    blocks = blocks.reshape((shards // 2, 2) + blocks.shape[1:])
    pick = lambda f: lax.dynamic_index_in_dim(blocks, (me % 2) ^ f, 1, keepdims=False)
    (came,) = yield [(sender("shard", [(i, i ^ 1) for i in range(shards)]), pick(1))]
    pair = pick(0) + came
    take = lambda q: lax.dynamic_index_in_dim(pair, (me // 2) ^ q, 0, keepdims=False)
    total = take(0)
    came = yield [
        (sender("shard", [(i, i ^ (2 * q)) for i in range(shards)]), take(q)) for q in range(1, shards // 2)
    ]
    for v in came:
        total = total + v
    came = yield [(sender("rep", [(i, i ^ k) for i in range(reps)]), total) for k in range(1, reps)]
    stacked = jnp.stack([total, *came])
    me = lax.axis_index("rep")
    return sum(lax.dynamic_index_in_dim(stacked, me ^ k, 0, keepdims=False) for k in range(reps))


def lane(shape):
    return lax.broadcasted_iota(jnp.int32, shape, len(shape) - 1)


def column(values, index):
    return values[:, index : index + 1]


def split(values):
    high = values.astype(BF16)
    return high, (values - high.astype(F32)).astype(BF16)


def moments(values):
    mean = jnp.mean(values, axis=-1, keepdims=True)
    centred = values - mean
    spread = jnp.mean(centred * centred, axis=-1, keepdims=True)
    return mean, centred, lax.rsqrt(spread + EPSILON)


def mix_forward(streams, weight, static):
    count = len(streams)
    rows = streams[0].shape[0]
    stats = [moments(y) for y in streams]
    parts = [split(centred) for _, centred, _ in stats]
    raw = dot(jnp.concatenate([p[0] for p in parts] + [p[1] for p in parts], axis=0), weight, NT)
    at = lane((rows, LANES))
    pres, coefficients = [], []
    for i in range(count):
        pre = (raw[i * rows : (i + 1) * rows] + raw[(count + i) * rows : (count + i + 1) * rows]) * stats[i][2]
        pres.append(pre)
        coefficients.append(static[i : i + 1] + jnp.tanh(pre))
    entering = sum(column(c, 0) * y for c, y in zip(coefficients, streams))
    mean, centred, scale = moments(entering)
    packed = []
    for i in range(count):
        value = jnp.where(at < 6, pres[i], 0.0)
        value = jnp.where(at == 6, stats[i][0], jnp.where(at == 7, stats[i][2], value))
        packed.append(jnp.where(at == 8, mean, jnp.where(at == 9, scale, value)))
    return centred * scale, coefficients, packed


def mix_carry(streams, coefficients, j):
    return sum(column(c, 1 + j) * y for c, y in zip(coefficients, streams))


def mix_backward(streams, packed, static, grad_entering, grad_carried, grad_beta, weight_rows, weight_mean):
    count = len(streams)
    rows, width = streams[0].shape
    at = lane((rows, LANES))
    tanhs = [jnp.where(at < 6, jnp.tanh(p), 0.0) for p in packed]
    coefficients = [static[i : i + 1] + tanhs[i] for i in range(count)]
    mean, scale = column(packed[0], 8), column(packed[0], 9)
    entering = (sum(column(c, 0) * y for c, y in zip(coefficients, streams)) - mean) * scale
    inner = jnp.mean(grad_entering * entering, axis=-1, keepdims=True)
    outer = jnp.mean(grad_entering, axis=-1, keepdims=True)
    grad_sum = scale * (grad_entering - outer - entering * inner)
    grads, both, normed, scalars = [], [], [], []
    for i in range(count):
        y = streams[i]
        value = jnp.where(at == 0, jnp.sum(grad_sum * y, axis=-1, keepdims=True), 0.0)
        for j in range(count):
            value = jnp.where(at == 1 + j, jnp.sum(grad_carried[j] * y, axis=-1, keepdims=True), value)
        value = jnp.where(at == 1 + count, grad_beta[i], value)
        grad_pre = value * (1.0 - tanhs[i] * tanhs[i])
        high = grad_pre.astype(BF16).astype(F32)
        low = grad_pre - high
        both.append((high + pltpu.roll(low, 8, 1)).astype(BF16))
        grads.append(value)
        normed.append((y - column(packed[i], 6)) * column(packed[i], 7))
        scalars.append((
            jnp.sum(grad_pre * weight_mean, axis=-1, keepdims=True),
            jnp.sum(jnp.where(at < 6, grad_pre * packed[i], 0.0), axis=-1, keepdims=True) / width,
        ))
    both = jnp.concatenate(both, axis=0)
    grad_normed = dot(both, weight_rows)
    mixing_sum = dot(both, jnp.concatenate([n.astype(BF16) for n in normed], axis=0), TN)
    out = []
    for i in range(count):
        value = column(coefficients[i], 0) * grad_sum
        for j in range(count):
            value = value + column(coefficients[i], 1 + j) * grad_carried[j]
        a, b = scalars[i]
        out.append(
            value + column(packed[i], 7) * (grad_normed[i * rows : (i + 1) * rows] - a - normed[i] * b)
        )
    return out, mixing_sum, grads


def load_streams(ref):
    return [ref[i].astype(F32) for i in range(ref.shape[0])]


def coefficients_of(packed, static):
    return [static[i : i + 1] + jnp.tanh(packed[i]) for i in range(len(packed))]


def first_kernel(x_ref, weight_ref, static_ref, entering_ref, packed_ref, turned_ref):
    streams = [x_ref[:, i, :] for i in range(x_ref.shape[1])]
    for i, stream in enumerate(streams):
        turned_ref[i] = stream
    entering, _, packed = mix_forward([v.astype(F32) for v in streams], weight_ref[...], static_ref[...])
    entering_ref[...] = entering.astype(BF16)
    for i, value in enumerate(packed):
        packed_ref[i] = value


def middle_kernel(
    x_ref, packed_ref, static_ref, branch_ref, w_ref, weight_ref, static_next_ref,
    m_ref, entering_ref, down_ref, packed_next_ref,
):
    streams = load_streams(x_ref)
    count = len(streams)
    coefficients = coefficients_of([packed_ref[i] for i in range(count)], static_ref[...])
    branch = branch_ref[...]
    middle = []
    for j in range(count):
        middle.append(mix_carry(streams, coefficients, j) + column(coefficients[j], 5) * branch)
        m_ref[j] = middle[j]
    entering, following, packed = mix_forward(middle, weight_ref[...], static_next_ref[...])
    entering_ref[...] = entering.astype(BF16)
    for i, value in enumerate(packed):
        packed_next_ref[i] = value
    down_ref[...] = sum(column(following[j], 5) * w_ref[j].astype(F32) for j in range(count)).astype(BF16)


def total(refs):
    return sum(ref[...].astype(F32) for ref in refs)


def out_kernel(m_ref, packed_ref, static_ref, *refs):
    out_ref = refs[-1]
    streams = load_streams(m_ref)
    count = len(streams)
    coefficients = coefficients_of([packed_ref[i] for i in range(count)], static_ref[...])
    z = total(refs[:-1])
    for j in range(count):
        out_ref[:, j, :] = (mix_carry(streams, coefficients, j) + column(coefficients[j], 5) * z).astype(BF16)


def accumulate(step, mixing_ref, static_ref, mixing_sum, grads):
    @pl.when(step == 0)
    def _():
        mixing_ref[...] = jnp.zeros_like(mixing_ref)
        static_ref[...] = jnp.zeros_like(static_ref)

    mixing_ref[...] += mixing_sum
    at = lax.broadcasted_iota(jnp.int32, static_ref.shape, 0)
    sums = jnp.zeros(static_ref.shape, F32)
    for i, grad in enumerate(grads):
        sums = jnp.where(at == i, jnp.sum(grad, axis=0, keepdims=True), sums)
    static_ref[...] += sums


def middle_back_kernel(
    terms, m_ref, packed_ref, static_ref, packed_first_ref, static_first_ref, w_ref, branch_ref,
    weight_rows_ref, weight_mean_ref, *refs,
):
    grad_m_ref, grad_branch_ref, grad_beta_ref, mixing_ref, static_sum_ref = refs[2 * terms :]
    streams = load_streams(m_ref)
    count = len(streams)
    cotangent = load_streams(w_ref)
    z = total(refs[:terms])
    grad_entering = total(refs[terms : 2 * terms])
    grad_beta = [jnp.sum(w * z, axis=-1, keepdims=True) for w in cotangent]
    grads, mixing_sum, grad_pres = mix_backward(
        streams, [packed_ref[i] for i in range(count)], static_ref[...], grad_entering, cotangent, grad_beta,
        weight_rows_ref[...], weight_mean_ref[...],
    )
    accumulate(pl.program_id(0), mixing_ref, static_sum_ref, mixing_sum, grad_pres)
    first = coefficients_of([packed_first_ref[i] for i in range(count)], static_first_ref[...])
    branch = branch_ref[...]
    at = lane(grad_beta_ref.shape)
    beta = jnp.zeros(grad_beta_ref.shape, F32)
    for j in range(count):
        grad_m_ref[j] = grads[j]
        beta = jnp.where(at == j, jnp.sum(grads[j] * branch, axis=-1, keepdims=True), beta)
    grad_beta_ref[...] = beta
    grad_branch_ref[...] = sum(column(first[j], 5) * grads[j] for j in range(count)).astype(BF16)


def first_back_kernel(
    x_ref, packed_ref, static_ref, grad_m_ref, grad_beta_ref, weight_rows_ref, weight_mean_ref, *refs
):
    grad_ref, mixing_ref, static_sum_ref = refs[-3:]
    streams = load_streams(x_ref)
    count = len(streams)
    grad_entering = total(refs[:-3])
    beta = grad_beta_ref[...]
    grads, mixing_sum, grad_pres = mix_backward(
        streams, [packed_ref[i] for i in range(count)], static_ref[...], grad_entering,
        [grad_m_ref[i] for i in range(count)], [column(beta, i) for i in range(count)],
        weight_rows_ref[...], weight_mean_ref[...],
    )
    accumulate(pl.program_id(0), mixing_ref, static_sum_ref, mixing_sum, grad_pres)
    for i in range(count):
        grad_ref[:, i, :] = grads[i]


def token_call(kernel, tokens, operands, outputs, flops=0, mib=40):
    block = 32 if tokens % 32 == 0 else tokens

    def spec(shape):
        if tokens not in shape[:-1]:
            return pl.BlockSpec(shape, lambda i, n=len(shape): (0,) * n)
        axis = shape.index(tokens)
        cut = tuple(block if d == axis else s for d, s in enumerate(shape))
        return pl.BlockSpec(cut, lambda i, axis=axis, n=len(shape): tuple(i if d == axis else 0 for d in range(n)))

    size = sum(math.prod(o.shape) * o.dtype.itemsize for o in list(operands) + list(outputs))
    return pl.pallas_call(
        kernel,
        grid=(tokens // block,),
        in_specs=[spec(o.shape) for o in operands],
        out_specs=[spec(o.shape) for o in outputs],
        out_shape=list(outputs),
        compiler_params=params(mib),
        cost_estimate=NO_COST,
    )(*operands)


def rows_of(operand):
    return operand[0].shape[0] // 2 if isinstance(operand, tuple) else operand.shape[0]


def whole_of(operand):
    return operand[0] if isinstance(operand, tuple) else operand


def half_of(operand):
    return operand[1] if isinstance(operand, tuple) else 0


def tile_of(size):
    return next((t for t in (512, 384, 256, 128) if size % t == 0), size)


def product_kernel(dims, added, a_ref, b_ref, *refs):
    out = dot(a_ref[...], b_ref[...], dims)
    if added:
        out = out + refs[0][...].astype(F32)
    refs[-1][...] = out.astype(refs[-1].dtype)


def product(a, b, dims=NN, add=None, into=None, filled=()):
    rows, depth = rows_of(a), whole_of(a).shape[1]
    half, columns = half_of(a), b.shape[0] if dims == NT else b.shape[1]
    tile = tile_of(columns)
    operands = [whole_of(a), b] + ([] if add is None else [add]) + list(filled)
    specs = [
        pl.BlockSpec((rows, depth), lambda j: (half, 0)),
        pl.BlockSpec((tile, depth), lambda j: (j, 0)) if dims == NT else pl.BlockSpec((depth, tile), lambda j: (0, j)),
    ]
    if add is not None:
        specs.append(pl.BlockSpec((rows, tile), lambda j: (0, j)))
    specs += [pl.BlockSpec(memory_space=pl.ANY)] * len(filled)
    at = into or 0
    return pl.pallas_call(
        functools.partial(product_kernel, dims, add is not None),
        grid=(columns // tile,),
        in_specs=specs,
        out_specs=pl.BlockSpec((rows, tile), lambda j: (at, j)),
        out_shape=jax.ShapeDtypeStruct((rows if into is None else 2 * rows, columns), BF16),
        input_output_aliases={len(operands) - 1: 0} if filled else {},
        compiler_params=params(40),
        cost_estimate=NO_COST,
    )(*operands)


def columns_product_kernel(units, reps, me_ref, x0, x1, y0, y1, *refs):
    outs, sums = refs[:-1], refs[-1]
    sums[...] = dot(x0[...], y0[...], TN) + dot(x1[...], y1[...], TN)
    step = pl.program_id(0)
    size = pl.num_programs(0) // units
    part = sums.shape[0] // reps
    for u in range(units):
        @pl.when(step // size == u)
        def _(u=u):
            for m in range(reps):
                row = pl.multiple_of((me_ref[0] ^ m) * part, part)
                outs[u * reps + m][0] = sums[pl.ds(row, part), :].astype(BF16)


def columns_product(xs, ys, units):
    shards, reps = lax.axis_size("shard"), lax.axis_size("rep")
    tokens, columns = rows_of(ys[0]), whole_of(ys[0]).shape[1]
    rows = whole_of(xs[0]).shape[1] // shards
    size, part = shards // units, rows // reps
    x_specs = [pl.BlockSpec((tokens, rows), lambda s, me, h=half_of(x): (h, s)) for x in xs]
    y_specs = [pl.BlockSpec((tokens, columns), lambda s, me, h=half_of(y): (h, 0)) for y in ys]
    out = pl.pallas_call(
        functools.partial(columns_product_kernel, units, reps),
        grid_spec=pltpu.PrefetchScalarGridSpec(
            num_scalar_prefetch=1,
            grid=(shards,),
            in_specs=x_specs + y_specs,
            out_specs=[
                pl.BlockSpec((1, part, columns), lambda s, me, u=u: (jnp.clip(s - u * size, 0, size - 1), 0, 0))
                for u in range(units) for _ in range(reps)
            ],
            scratch_shapes=[pltpu.VMEM((rows, columns), F32)],
        ),
        out_shape=[jax.ShapeDtypeStruct((size, part, columns), BF16)] * (units * reps),
        compiler_params=params(48),
        cost_estimate=NO_COST,
    )(lax.axis_index("rep").astype(jnp.int32)[None], *[whole_of(v) for v in [*xs, *ys]])
    return [out[u * reps : (u + 1) * reps] for u in range(units)]


def rows_product_kernel(units, reps, me_ref, x0, x1, y0, y1, *refs):
    outs, sums = refs[:-1], refs[-1]
    sums[...] = dot(x0[...], y0[...], TN) + dot(x1[...], y1[...], TN)
    part = outs[0].shape[0]
    for u in range(units):
        for m in range(reps):
            row = pl.multiple_of((me_ref[0] ^ m) * (units * part) + u * part, part)
            outs[u * reps + m][...] = sums[pl.ds(row, part), :].astype(BF16)


def rows_product(xs, ys, units):
    reps = lax.axis_size("rep")
    tokens, columns = rows_of(ys[0]), whole_of(ys[0]).shape[1]
    rows = whole_of(xs[0]).shape[1]
    part, tile = rows // (units * reps), tile_of(columns)
    x_specs = [pl.BlockSpec((tokens, rows), lambda j, me, h=half_of(x): (h, 0)) for x in xs]
    y_specs = [pl.BlockSpec((tokens, tile), lambda j, me, h=half_of(y): (h, j)) for y in ys]
    out = pl.pallas_call(
        functools.partial(rows_product_kernel, units, reps),
        grid_spec=pltpu.PrefetchScalarGridSpec(
            num_scalar_prefetch=1,
            grid=(columns // tile,),
            in_specs=x_specs + y_specs,
            out_specs=[pl.BlockSpec((part, tile), lambda j, me: (0, j))] * (units * reps),
            scratch_shapes=[pltpu.VMEM((rows, tile), F32)],
        ),
        out_shape=[jax.ShapeDtypeStruct((part, columns), BF16)] * (units * reps),
        compiler_params=params(48),
        cost_estimate=NO_COST,
    )(lax.axis_index("rep").astype(jnp.int32)[None], *[whole_of(v) for v in [*xs, *ys]])
    return [out[u * reps : (u + 1) * reps] for u in range(units)]


def ffn_tile(hidden):
    return 256 if hidden % 256 == 0 else hidden


def chunks(rows):
    step = 320 if rows % 320 == 0 else rows
    return [slice(i, i + step) for i in range(0, rows, step)]


def ffn_kernel(x_ref, gate_ref, up_ref, *refs):
    active_ref, by_gate_ref, by_up_ref = refs[-3:]
    for cut in chunks(x_ref.shape[0]):
        gate = dot(x_ref[cut, :], gate_ref[...])
        up = dot(x_ref[cut, :], up_ref[...])
        sigmoid = 1.0 / (1.0 + jnp.exp2(gate * -LOG2E))
        swish = gate * sigmoid
        active_ref[cut, :] = (swish * up).astype(BF16)
        by_gate_ref[cut, :] = (up * sigmoid * (1.0 + gate - swish)).astype(BF16)
        by_up_ref[cut, :] = swish.astype(BF16)


def ffn_forward(x, weight, half, filled=()):
    rows, width = x.shape
    hidden = weight.shape[1] // 2
    tile = ffn_tile(hidden)
    tiles = hidden // tile
    return pl.pallas_call(
        ffn_kernel,
        grid=(tiles,),
        in_specs=[
            pl.BlockSpec((rows, width), lambda j: (0, 0)),
            pl.BlockSpec((width, tile), lambda j: (0, j)),
            pl.BlockSpec((width, tile), lambda j: (0, j + tiles)),
        ] + [pl.BlockSpec(memory_space=pl.ANY)] * len(filled),
        out_specs=[pl.BlockSpec((rows, tile), lambda j: (half, j))] * 3,
        out_shape=[jax.ShapeDtypeStruct((2 * rows, hidden), BF16)] * 3,
        input_output_aliases={3 + i: i for i in range(len(filled))},
        compiler_params=params(40),
        cost_estimate=NO_COST,
    )(x, weight, weight, *filled)


def ffn_back_kernel(tiles, x_ref, down_ref, by_gate_ref, by_up_ref, *refs):
    out_ref = refs[-1]
    step = pl.program_id(0)
    tile = down_ref.shape[0]
    for cut in chunks(x_ref.shape[0]):
        grad = dot(x_ref[cut, :], down_ref[...], NT)
        first = pl.multiple_of(step * tile, tile)
        second = pl.multiple_of((step + tiles) * tile, tile)
        out_ref[cut, pl.ds(first, tile)] = (grad * by_gate_ref[cut, :].astype(F32)).astype(BF16)
        out_ref[cut, pl.ds(second, tile)] = (grad * by_up_ref[cut, :].astype(F32)).astype(BF16)


def ffn_backward(x, down, by_gate, by_up, half, filled=()):
    rows, width = x.shape
    hidden = down.shape[0]
    tile = ffn_tile(hidden)
    tiles = hidden // tile
    return pl.pallas_call(
        functools.partial(ffn_back_kernel, tiles),
        grid=(tiles,),
        in_specs=[
            pl.BlockSpec((rows, width), lambda j: (0, 0)),
            pl.BlockSpec((tile, width), lambda j: (j, 0)),
            pl.BlockSpec((rows, tile), lambda j: (half, j)),
            pl.BlockSpec((rows, tile), lambda j: (half, j)),
        ] + [pl.BlockSpec(memory_space=pl.ANY)] * len(filled),
        out_specs=pl.BlockSpec((rows, 2 * hidden), lambda j: (half, 0)),
        out_shape=jax.ShapeDtypeStruct((2 * rows, 2 * hidden), BF16),
        input_output_aliases={4 + i: i for i in range(len(filled))},
        compiler_params=params(40),
        cost_estimate=NO_COST,
    )(x, down, by_gate, by_up, *filled)


def turn(values):
    return pltpu.roll(values, values.shape[-1] // 2, 1)


def allowed(place_ref, query_place, query_start):
    keys = place_ref[...]
    return (keys <= query_place) & (keys >= query_start)


def attend_kernel(
    heads, width, q_ref, k_ref, v_ref, cos_q, sin_q, cos_k, sin_k, key_place, query_place, query_start,
    out_ref, rot_q_ref, rot_k_ref, log_ref, value_t,
):
    scale = width ** (-0.5)

    @pl.when(pl.program_id(0) == 0)
    def _():
        for h in range(heads):
            cut = slice(h * width, (h + 1) * width)
            key = k_ref[:, cut].astype(F32)
            rot_k_ref[:, cut] = (key * cos_k[...] + turn(key) * sin_k[...]).astype(BF16)
            value_t[cut, :] = v_ref[:, cut].T

    mask = allowed(key_place, query_place[...], query_start[...])
    for h in range(heads):
        cut = slice(h * width, (h + 1) * width)
        query = q_ref[:, cut].astype(F32)
        query = (query * cos_q[...] + turn(query) * sin_q[...]).astype(BF16)
        rot_q_ref[:, cut] = query
        scores = jnp.where(mask, dot(rot_k_ref[:, cut], query, NT), NEGATIVE)
        top = jnp.max(scores, axis=0, keepdims=True)
        weights = jnp.exp2((scores - top) * (scale * LOG2E))
        total = jnp.sum(weights, axis=0, keepdims=True)
        weights = (weights * (1.0 / total)).astype(BF16)
        out_ref[:, cut] = dot(value_t[cut, :], weights).T.astype(BF16)
        log_ref[h : h + 1] = top * (scale * LOG2E) + jnp.log2(total)


def attend_back_kernel(
    heads, width, q_ref, k_ref, v_ref, grad_ref, log_ref, cos_q, sin_q, cos_k, sin_k, key_place, query_place,
    query_start, out_ref, key_t, sum_k, sum_v,
):
    scale = width ** (-0.5)
    step = pl.program_id(0)
    block = q_ref.shape[0]
    here = pl.ds(pl.multiple_of(step * block, block), block)

    @pl.when(step == 0)
    def _():
        for h in range(heads):
            cut = slice(h * width, (h + 1) * width)
            key_t[cut, :] = k_ref[:, cut].T
        sum_k[...] = jnp.zeros_like(sum_k)
        sum_v[...] = jnp.zeros_like(sum_v)

    mask = allowed(key_place, query_place[...], query_start[...])
    for h in range(heads):
        cut = slice(h * width, (h + 1) * width)
        query = q_ref[:, cut]
        grad = grad_ref[:, cut]
        scores = dot(k_ref[:, cut], query, NT) * (scale * LOG2E) - log_ref[h : h + 1]
        weights = jnp.exp2(jnp.where(mask, scores, NEGATIVE))
        grad_weights = dot(v_ref[:, cut], grad, NT)
        centre = jnp.sum(weights * grad_weights, axis=0, keepdims=True)
        grad_scores = (weights * (grad_weights - centre)).astype(BF16)
        grad_query = (dot(key_t[cut, :], grad_scores) * scale).T
        out_ref[here, cut] = (grad_query * cos_q[...] - turn(grad_query) * sin_q[...]).astype(BF16)
        sum_k[:, cut] += dot(grad_scores, query)
        sum_v[:, cut] += dot(weights.astype(BF16), grad)

    @pl.when(step == pl.num_programs(0) - 1)
    def _():
        for h in range(heads):
            cut = slice(h * width, (h + 1) * width)
            key = sum_k[:, cut] * scale
            second = slice((heads + h) * width, (heads + h + 1) * width)
            third = slice((2 * heads + h) * width, (2 * heads + h + 1) * width)
            out_ref[:, second] = (key * cos_k[...] - turn(key) * sin_k[...]).astype(BF16)
            out_ref[:, third] = sum_v[:, cut].astype(BF16)


def attention(qkv, cosine, sine, place, start, heads):
    tokens, width = qkv.shape[0], qkv.shape[1] // 3
    head_width = width // heads
    block = 256 if tokens % 256 == 0 else tokens
    row = lambda i: (i, 0)
    whole = lambda i: (0, 0)
    along = lambda i: (0, i)
    key_place = jnp.broadcast_to(place[:, None], (tokens, block))
    blocks = tokens // block
    return pl.pallas_call(
        functools.partial(attend_kernel, heads, head_width),
        grid=(blocks,),
        in_specs=[
            pl.BlockSpec((block, width), row),
            pl.BlockSpec((tokens, width), lambda i: (0, 1)),
            pl.BlockSpec((tokens, width), lambda i: (0, 2)),
            pl.BlockSpec((block, head_width), row),
            pl.BlockSpec((block, head_width), row),
            pl.BlockSpec((tokens, head_width), whole),
            pl.BlockSpec((tokens, head_width), whole),
            pl.BlockSpec((tokens, block), whole),
            pl.BlockSpec((1, block), along),
            pl.BlockSpec((1, block), along),
        ],
        out_specs=[
            pl.BlockSpec((block, width), row),
            pl.BlockSpec((block, width), row),
            pl.BlockSpec((tokens, width), whole),
            pl.BlockSpec((heads, block), along),
        ],
        out_shape=[
            jax.ShapeDtypeStruct((tokens, width), BF16),
            jax.ShapeDtypeStruct((tokens, width), BF16),
            jax.ShapeDtypeStruct((tokens, width), BF16),
            jax.ShapeDtypeStruct((heads, tokens), F32),
        ],
        scratch_shapes=[pltpu.VMEM((width, tokens), BF16)],
        compiler_params=params(48),
        cost_estimate=NO_COST,
    )(qkv, qkv, qkv, cosine, sine, cosine, sine, key_place, place[None], start[None])


def attention_back(qkv, rot_q, rot_k, grad, logs, cosine, sine, place, start, heads):
    tokens, width = rot_q.shape
    head_width = width // heads
    block = 256 if tokens % 256 == 0 else tokens
    row = lambda i: (i, 0)
    whole = lambda i: (0, 0)
    along = lambda i: (0, i)
    key_place = jnp.broadcast_to(place[:, None], (tokens, block))
    return pl.pallas_call(
        functools.partial(attend_back_kernel, heads, head_width),
        grid=(tokens // block,),
        in_specs=[
            pl.BlockSpec((block, width), row),
            pl.BlockSpec((tokens, width), whole),
            pl.BlockSpec((tokens, width), lambda i: (0, 2)),
            pl.BlockSpec((block, width), row),
            pl.BlockSpec((heads, block), along),
            pl.BlockSpec((block, head_width), row),
            pl.BlockSpec((block, head_width), row),
            pl.BlockSpec((tokens, head_width), whole),
            pl.BlockSpec((tokens, head_width), whole),
            pl.BlockSpec((tokens, block), whole),
            pl.BlockSpec((1, block), along),
            pl.BlockSpec((1, block), along),
        ],
        out_specs=pl.BlockSpec((tokens, 3 * width), whole),
        out_shape=jax.ShapeDtypeStruct((tokens, 3 * width), BF16),
        scratch_shapes=[
            pltpu.VMEM((width, tokens), BF16),
            pltpu.VMEM((tokens, width), F32),
            pltpu.VMEM((tokens, width), F32),
        ],
        compiler_params=params(56),
        cost_estimate=NO_COST,
    )(rot_q, rot_k, qkv, grad, logs, cosine, sine, cosine, sine, key_place, place[None], start[None])


def sequence_places(ordering, lengths):
    ending = jnp.cumsum(lengths)
    segment = jnp.sum((ordering[:, None] >= ending[None, :]).astype(jnp.int32), axis=1)
    opening = ending - lengths
    chosen = segment[:, None] == jnp.arange(lengths.shape[0], dtype=jnp.int32)[None, :]
    return jnp.sum(jnp.where(chosen, opening[None, :], 0), axis=1)


def rope_tables(position, head_width):
    middle = head_width // 2
    frequency = jnp.exp(
        jnp.arange(middle, dtype=F32) * (-2.0 * math.log(10000.0) / head_width)
    )
    angles = position.astype(F32)[:, None] * frequency[None, :]
    sine = jnp.sin(angles)
    cosine = jnp.cos(angles)
    return jnp.concatenate([cosine, cosine], axis=1), jnp.concatenate([-sine, sine], axis=1)


def per_device(
    streams, cotangent, lengths, packed_at, query_weight, key_weight, value_weight, output_weight,
    gate_weight, up_weight, down_weight, mixing_weight, mixing_static,
):
    shards = lax.axis_size("shard")
    line = shards // 2
    me = lax.axis_index("shard")
    spot, core = me // 2, me % 2
    tokens, count, width = streams.shape
    head_width = width // HEADS
    heads = HEADS // shards
    local = heads * head_width
    shape = jax.ShapeDtypeStruct

    rounds = Rounds()
    run, also, then, tie, hold, finish = (
        rounds.run, rounds.also, rounds.then, rounds.tie, rounds.hold, rounds.finish
    )
    me_rep = lax.axis_index("rep")

    gather_mixing = Task(mixing_gather(mixing_weight))
    recut_qkv = Task(chip_exchange(recut_piece([query_weight, key_weight, value_weight])))
    run(gather_mixing, recut_qkv)
    run(gather_mixing, recut_qkv)
    finish(gather_mixing)
    mixing_rows = gather_mixing.value
    mixing_mean = jnp.sum(mixing_rows.astype(F32), axis=2)[:, None, :] / width
    static = jnp.pad(mixing_static, ((0, 0), (0, 0), (0, LANES - 6)))
    entering, packed, x = token_call(
        first_kernel, tokens, [streams, mixing_rows[0], static[0]],
        [
            shape((tokens, width), BF16), shape((count, tokens, LANES), F32),
            shape((count, tokens, width), BF16),
        ],
    )
    part = output_weight.shape[0] // lax.axis_size("rep")
    output_part = lax.dynamic_slice_in_dim(output_weight, me_rep * part, part, 0)
    gather_in = Task(line_gather(jnp.concatenate([entering, output_part], axis=0)))
    finish(recut_qkv)
    gather_qkv = Task(rep_gather(stack_units(recut_qkv.value, 2), True))
    run(gather_in, gather_qkv)
    gate_up_piece = recut_piece([tie(gate_weight), up_weight])
    run(gather_in, gather_qkv)
    hold(gate_up_piece)

    places = tie(packed_at)[0].reshape(line, 2, tokens)
    turned = jnp.roll(places, -spot, axis=0)
    place = jnp.concatenate(
        [
            lax.dynamic_index_in_dim(turned, core, 1, keepdims=False).reshape(-1),
            lax.dynamic_index_in_dim(turned, 1 - core, 1, keepdims=False).reshape(-1),
        ]
    )
    start = sequence_places(place, lengths[0])
    cosine, sine = rope_tables(place - start, head_width)
    w = tie(cotangent).transpose(1, 0, 2)
    run(gather_in)
    hold(cosine, sine, w)
    finish(gather_in, gather_qkv)
    gathered = gather_in.value.reshape(line, tokens + part, width)
    mine_in = gathered[:, :tokens].reshape(line * tokens, width)
    swap = Task(other_core(mine_in))
    gather_output = Task(rep_gather(cut_units(gathered[:, tokens:], 2), True))
    recut_gate_up = Task(shard_exchange(gate_up_piece, (shards // 4, 3 * shards // 8, shards // 8)))
    run(swap, recut_gate_up, gather_output)
    attention_weight = recut_join(gather_qkv.value)
    hold(attention_weight)
    mine_qkv = product(mine_in, attention_weight, into=0)
    other_in = swap.value
    run(recut_gate_up, gather_output)
    qkv = product(other_in, attention_weight, into=1, filled=(mine_qkv,))
    attended, rot_q, rot_k, logs = attention(qkv, cosine, sine, place, start, heads)
    finish(gather_output)
    hold(attended)
    gate_up_low = [lax.dynamic_index_in_dim(gate_up_piece, me, 0, keepdims=False)]
    gate_up_low += recut_gate_up.arrived[: shards // 2 - 1]
    gather_low = Task(rep_gather(stack_units(gate_up_low, 2), True))
    tokens_out = Task(to_tokens(attended.reshape(2, line, tokens, local)))
    run(tokens_out, recut_gate_up, gather_low)
    output_mine = rows_in_order(gather_output.value)
    swap = Task(other_core(output_mine))
    run(tokens_out, swap, recut_gate_up)
    branch = dot(tokens_out.value[0], output_mine) + dot(tokens_out.value[1], swap.value)

    middle, entering_next, down_in, packed_next = token_call(
        middle_kernel, tokens,
        [x, packed, static[0], branch, w, mixing_rows[1], static[1]],
        [
            shape((count, tokens, width), F32), shape((tokens, width), BF16),
            shape((tokens, width), BF16), shape((count, tokens, LANES), F32),
        ],
    )
    finish(recut_gate_up)
    gather_high = Task(rep_gather(stack_units(recut_gate_up.value[shards // 2 :], 2), True))
    gather_ffn, gather_down = Task(direct_gather(entering_next, 2)), Task(direct_gather(down_in, 2))
    run(gather_ffn, gather_low)
    finish(gather_low)
    gate_up = recut_join(gather_low.value)
    run(gather_ffn, gather_high)
    finish(gather_ffn)
    mine_ffn = gather_ffn.value
    swap = Task(other_core(mine_ffn))
    run(gather_down, swap, gather_high)
    finish(gather_high)
    gate_up = recut_join(gather_high.value, shards // 2, (gate_up,))
    hidden = gate_up.shape[1] // 2
    filled = ffn_forward(mine_ffn, gate_up, 0)
    other_ffn = swap.value
    run(gather_down)
    active, by_gate, by_up = ffn_forward(other_ffn, gate_up, 1, filled)
    theirs = product((active, 1), down_weight)
    finish(gather_down)
    mine_down = gather_down.value
    swap_z, swap = Task(other_core(theirs)), Task(other_core(mine_down))
    run(swap_z, swap)
    filled = ffn_backward(mine_down, down_weight, by_gate, by_up, 0)
    other_down = swap.value
    scatter_z = Task(direct_scatter(product((active, 0), down_weight, add=swap_z.value), 2))
    run(scatter_z)
    grad_both = ffn_backward(other_down, down_weight, by_gate, by_up, 1, (filled,))
    theirs = product((grad_both, 1), gate_up, NT)
    hold(theirs)
    swap = Task(other_core(theirs))
    run(scatter_z, swap)
    gate_up_blocks = columns_product([mine_ffn, other_ffn], [(grad_both, 0), (grad_both, 1)], 2)
    hold(*gate_up_blocks[0])
    finish(scatter_z)
    scatter_f = Task(direct_scatter(product((grad_both, 0), gate_up, NT, add=swap.value), 2))
    scatter_gate_up = Task(rep_scatter(gate_up_blocks))
    run(scatter_f, (scatter_gate_up, 1))
    down_blocks = rows_product([(active, 0), (active, 1)], [mine_down, other_down], 2)
    hold(*down_blocks[0])
    run(scatter_f, scatter_gate_up)
    finish(scatter_f)

    grad_middle, grad_branch, grad_beta, mixing_sum_next, static_sum_next = token_call(
        functools.partial(middle_back_kernel, line), tokens,
        [
            middle, packed_next, static[1], packed, static[0], w, branch, mixing_rows[1], mixing_mean[1],
            *scatter_z.value, *scatter_f.value,
        ],
        [
            shape((count, tokens, width), F32), shape((tokens, width), BF16), shape((tokens, LANES), F32),
            shape((LANES, width), F32), shape((8, LANES), F32),
        ],
    )
    gather_branch = Task(direct_gather(grad_branch, 2))
    run(gather_branch, scatter_gate_up)
    finish(scatter_gate_up)
    low = []
    recut_grad = Task(chip_exchange(jnp.concatenate(scatter_gate_up.value, axis=0), (line // 4, line // 4), low))
    (result,) = token_call(
        out_kernel, tokens, [tie(middle), packed_next, static[1], *scatter_z.value],
        [shape((tokens, count, width), BF16)],
    )
    scatter_down = Task(rep_scatter(down_blocks, True))
    run(gather_branch, scatter_down)
    hold(result)
    finish(gather_branch)
    mine_branch = gather_branch.value
    swap = Task(other_core(mine_branch))
    run(swap, scatter_down, recut_grad)
    finish(scatter_down)
    gather_down_rows = Task(rep_gather(scatter_down.value, True))
    grad_mine = product(mine_branch, output_weight, NT, into=0)
    other_branch = swap.value
    run(recut_grad, gather_down_rows)
    grad_attended = product(other_branch, output_weight, NT, into=1, filled=(grad_mine,))
    grad_qkv = attention_back(qkv, rot_q, rot_k, grad_attended, logs, cosine, sine, place, start, heads)
    theirs = product((grad_qkv, 1), attention_weight, NT)
    run(recut_grad, gather_down_rows)
    gather_low = Task(rep_gather(stack_units(low[: shards // 2], 2), True))
    hold(theirs)
    run(recut_grad, gather_low)
    qkv_blocks = columns_product([mine_in, other_in], [(grad_qkv, 0), (grad_qkv, 1)], 2)
    output_blocks = rows_product([(attended, 0), (attended, 1)], [mine_branch, other_branch], 2)
    hold(*qkv_blocks[0], *output_blocks[0])
    finish(recut_grad, gather_down_rows)
    gather_high = Task(rep_gather(stack_units(low[shards // 2 :], 2), True))
    swap = Task(other_core(theirs))
    scatter_output = Task(rep_scatter(output_blocks, True))
    run(swap, scatter_output)
    down_rows = rows_join(gather_down_rows.value)
    hold(down_rows)
    scatter_a = Task(direct_scatter(product((grad_qkv, 0), attention_weight, NT, add=swap.value), 2))
    scatter_qkv = Task(rep_scatter(qkv_blocks, True))
    run(scatter_a, scatter_qkv)
    run(scatter_a, scatter_qkv, gather_low)
    finish(scatter_qkv, scatter_a, gather_low)
    recut_qkv_grad = Task(chip_exchange(jnp.concatenate(scatter_qkv.value, axis=0)))
    grad_streams, mixing_sum, static_sum = token_call(
        first_back_kernel, tokens,
        [x, packed, static[0], grad_middle, grad_beta, mixing_rows[0], mixing_mean[0], *scatter_a.value],
        [shape((tokens, count, width), F32), shape((LANES, width), F32), shape((8, LANES), F32)],
    )
    run(recut_qkv_grad, gather_high, scatter_output)
    hold(grad_streams)
    run(recut_qkv_grad, gather_high)
    finish(recut_qkv_grad, gather_high, scatter_output)
    gather_qkv_grad = Task(rep_gather(stack_units(recut_qkv_grad.value, 2), True))
    gather_output = Task(rep_gather(scatter_output.value, True))
    mixing_sums = jnp.stack([mixing_sum, mixing_sum_next])
    mixing_sums = (mixing_sums[:, :6] + mixing_sums[:, 8:14]).reshape(12, shards, -1)
    small = jnp.concatenate(
        [
            jnp.pad(mixing_sums.transpose(1, 0, 2), ((0, 0), (0, 4), (0, 0))),
            jnp.broadcast_to(jnp.concatenate([static_sum, static_sum_next])[None], (shards, 16, LANES)),
        ],
        axis=2,
    )
    sum_last = Task(sum_small(small))
    run(sum_last, gather_qkv_grad, gather_output)
    gate_rows, up_rows = columns_join([[tie(v) for v in u] for u in gather_low.value + gather_high.value], 2)
    run(sum_last, gather_qkv_grad)
    hold(gate_rows)
    run(sum_last, gather_output)
    finish(gather_qkv_grad, gather_output, sum_last)
    output_rows = rows_join(gather_output.value)
    small = sum_last.value
    rows = width // shards
    own_mixing = jnp.swapaxes(small[:12, :rows].reshape(2, 6, rows), 1, 2)
    static_sums = jnp.stack([small[0:count, rows : rows + 6], small[8 : 8 + count, rows : rows + 6]])
    query_rows, key_rows, value_rows = columns_join(gather_qkv_grad.value, 3)
    return (
        result, grad_streams, query_rows, key_rows, value_rows, output_rows,
        gate_rows, up_rows, down_rows, own_mixing, static_sums,
    )


def solution(mesh):
    tokens = P(("rep", "shard"), None, None)
    rows = P("shard", None)
    return jax.shard_map(
        per_device,
        mesh=mesh,
        in_specs=(tokens, tokens, P("rep", None), P("rep", None)) + (rows,) * 7 + (P(None, "shard", None), P()),
        out_specs=(tokens, tokens) + (rows,) * 7 + (P(None, "shard", None), P()),
        check_vma=False,
    )
```

time: 3140 us -> 873 us (0.28)
  waiting for transfers between devices: 2350 us -> 355 us
  matrix products: 455 us -> 1.75 us
  Pallas kernels: 0 us -> 237 us
  starting transfers between devices: 26.7 us -> 153 us
  other arithmetic: 124 us -> 46.6 us
  blocking collectives: 54 us -> 0 us
  local copies, waits for them, and re-layouts: 106 us -> 66.3 us
    all_gather x7 -> x0, waiting for transfers between devices: 906 us -> none  [the longest x1 270 us: per_device(): lax.all_gather(up_weight, 'shard', axis=0, tiled=True)]
    reduce_scatter x3 -> x0, waiting for transfers between devices: 867 us -> none  [reduce_gradient(): lax.psum_scatter(jnp.concatenate(columns, axis=1).astype(jnp.bfloat16), '...]
    dot_general x70 -> x2, matrix products: 455 us -> 1.75 us  [dot(): return lax.dot_general(a, b, dims, preferred_element_type=F32)]
    ppermute x0 -> x120, waiting for transfers between devices: none -> 355 us  [sender(): return lambda x: lax.ppermute(x, axis, pairs)]
    psum x2 -> x0, waiting for transfers between devices: 347 us -> none  [the longest x1 311 us: reduce_gradient(): return lax.psum(group_sum, 'rep').astype(jnp.float32)]
    pallas_call x0 -> x38, Pallas kernels: none -> 237 us  [the longest x9 60.4 us: token_call(): pl.pallas_call(kernel, grid=(tokens // block,), in_specs=[spec(o.shape) f...]
    all_to_all x4 -> x0, waiting for transfers between devices: 225 us -> none  [the longest x1 89.9 us: per_device(): lax.all_to_all(projected, 'shard', split_axis=2, concat_axis=0, tiled=True)]
    ppermute x0 -> x120, starting transfers between devices: none -> 153 us  [sender(): return lambda x: lax.ppermute(x, axis, pairs)]
  transfers between devices with their start and end apart: 16 -> 120, of which waited for: 14 -> 58; matrix products, arithmetic and copies ran while one was open for 19% -> 10% of each run, Pallas kernels for 0% -> 27%
where the time goes in v1:
time: 873 us; the launch traced here: 863 us
  waiting for transfers between devices  355 us (41%)
  Pallas kernels  237 us (27%)
  starting transfers between devices  153 us (18%)
  local copies, waits for them, and re-layouts  66.3 us (8%)
  other arithmetic  46.6 us (5%)
    ppermute x120, waiting for transfers between devices, sender(): return lambda x: lax.ppermute(x, axis, pairs)  355 us
    ppermute x120, starting transfers between devices, sender(): return lambda x: lax.ppermute(x, axis, pairs)  153 us
    pallas_call x9, Pallas kernels, token_call(): pl.pallas_call(kernel, grid=(tokens // block,), in_specs=[spec(o.shape) f...  60.4 us
    pallas_call x10, Pallas kernels, product(): pl.pallas_call(functools.partial(product_kernel, dims, add is not None),...  42.5 us
    unnamed x363, local copies, waits for them, and re-layouts  31.9 us
    pallas_call x2, Pallas kernels, columns_product(): pl.pallas_call(functools.partial(columns_product_kernel, units, reps), gr...  28.3 us
    pallas_call x6, Pallas kernels, join(): pl.pallas_call(functools.partial(columns_kernel, len(units), reps, parts)...  24.3 us
  transfers between devices with their start and end apart: 120, of which 58 were waited for; matrix products, arithmetic and copies ran while one was open for 10% of the time, Pallas kernels for 27%

profile of v1, /device:TPU:0, one launch (start us, length us, event | category | flops | bytes accessed | tf_op | source)
XLA Modules:
  0.0 863.2 jit_solution(17871986026354515142)
XLA Ops:
  19.1 11.5 %shard_map.213 = (bf16[160,2048]{1,0:T(8,128)(2,1)S(1)}, f32[4,160,128]{2,1,0:T(8,128)S(1)}, bf16[4,160,2048]{2,1,0:T(8,128)(2,1)S(1)}) custom-call(bf16[160,4,2048]{2,1,0:T(4,128)(2,1)S(1)} %copy-done.49, bf16[128,2048]{1,0:T(8,128)(2,1)S(1)} %get-tuple-element.485.weight_ref.weight_rows_ref, f32[4,128]{1,0:T(4,128)S(1)} %get-tuple-element.556.static_ref.static_first_ref), custom_call_target="tpu_custom_call" | custom-call | tf_op jit(solution)/shard_map/pallas_call | solution.py:663
  69.2 10.3 %collective-permute-done.14 = bf16[8,64,768]{2,1,0:T(8,128)(2,1)} collective-permute-done((bf16[8,64,768]{2,1,0:T(8,128)(2,1)S(1)}, bf16[8,64,768]{2,1,0:T(8,128)(2,1)}, u32[]{:S(2)}, u32[]{:S(2)}) %collective-permute-start.14) | collective-permute-done | bytes 786464 | tf_op jit(solution)/shard_map/ppermute | solution.py:100
  147.8 14.0 %shard_map.218 = (bf16[1280,256]{1,0:T(8,128)(2,1)S(1)}, bf16[1280,256]{1,0:T(8,128)(2,1)S(1)}, bf16[1280,256]{1,0:T(8,128)(2,1)S(1)}, f32[2,1280]{1,0:T(2,128)S(1)}) custom-call(bf16[1280,768]{1,0:T(8,128)(2,1)} %copy-done.6, bf16[1280,768]{1,0:T(8,128)(2,1)} %copy-done.6, bf16[1280,768]{1,0:T(8,128)(2,1)} %copy-done.6, ...), custom_call_target="tpu_custom_call" | custom-call | tf_op jit(solution)/shard_map/pallas_call | solution.py:961
  226.2 15.0 %collective-permute-done.37.refs_1_ = bf16[160,2048]{1,0:T(8,128)(2,1)S(1)} collective-permute-done((bf16[160,2048]{1,0:T(8,128)(2,1)S(1)}, bf16[160,2048]{1,0:T(8,128)(2,1)S(1)}, u32[]{:S(2)}, u32[]{:S(2)}) %collective-permute-start.37) | collective-permute-done | bytes 655392 | tf_op jit(solution)/shard_map/ppermute | solution.py:100
  241.2 13.7 %collective-permute-done.38.refs_3_ = bf16[160,2048]{1,0:T(8,128)(2,1)S(1)} collective-permute-done((bf16[160,2048]{1,0:T(8,128)(2,1)S(1)}, bf16[160,2048]{1,0:T(8,128)(2,1)S(1)}, u32[]{:S(2)}, u32[]{:S(2)}) %collective-permute-start.38) | collective-permute-done | bytes 655392 | tf_op jit(solution)/shard_map/ppermute | solution.py:100
  263.8 18.9 %collective-permute-done.41.refs_2_ = bf16[160,2048]{1,0:T(8,128)(2,1)S(1)} collective-permute-done((bf16[160,2048]{1,0:T(8,128)(2,1)S(1)}, bf16[160,2048]{1,0:T(8,128)(2,1)S(1)}, u32[]{:S(2)}, u32[]{:S(2)}) %collective-permute-start.41) | collective-permute-done | bytes 655392 | tf_op jit(solution)/shard_map/ppermute | solution.py:100
  291.5 14.7 %collective-permute-done.47.refs_3_ = bf16[160,2048]{1,0:T(8,128)(2,1)S(1)} collective-permute-done((bf16[160,2048]{1,0:T(8,128)(2,1)}, bf16[160,2048]{1,0:T(8,128)(2,1)S(1)}, u32[]{:S(2)}, u32[]{:S(2)}) %collective-permute-start.47) | collective-permute-done | bytes 655392 | tf_op jit(solution)/shard_map/ppermute | solution.py:100
  306.1 10.8 %collective-permute-done.48.refs_1_ = bf16[160,2048]{1,0:T(8,128)(2,1)S(1)} collective-permute-done((bf16[160,2048]{1,0:T(8,128)(2,1)}, bf16[160,2048]{1,0:T(8,128)(2,1)S(1)}, u32[]{:S(2)}, u32[]{:S(2)}) %collective-permute-start.48) | collective-permute-done | bytes 655392 | tf_op jit(solution)/shard_map/ppermute | solution.py:100
  395.9 19.5 %shard_map.233 = (bf16[4,64,2048]{2,1,0:T(8,128)(2,1)S(1)}, bf16[4,64,2048]{2,1,0:T(8,128)(2,1)}, bf16[4,64,2048]{2,1,0:T(8,128)(2,1)S(1)}, bf16[4,64,2048]{2,1,...) custom-call(s32[1]{0:T(128)} %bitcast.23.me_ref, ...), custom_call_target="tpu_custom_call" | custom-call | tf_op jit(solution)/shard_map/pallas_call | solution.py:743
  415.4 10.4 %collective-permute-done.54.refs_3_ = bf16[160,2048]{1,0:T(8,128)(2,1)S(1)} collective-permute-done((bf16[160,2048]{1,0:T(8,128)(2,1)}, bf16[160,2048]{1,0:T(8,128)(2,1)S(1)}, u32[]{:S(2)}, u32[]{:S(2)}) %collective-permute-start.54) | collective-permute-done | bytes 655392 | tf_op jit(solution)/shard_map/ppermute | solution.py:100
  440.9 10.3 %shard_map.234 = (bf16[128,2048]{1,0:T(8,128)(2,1)S(1)}, bf16[128,2048]{1,0:T(8,128)(2,1)S(1)}, bf16[128,2048]{1,0:T(8,128)(2,1)S(1)}, bf16[128,2048]{1,0:T(8,12...) custom-call(s32[1]{0:T(128)} %bitcast.23.me_ref, ...), custom_call_target="tpu_custom_call" | custom-call | tf_op jit(solution)/shard_map/pallas_call | solution.py:779
  456.6 10.9 %collective-permute-done.57.refs_6_ = bf16[160,2048]{1,0:T(8,128)(2,1)S(1)} collective-permute-done((bf16[160,2048]{1,0:T(8,128)(2,1)S(1)}, bf16[160,2048]{1,0:T(8,128)(2,1)S(1)}, u32[]{:S(2)}, u32[]{:S(2)}) %collective-permute-start.57) | collective-permute-done | bytes 655392 | tf_op jit(solution)/shard_map/ppermute | solution.py:100
  471.1 20.3 %collective-permute-done.61 = bf16[4,64,2048]{2,1,0:T(8,128)(2,1)S(1)} collective-permute-done((bf16[4,64,2048]{2,1,0:T(8,128)(2,1)S(1)}, bf16[4,64,2048]{2,1,0:T(8,128)(2,1)S(1)}, u32[]{:S(2)}, u32[]{:S(2)}) %collective-permute-start.61) | collective-permute-done | bytes 1048608 | tf_op jit(solution)/shard_map/ppermute | solution.py:100
  503.3 13.9 %shard_map.235 = (f32[4,160,2048]{2,1,0:T(8,128)}, bf16[160,2048]{1,0:T(8,128)(2,1)S(1)}, f32[160,128]{1,0:T(8,128)S(1)}, f32[128,2048]{1,0:T(8,128)S(1)}, f32[8,128]{1,0:T(8,128)S(1)}) custom-call(f32[4,160,2048]{2,1,0:T(8,128)} %copy-done.19, f32[4,160,128]{2,1,0:T(8,128)S(1)} %copy-done.78, f32[4,128]{1,0:T(4,128)S(1)} %copy-done.125, ...), custom_call_target="tpu_custom_call" | custom-call | tf_op jit(solution)/shard_map/pallas_call | solution.py:663
  521.7 15.1 %collective-permute-done.63.refs_3_ = bf16[160,2048]{1,0:T(8,128)(2,1)S(1)} collective-permute-done((bf16[160,2048]{1,0:T(8,128)(2,1)S(1)}, bf16[160,2048]{1,0:T(8,128)(2,1)S(1)}, u32[]{:S(2)}, u32[]{:S(2)}) %collective-permute-start.63) | collective-permute-done | bytes 655392 | tf_op jit(solution)/shard_map/ppermute | solution.py:100
  536.7 10.6 %collective-permute-done.64.refs_1_ = bf16[160,2048]{1,0:T(8,128)(2,1)S(1)} collective-permute-done((bf16[160,2048]{1,0:T(8,128)(2,1)S(1)}, bf16[160,2048]{1,0:T(8,128)(2,1)S(1)}, u32[]{:S(2)}, u32[]{:S(2)}) %collective-permute-start.64) | collective-permute-done | bytes 655392 | tf_op jit(solution)/shard_map/ppermute | solution.py:100
  559.1 18.8 %collective-permute-done.67.refs_2_ = bf16[160,2048]{1,0:T(8,128)(2,1)S(1)} collective-permute-done((bf16[160,2048]{1,0:T(8,128)(2,1)S(1)}, bf16[160,2048]{1,0:T(8,128)(2,1)S(1)}, u32[]{:S(2)}, u32[]{:S(2)}) %collective-permute-start.67) | collective-permute-done | bytes 655392 | tf_op jit(solution)/shard_map/ppermute | solution.py:100
  581.7 12.1 %collective-permute-done.72 = bf16[128,2048]{1,0:T(8,128)(2,1)S(1)} collective-permute-done((bf16[128,2048]{1,0:T(8,128)(2,1)S(1)}, bf16[128,2048]{1,0:T(8,128)(2,1)S(1)}, u32[]{:S(2)}, u32[]{:S(2)}) %collective-permute-start.72) | collective-permute-done | bytes 524320 | tf_op jit(solution)/shard_map/ppermute | solution.py:100
  618.1 17.4 %shard_map.240.a_ref.y0.y1 = bf16[1280,768]{1,0:T(8,128)(2,1)} custom-call(bf16[1280,256]{1,0:T(8,128)(2,1)} %copy-done.85, bf16[1280,256]{1,0:T(8,128)(2,1)} %copy-done.86, bf16[1280,768]{1,0:T(8,128)(2,1)} %copy-done.6, bf16[1280,256]{1,0:T(8,128)(2,1)} %copy-done.35, f32[2,1280]{1,0:T(2,128)} %copy-done.128, f32[1280,128]{1,0:T(8,128)} %copy-done.20, ...), custom_call_target="tpu_custom_call" | custom-call | tf_op jit(solution)/shard_map/pallas_call | solution.py:1002
  738.8 16.2 %collective-permute-done.90.refs_3_ = bf16[160,2048]{1,0:T(8,128)(2,1)S(1)} collective-permute-done((bf16[160,2048]{1,0:T(8,128)(2,1)S(1)}, bf16[160,2048]{1,0:T(8,128)(2,1)S(1)}, u32[]{:S(2)}, u32[]{:S(2)}) %collective-permute-start.90) | collective-permute-done | bytes 655392 | tf_op jit(solution)/shard_map/ppermute | solution.py:100
  755.0 12.3 %shard_map.246 = (f32[160,4,2048]{2,1,0:T(4,128)}, f32[128,2048]{1,0:T(8,128)S(1)}, f32[8,128]{1,0:T(8,128)S(1)}) custom-call(bf16[4,160,2048]{2,1,0:T(8,128)(2,1)S(1)} %copy-done.26, f32[4,160,128]{2,1,0:T(8,128)S(1)} %copy-done.48, f32[4,128]{1,0:T(4,128)S(1)} %copy-done.121, f32[4,160,2048]{2,1,0:T(8,128)S(1)} %bitcast.180, ...), custom_call_target="tpu_custom_call" | custom-call | tf_op jit(solution)/shard_map/pallas_call | solution.py:663
  775.6 11.2 %collective-permute-done.98 = bf16[32,2048]{1,0:T(8,128)(2,1)S(1)} collective-permute-done((bf16[32,2048]{1,0:T(8,128)(2,1)}, bf16[32,2048]{1,0:T(8,128)(2,1)S(1)}, u32[]{:S(2)}, u32[]{:S(2)}) %collective-permute-start.98) | collective-permute-done | bytes 131104 | tf_op jit(solution)/shard_map/ppermute | solution.py:100
  794.0 11.0 %collective-permute-done.101 = bf16[2,64,768]{2,1,0:T(8,128)(2,1)S(1)} collective-permute-done((bf16[2,64,768]{2,1,0:T(8,128)(2,1)S(1)}, bf16[2,64,768]{2,1,0:T(8,128)(2,1)S(1)}, u32[]{:S(2)}, u32[]{:S(2)}) %collective-permute-start.101) | collective-permute-done | bytes 196640 | tf_op jit(solution)/shard_map/ppermute | solution.py:100
  836.0 12.1 %shard_map.248 = (f32[256,8192]{1,0:T(8,128)}, f32[256,8192]{1,0:T(8,128)}) custom-call(s32[2]{0:T(128)} %copy-done.126, bf16[2,64,2048]{2,1,0:T(8,128)(2,1)} %copy-done.138, bf16[2,64,2048]{2,1,0:T(8,128)(2,1)} %get-tuple-element.375.refs_1_, bf16[2,64,2048]{2,1,0:T(8,128)(2,1)} %copy-done.143, bf16[2,64,2048]{2,1,0:T(8,128)(2,1)} %get-tuple-element.377.refs_3_, ...), custom_call_target="tpu_custom_call" | custom-call | tf_op jit(solution)/shard_map/pallas_call | solution.py:329
  (784 shorter events, 528.5 us)
Async XLA Ops:
  132.7 33.6 %collective-permute-start.26 = (bf16[4,64,2048]{2,1,0:T(8,128)(2,1)}, bf16[4,64,2048]{2,1,0:T(8,128)(2,1)}, u32[]{:S(2)}, u32[]{:S(2)}) collective-permute-start(bf16[4,64,2048]{2,1,0:T(8,128)(2,1)} %pad_maximum_fusion.1), channel_id=1, source_target_pairs={{0,8},{8,0},{16,24},{24,16},{1,9},{9,1},{17,25},{25,17},{2,10},{10... | collective-permute-start | bytes 3145736 | tf_op jit(solution)/shard_map/ppermute | solution.py:100
  133.4 32.9 %collective-permute-start.27 = (bf16[4,64,2048]{2,1,0:T(8,128)(2,1)}, bf16[4,64,2048]{2,1,0:T(8,128)(2,1)}, u32[]{:S(2)}, u32[]{:S(2)}) collective-permute-start(bf16[4,64,2048]{2,1,0:T(8,128)(2,1)} %pad_maximum_fusion.2), channel_id=1, source_target_pairs={{0,16},{8,24},{16,0},{24,8},{1,17},{9,25},{17,1},{25,9},{2,18},{10... | collective-permute-start | bytes 3145736 | tf_op jit(solution)/shard_map/ppermute | solution.py:100
  203.3 51.6 %collective-permute-start.39 = (bf16[4,64,2048]{2,1,0:T(8,128)(2,1)S(1)}, bf16[4,64,2048]{2,1,0:T(8,128)(2,1)S(1)}, u32[]{:S(2)}, u32[]{:S(2)}) collective-permute-start(bf16[4,64,2048]{2,1,0:T(8,128)(2,1)S(1)} %pad_maximum_fusion.3), channel_id=1, source_target_pairs={{0,8},{8,0},{16,24},{24,16},{1,9},{9,1},{17,25},{25,17},{2,10},{10... | collective-permute-start | bytes 3145736 | tf_op jit(solution)/shard_map/ppermute | solution.py:100
  204.4 50.5 %collective-permute-start.40 = (bf16[4,64,2048]{2,1,0:T(8,128)(2,1)S(1)}, bf16[4,64,2048]{2,1,0:T(8,128)(2,1)S(1)}, u32[]{:S(2)}, u32[]{:S(2)}) collective-permute-start(bf16[4,64,2048]{2,1,0:T(8,128)(2,1)S(1)} %pad_maximum_fusion.4), channel_id=1, source_target_pairs={{0,16},{8,24},{16,0},{24,8},{1,17},{9,25},{17,1},{25,9},{2,18},{10... | collective-permute-start | bytes 3145736 | tf_op jit(solution)/shard_map/ppermute | solution.py:100
  219.8 35.1 %collective-permute-start.38 = (bf16[160,2048]{1,0:T(8,128)(2,1)S(1)}, bf16[160,2048]{1,0:T(8,128)(2,1)S(1)}, u32[]{:S(2)}, u32[]{:S(2)}) collective-permute-start(bf16[160,2048]{1,0:T(8,128)(2,1)S(1)} %get-tuple-element.248.refs_0_), channel_id=1, source_target_pairs={{0,2},{1,3},{2,4},{3,5},{4,6},{5,7},{6,0},{7,1},{8,10},{9,11},{10,... | collective-permute-start | bytes 1966088 | tf_op jit(solution)/shard_map/ppermute | solution.py:100
  283.2 33.7 %collective-permute-start.44 = (bf16[640,2048]{1,0:T(8,128)(2,1)S(1)}, bf16[640,2048]{1,0:T(8,128)(2,1)S(1)}, u32[]{:S(2)}, u32[]{:S(2)}) collective-permute-start(bf16[640,2048]{1,0:T(8,128)(2,1)S(1)} %bitcast.169), channel_id=1, source_target_pairs={{0,1},{1,0},{2,3},{3,2},{4,5},{5,4},{6,7},{7,6},{8,9},{9,8},{10,11... | collective-permute-start | bytes 7864328 | tf_op jit(solution)/shard_map/ppermute | solution.py:100
  285.0 32.0 %collective-permute-start.45 = (bf16[4,64,2048]{2,1,0:T(8,128)(2,1)S(1)}, bf16[4,64,2048]{2,1,0:T(8,128)(2,1)S(1)}, u32[]{:S(2)}, u32[]{:S(2)}) collective-permute-start(bf16[4,64,2048]{2,1,0:T(8,128)(2,1)S(1)} %pad_maximum_fusion.5), channel_id=1, source_target_pairs={{0,8},{8,0},{16,24},{24,16},{1,9},{9,1},{17,25},{25,17},{2,10},{10... | collective-permute-start | bytes 3145736 | tf_op jit(solution)/shard_map/ppermute | solution.py:100
  285.9 31.0 %collective-permute-start.46 = (bf16[4,64,2048]{2,1,0:T(8,128)(2,1)S(1)}, bf16[4,64,2048]{2,1,0:T(8,128)(2,1)S(1)}, u32[]{:S(2)}, u32[]{:S(2)}) collective-permute-start(bf16[4,64,2048]{2,1,0:T(8,128)(2,1)S(1)} %pad_maximum_fusion.6), channel_id=1, source_target_pairs={{0,16},{8,24},{16,0},{24,8},{1,17},{9,25},{17,1},{25,9},{2,18},{10... | collective-permute-start | bytes 3145736 | tf_op jit(solution)/shard_map/ppermute | solution.py:100
  286.5 30.5 %collective-permute-start.48 = (bf16[160,2048]{1,0:T(8,128)(2,1)}, bf16[160,2048]{1,0:T(8,128)(2,1)S(1)}, u32[]{:S(2)}, u32[]{:S(2)}) collective-permute-start(bf16[160,2048]{1,0:T(8,128)(2,1)} %get-tuple-element.260.refs_0_), channel_id=1, source_target_pairs={{0,6},{1,7},{2,0},{3,1},{4,2},{5,3},{6,4},{7,5},{8,14},{9,15},{10,... | collective-permute-start | bytes 1966088 | tf_op jit(solution)/shard_map/ppermute | solution.py:100
  317.0 30.2 %collective-permute-start.49 = (bf16[160,2048]{1,0:T(8,128)(2,1)}, bf16[160,2048]{1,0:T(8,128)(2,1)S(1)}, u32[]{:S(2)}, u32[]{:S(2)}) collective-permute-start(bf16[160,2048]{1,0:T(8,128)(2,1)} %get-tuple-element.260.refs_0_), channel_id=1, source_target_pairs={{0,4},{1,5},{2,6},{3,7},{4,0},{5,1},{6,2},{7,3},{8,12},{9,13},{10,... | collective-permute-start | bytes 1966088 | tf_op jit(solution)/shard_map/ppermute | solution.py:100
  361.5 31.2 %collective-permute-start.53 = (bf16[160,2048]{1,0:T(8,128)(2,1)S(1)}, bf16[160,2048]{1,0:T(8,128)(2,1)S(1)}, u32[]{:S(2)}, u32[]{:S(2)}) collective-permute-start(bf16[160,2048]{1,0:T(8,128)(2,1)S(1)} %get-tuple-element.264), channel_id=1, source_target_pairs={{0,6},{1,7},{2,0},{3,1},{4,2},{5,3},{6,4},{7,5},{8,14},{9,15},{10,... | collective-permute-start | bytes 1966088 | tf_op jit(solution)/shard_map/ppermute | solution.py:100
  393.6 32.3 %collective-permute-start.55 = (bf16[640,2048]{1,0:T(8,128)(2,1)}, bf16[640,2048]{1,0:T(8,128)(2,1)S(1)}, u32[]{:S(2)}, u32[]{:S(2)}) collective-permute-start(bf16[640,2048]{1,0:T(8,128)(2,1)} %shard_map.231), channel_id=1, source_target_pairs={{0,1},{1,0},{2,3},{3,2},{4,5},{5,4},{6,7},{7,6},{8,9},{9,8},{10,11... | collective-permute-start | bytes 7864328 | tf_op jit(solution)/shard_map/ppermute | solution.py:100
  393.6 32.3 %collective-permute-start.54 = (bf16[160,2048]{1,0:T(8,128)(2,1)}, bf16[160,2048]{1,0:T(8,128)(2,1)S(1)}, u32[]{:S(2)}, u32[]{:S(2)}) collective-permute-start(bf16[160,2048]{1,0:T(8,128)(2,1)} %get-tuple-element.267), channel_id=1, source_target_pairs={{0,4},{1,5},{2,6},{3,7},{4,0},{5,1},{6,2},{7,3},{8,12},{9,13},{10,... | collective-permute-start | bytes 1966088 | tf_op jit(solution)/shard_map/ppermute | solution.py:100
  425.9 41.7 %collective-permute-start.58 = (bf16[4,64,2048]{2,1,0:T(8,128)(2,1)}, bf16[4,64,2048]{2,1,0:T(8,128)(2,1)}, u32[]{:S(2)}, u32[]{:S(2)}) collective-permute-start(bf16[4,64,2048]{2,1,0:T(8,128)(2,1)} %get-tuple-element.275), channel_id=1, source_target_pairs={{0,8},{8,0},{16,24},{24,16},{1,9},{9,1},{17,25},{25,17},{2,10},{10... | collective-permute-start | bytes 3145736 | tf_op jit(solution)/shard_map/ppermute | solution.py:100
  427.0 40.6 %collective-permute-start.59 = (bf16[4,64,2048]{2,1,0:T(8,128)(2,1)}, bf16[4,64,2048]{2,1,0:T(8,128)(2,1)}, u32[]{:S(2)}, u32[]{:S(2)}) collective-permute-start(bf16[4,64,2048]{2,1,0:T(8,128)(2,1)} %get-tuple-element.277), channel_id=1, source_target_pairs={{0,16},{8,24},{16,0},{24,8},{1,17},{9,25},{17,1},{25,9},{2,18},{10... | collective-permute-start | bytes 3145736 | tf_op jit(solution)/shard_map/ppermute | solution.py:100
  468.5 30.2 %collective-permute-start.62 = (bf16[4,64,2048]{2,1,0:T(8,128)(2,1)}, bf16[4,64,2048]{2,1,0:T(8,128)(2,1)S(1)}, u32[]{:S(2)}, u32[]{:S(2)}) collective-permute-start(bf16[4,64,2048]{2,1,0:T(8,128)(2,1)} %get-tuple-element.286), channel_id=1, source_target_pairs={{0,16},{8,24},{16,0},{24,8},{1,17},{9,25},{17,1},{25,9},{2,18},{10... | collective-permute-start | bytes 3145736 | tf_op jit(solution)/shard_map/ppermute | solution.py:100
  498.7 48.6 %collective-permute-start.65 = (bf16[4,64,2048]{2,1,0:T(8,128)(2,1)}, bf16[4,64,2048]{2,1,0:T(8,128)(2,1)}, u32[]{:S(2)}, u32[]{:S(2)}) collective-permute-start(bf16[4,64,2048]{2,1,0:T(8,128)(2,1)} %add.244), channel_id=1, source_target_pairs={{0,16},{8,24},{16,0},{24,8},{1,17},{9,25},{17,1},{25,9},{2,18},{10... | collective-permute-start | bytes 3145736 | tf_op jit(solution)/shard_map/ppermute | solution.py:100
  501.6 45.7 %collective-permute-start.66 = (bf16[4,64,2048]{2,1,0:T(8,128)(2,1)}, bf16[4,64,2048]{2,1,0:T(8,128)(2,1)}, u32[]{:S(2)}, u32[]{:S(2)}) collective-permute-start(bf16[4,64,2048]{2,1,0:T(8,128)(2,1)} %add.245), channel_id=1, source_target_pairs={{0,8},{8,0},{16,24},{24,16},{1,9},{9,1},{17,25},{25,17},{2,10},{10... | collective-permute-start | bytes 3145736 | tf_op jit(solution)/shard_map/ppermute | solution.py:100
  547.4 30.6 %collective-permute-start.67 = (bf16[160,2048]{1,0:T(8,128)(2,1)S(1)}, bf16[160,2048]{1,0:T(8,128)(2,1)S(1)}, u32[]{:S(2)}, u32[]{:S(2)}) collective-permute-start(bf16[160,2048]{1,0:T(8,128)(2,1)S(1)} %get-tuple-element.296.refs_0_), channel_id=1, source_target_pairs={{0,4},{1,5},{2,6},{3,7},{4,0},{5,1},{6,2},{7,3},{8,12},{9,13},{10,... | collective-permute-start | bytes 1966088 | tf_op jit(solution)/shard_map/ppermute | solution.py:100
  608.6 32.2 %collective-permute-start.78 = (bf16[256,2048]{1,0:T(8,128)(2,1)}, bf16[256,2048]{1,0:T(8,128)(2,1)}, u32[]{:S(2)}, u32[]{:S(2)}) collective-permute-start(bf16[256,2048]{1,0:T(8,128)(2,1)} %pad_maximum_fusion.10), channel_id=1, source_target_pairs={{0,8},{8,0},{16,24},{24,16},{1,9},{9,1},{17,25},{25,17},{2,10},{10... | collective-permute-start | bytes 3145736 | tf_op jit(solution)/shard_map/ppermute | solution.py:100
  610.6 30.3 %collective-permute-start.79 = (bf16[256,2048]{1,0:T(8,128)(2,1)}, bf16[256,2048]{1,0:T(8,128)(2,1)}, u32[]{:S(2)}, u32[]{:S(2)}) collective-permute-start(bf16[256,2048]{1,0:T(8,128)(2,1)} %pad_maximum_fusion.11), channel_id=1, source_target_pairs={{0,16},{8,24},{16,0},{24,8},{1,17},{9,25},{17,1},{25,9},{2,18},{10... | collective-permute-start | bytes 3145736 | tf_op jit(solution)/shard_map/ppermute | solution.py:100
  687.4 35.2 %collective-permute-start.89 = (bf16[8,64,768]{2,1,0:T(8,128)(2,1)S(1)}, bf16[8,64,768]{2,1,0:T(8,128)(2,1)S(1)}, u32[]{:S(2)}, u32[]{:S(2)}) collective-permute-start(bf16[8,64,768]{2,1,0:T(8,128)(2,1)S(1)} %pad_maximum_fusion.21), channel_id=1, source_target_pairs={{0,16},{8,24},{16,0},{24,8},{1,17},{9,25},{17,1},{25,9},{2,18},{10... | collective-permute-start | bytes 2359304 | tf_op jit(solution)/shard_map/ppermute | solution.py:100
  728.1 41.2 %collective-permute-start.93 = (bf16[4,64,2048]{2,1,0:T(8,128)(2,1)}, bf16[4,64,2048]{2,1,0:T(8,128)(2,1)S(1)}, u32[]{:S(2)}, u32[]{:S(2)}) collective-permute-start(bf16[4,64,2048]{2,1,0:T(8,128)(2,1)} %pad_maximum_fusion.12), channel_id=1, source_target_pairs={{0,8},{8,0},{16,24},{24,16},{1,9},{9,1},{17,25},{25,17},{2,10},{10... | collective-permute-start | bytes 3145736 | tf_op jit(solution)/shard_map/ppermute | solution.py:100
  729.2 40.0 %collective-permute-start.94 = (bf16[4,64,2048]{2,1,0:T(8,128)(2,1)}, bf16[4,64,2048]{2,1,0:T(8,128)(2,1)S(1)}, u32[]{:S(2)}, u32[]{:S(2)}) collective-permute-start(bf16[4,64,2048]{2,1,0:T(8,128)(2,1)} %pad_maximum_fusion.13), channel_id=1, source_target_pairs={{0,16},{8,24},{16,0},{24,8},{1,17},{9,25},{17,1},{25,9},{2,18},{10... | collective-permute-start | bytes 3145736 | tf_op jit(solution)/shard_map/ppermute | solution.py:100
  (274 other events, 4631.9 us)

commit v2 on v1

--- a/solution.py
+++ b/solution.py
@@ -121,7 +121,7 @@
     rows, width = x.shape
     (mine,) = token_call(
         functools.partial(assemble_kernel, line), rows, [x, *rights, *lefts],
-        [jax.ShapeDtypeStruct((line, rows, width), x.dtype)],
+        [jax.ShapeDtypeStruct((line, rows, width), x.dtype)], block=rows // 2 if rows % 32 == 0 else rows,
     )
     return mine.reshape(line * rows, width)
 
@@ -135,11 +135,6 @@
 def line_shift(k):
     line = lax.axis_size("shard") // 2
     return sender("shard", [(2 * p + c, 2 * ((p + k) % line) + c) for p in range(line) for c in range(2)])
-
-
-def stack_kernel(*refs):
-    for k, ref in enumerate(refs[:-1]):
-        refs[-1][k] = ref[...]
 
 
 def shifts(line, steps):
@@ -151,12 +146,7 @@
     came = {}
     for step in shifts(line, steps):
         came |= dict(zip(step, (yield [(line_shift(k), x) for k in step])))
-    rows, width = x.shape
-    (mine,) = token_call(
-        stack_kernel, rows, [x] + [came[line - q] for q in range(1, line)],
-        [jax.ShapeDtypeStruct((line, rows, width), x.dtype)],
-    )
-    return mine.reshape(line * rows, width)
+    return jnp.concatenate([x] + [came[line - q] for q in range(1, line)], axis=0)
 
 
 def direct_scatter(rows, steps=1):
@@ -233,17 +223,6 @@
     came = yield [(rep_sender(bits[u]), units[u][m]) for u, m in flat]
     came = dict(zip(flat, came))
     return [[came[u, m] for m in key] for u, key in enumerate(keys)]
-
-
-def shard_exchange(x, counts=()):
-    shards = lax.axis_size("shard")
-    me = lax.axis_index("shard")
-    take = lambda k: lax.dynamic_index_in_dim(x, me ^ k, 0, keepdims=False)
-    out, counts = [take(0)], list(counts)
-    while len(out) < shards:
-        step = range(len(out), min(shards, len(out) + (counts.pop(0) if counts else shards)))
-        out += yield [(sender("shard", [(i, i ^ k) for i in range(shards)]), take(k)) for k in step]
-    return out
 
 
 def chip_exchange(x, counts=(), out=None):
@@ -445,9 +424,10 @@
     for v in came:
         total = total + v
     came = yield [(sender("rep", [(i, i ^ k) for i in range(reps)]), total) for k in range(1, reps)]
-    stacked = jnp.stack([total, *came])
-    me = lax.axis_index("rep")
-    return sum(lax.dynamic_index_in_dim(stacked, me ^ k, 0, keepdims=False) for k in range(reps))
+    terms = [total, *came]
+    while len(terms) > 1:
+        terms = [a + b for a, b in zip(terms[::2], terms[1::2])]
+    return terms[0]
 
 
 def lane(shape):
@@ -649,8 +629,8 @@
         grad_ref[:, i, :] = grads[i]
 
 
-def token_call(kernel, tokens, operands, outputs, flops=0, mib=40):
-    block = 32 if tokens % 32 == 0 else tokens
+def token_call(kernel, tokens, operands, outputs, block=None, mib=40):
+    block = block or (32 if tokens % 32 == 0 else tokens)
 
     def spec(shape):
         if tokens not in shape[:-1]:
@@ -1103,14 +1083,15 @@
     start = sequence_places(place, lengths[0])
     cosine, sine = rope_tables(place - start, head_width)
     w = tie(cotangent).transpose(1, 0, 2)
-    run(gather_in)
+    gate_up_blocks = []
+    recut_gate_up = Task(chip_exchange(gate_up_piece, (line // 4, line // 4), gate_up_blocks))
+    run(gather_in, recut_gate_up)
     hold(cosine, sine, w)
     finish(gather_in, gather_qkv)
     gathered = gather_in.value.reshape(line, tokens + part, width)
     mine_in = gathered[:, :tokens].reshape(line * tokens, width)
     swap = Task(other_core(mine_in))
     gather_output = Task(rep_gather(cut_units(gathered[:, tokens:], 2), True))
-    recut_gate_up = Task(shard_exchange(gate_up_piece, (shards // 4, 3 * shards // 8, shards // 8)))
     run(swap, recut_gate_up, gather_output)
     attention_weight = recut_join(gather_qkv.value)
     hold(attention_weight)
@@ -1121,14 +1102,13 @@
     attended, rot_q, rot_k, logs = attention(qkv, cosine, sine, place, start, heads)
     finish(gather_output)
     hold(attended)
-    gate_up_low = [lax.dynamic_index_in_dim(gate_up_piece, me, 0, keepdims=False)]
-    gate_up_low += recut_gate_up.arrived[: shards // 2 - 1]
-    gather_low = Task(rep_gather(stack_units(gate_up_low, 2), True))
+    gather_low = Task(rep_gather(stack_units(gate_up_blocks[: shards // 2], 2), True))
     tokens_out = Task(to_tokens(attended.reshape(2, line, tokens, local)))
     run(tokens_out, recut_gate_up, gather_low)
+    finish(recut_gate_up)
     output_mine = rows_in_order(gather_output.value)
     swap = Task(other_core(output_mine))
-    run(tokens_out, swap, recut_gate_up)
+    run(tokens_out, swap)
     branch = dot(tokens_out.value[0], output_mine) + dot(tokens_out.value[1], swap.value)
 
     middle, entering_next, down_in, packed_next = token_call(
@@ -1140,7 +1120,7 @@
         ],
     )
     finish(recut_gate_up)
-    gather_high = Task(rep_gather(stack_units(recut_gate_up.value[shards // 2 :], 2), True))
+    gather_high = Task(rep_gather(stack_units(gate_up_blocks[shards // 2 :], 2), True))
     gather_ffn, gather_down = Task(direct_gather(entering_next, 2)), Task(direct_gather(down_in, 2))
     run(gather_ffn, gather_low)
     finish(gather_low)
@@ -1171,10 +1151,11 @@
     hold(theirs)
     swap = Task(other_core(theirs))
     run(scatter_z, swap)
-    gate_up_blocks = columns_product([mine_ffn, other_ffn], [(grad_both, 0), (grad_both, 1)], 2)
-    hold(*gate_up_blocks[0])
+    f_mine = product((grad_both, 0), gate_up, NT, add=swap.value)
+    ready = after(grad_both, f_mine)
+    gate_up_blocks = columns_product([mine_ffn, other_ffn], [(ready, 0), (ready, 1)], 2)
     finish(scatter_z)
-    scatter_f = Task(direct_scatter(product((grad_both, 0), gate_up, NT, add=swap.value), 2))
+    scatter_f = Task(direct_scatter(f_mine, 2))
     scatter_gate_up = Task(rep_scatter(gate_up_blocks))
     run(scatter_f, (scatter_gate_up, 1))
     down_blocks = rows_product([(active, 0), (active, 1)], [mine_down, other_down], 2)
@@ -1208,46 +1189,46 @@
     finish(gather_branch)
     mine_branch = gather_branch.value
     swap = Task(other_core(mine_branch))
-    run(swap, scatter_down, recut_grad)
+    run(swap, recut_grad)
+    grad_mine = product(mine_branch, output_weight, NT, into=0)
+    other_branch = swap.value
+    run(recut_grad, scatter_down)
     finish(scatter_down)
     gather_down_rows = Task(rep_gather(scatter_down.value, True))
-    grad_mine = product(mine_branch, output_weight, NT, into=0)
-    other_branch = swap.value
-    run(recut_grad, gather_down_rows)
+    output_blocks = rows_product([(attended, 0), (attended, 1)], [mine_branch, other_branch], 2)
+    hold(*output_blocks[0])
     grad_attended = product(other_branch, output_weight, NT, into=1, filled=(grad_mine,))
     grad_qkv = attention_back(qkv, rot_q, rot_k, grad_attended, logs, cosine, sine, place, start, heads)
     theirs = product((grad_qkv, 1), attention_weight, NT)
+    gather_low = Task(rep_gather(stack_units(low[: shards // 2], 2), True))
+    run(recut_grad, gather_down_rows, gather_low)
+    hold(theirs)
+    scatter_output = Task(rep_scatter(output_blocks, True))
     run(recut_grad, gather_down_rows)
-    gather_low = Task(rep_gather(stack_units(low[: shards // 2], 2), True))
-    hold(theirs)
-    run(recut_grad, gather_low)
+    finish(recut_grad, gather_down_rows)
     qkv_blocks = columns_product([mine_in, other_in], [(grad_qkv, 0), (grad_qkv, 1)], 2)
-    output_blocks = rows_product([(attended, 0), (attended, 1)], [mine_branch, other_branch], 2)
-    hold(*qkv_blocks[0], *output_blocks[0])
-    finish(recut_grad, gather_down_rows)
+    hold(*qkv_blocks[0])
     gather_high = Task(rep_gather(stack_units(low[shards // 2 :], 2), True))
     swap = Task(other_core(theirs))
-    scatter_output = Task(rep_scatter(output_blocks, True))
     run(swap, scatter_output)
-    down_rows = rows_join(gather_down_rows.value)
-    hold(down_rows)
     scatter_a = Task(direct_scatter(product((grad_qkv, 0), attention_weight, NT, add=swap.value), 2))
     scatter_qkv = Task(rep_scatter(qkv_blocks, True))
     run(scatter_a, scatter_qkv)
     run(scatter_a, scatter_qkv, gather_low)
     finish(scatter_qkv, scatter_a, gather_low)
     recut_qkv_grad = Task(chip_exchange(jnp.concatenate(scatter_qkv.value, axis=0)))
+    run(recut_qkv_grad, gather_high, scatter_output)
+    finish(scatter_output)
+    gather_output = Task(rep_gather(scatter_output.value, True))
     grad_streams, mixing_sum, static_sum = token_call(
         first_back_kernel, tokens,
-        [x, packed, static[0], grad_middle, grad_beta, mixing_rows[0], mixing_mean[0], *scatter_a.value],
+        [x, packed, static[0], tie(grad_middle), grad_beta, mixing_rows[0], mixing_mean[0], *scatter_a.value],
         [shape((tokens, count, width), F32), shape((LANES, width), F32), shape((8, LANES), F32)],
     )
-    run(recut_qkv_grad, gather_high, scatter_output)
+    run(recut_qkv_grad, gather_high)
     hold(grad_streams)
-    run(recut_qkv_grad, gather_high)
-    finish(recut_qkv_grad, gather_high, scatter_output)
+    finish(recut_qkv_grad, gather_high)
     gather_qkv_grad = Task(rep_gather(stack_units(recut_qkv_grad.value, 2), True))
-    gather_output = Task(rep_gather(scatter_output.value, True))
     mixing_sums = jnp.stack([mixing_sum, mixing_sum_next])
     mixing_sums = (mixing_sums[:, :6] + mixing_sums[:, 8:14]).reshape(12, shards, -1)
     small = jnp.concatenate(
@@ -1260,10 +1241,11 @@
     sum_last = Task(sum_small(small))
     run(sum_last, gather_qkv_grad, gather_output)
     gate_rows, up_rows = columns_join([[tie(v) for v in u] for u in gather_low.value + gather_high.value], 2)
+    down_rows = rows_join([[tie(v) for v in u] for u in gather_down_rows.value])
     run(sum_last, gather_qkv_grad)
-    hold(gate_rows)
+    hold(gate_rows, down_rows)
     run(sum_last, gather_output)
-    finish(gather_qkv_grad, gather_output, sum_last)
+    finish(gather_qkv_grad, sum_last, gather_output)
     output_rows = rows_join(gather_output.value)
     small = sum_last.value
     rows = width // shards

time: 873 us -> 844 us (0.967)
  waiting for transfers between devices: 355 us -> 341 us
    ppermute x120 -> x117, waiting for transfers between devices: 355 us -> 341 us  [sender(): return lambda x: lax.ppermute(x, axis, pairs)]
    pallas_call x9 -> x6, Pallas kernels: 60.4 us -> 53.9 us  [token_call(): pl.pallas_call(kernel, grid=(tokens // block,), in_specs=[spec(o.shape) f...]
    ppermute x120 -> x117, starting transfers between devices: 153 us -> 148 us  [sender(): return lambda x: lax.ppermute(x, axis, pairs)]
    unnamed x363 -> x396, local copies, waits for them, and re-layouts: 31.9 us -> 36.1 us
  transfers between devices with their start and end apart: 120 -> 117, of which waited for: 58 -> 55; matrix products, arithmetic and copies ran while one was open for 10% -> 10% of each run, Pallas kernels for 27% -> 27%
where the time goes in v2:
time: 844 us; the launch traced here: 834 us
  waiting for transfers between devices  341 us (40%)
  Pallas kernels  231 us (27%)
  starting transfers between devices  148 us (18%)
  local copies, waits for them, and re-layouts  64.9 us (8%)
  other arithmetic  44.2 us (5%)
    ppermute x117, waiting for transfers between devices, sender(): return lambda x: lax.ppermute(x, axis, pairs)  341 us
    ppermute x117, starting transfers between devices, sender(): return lambda x: lax.ppermute(x, axis, pairs)  148 us
    pallas_call x6, Pallas kernels, token_call(): pl.pallas_call(kernel, grid=(tokens // block,), in_specs=[spec(o.shape) f...  53.9 us
    pallas_call x10, Pallas kernels, product(): pl.pallas_call(functools.partial(product_kernel, dims, add is not None),...  41.1 us
    unnamed x396, local copies, waits for them, and re-layouts  36.1 us
    pallas_call x2, Pallas kernels, columns_product(): pl.pallas_call(functools.partial(columns_product_kernel, units, reps), gr...  28.5 us
    pallas_call x6, Pallas kernels, join(): pl.pallas_call(functools.partial(columns_kernel, len(units), reps, parts)...  23.2 us
    concatenate x24, other arithmetic, exchange_blocks(): jnp.concatenate([unit[m] for m in key])  18.6 us
  transfers between devices with their start and end apart: 117, of which 55 were waited for; matrix products, arithmetic and copies ran while one was open for 10% of the time, Pallas kernels for 27%

profile of v2, /device:TPU:0, one launch (start us, length us, event | category | flops | bytes accessed | tf_op | source)
XLA Modules:
  0.0 834.5 jit_solution(4687283522864802269)
XLA Ops:
  19.0 11.5 %shard_map.213 = (bf16[160,2048]{1,0:T(8,128)(2,1)S(1)}, f32[4,160,128]{2,1,0:T(8,128)S(1)}, bf16[4,160,2048]{2,1,0:T(8,128)(2,1)S(1)}) custom-call(bf16[160,4,2048]{2,1,0:T(4,128)(2,1)S(1)} %copy-done.49, bf16[128,2048]{1,0:T(8,128)(2,1)S(1)} %get-tuple-element.499.weight_ref.weight_rows_ref, f32[4,128]{1,0:T(4,128)S(1)} %get-tuple-element.574.static_ref.static_first_ref), custom_call_target="tpu_custom_call" | custom-call | tf_op jit(solution)/shard_map/pallas_call | solution.py:643
  68.7 9.8 %collective-permute-done.14 = bf16[8,64,768]{2,1,0:T(8,128)(2,1)S(1)} collective-permute-done((bf16[8,64,768]{2,1,0:T(8,128)(2,1)S(1)}, bf16[8,64,768]{2,1,0:T(8,128)(2,1)S(1)}, u32[]{:S(2)}, u32[]{:S(2)}) %collective-permute-start.14) | collective-permute-done | bytes 786464 | tf_op jit(solution)/shard_map/ppermute | solution.py:100
  91.3 12.8 %collective-permute-done.17.refs_5_ = bf16[224,2048]{1,0:T(8,128)(2,1)} collective-permute-done((bf16[224,2048]{1,0:T(8,128)(2,1)}, bf16[224,2048]{1,0:T(8,128)(2,1)}, u32[]{:S(2)}, u32[]{:S(2)}) %collective-permute-start.17) | collective-permute-done | bytes 917536 | tf_op jit(solution)/shard_map/ppermute | solution.py:100
  137.9 14.0 %shard_map.218 = (bf16[1280,256]{1,0:T(8,128)(2,1)S(1)}, bf16[1280,256]{1,0:T(8,128)(2,1)S(1)}, bf16[1280,256]{1,0:T(8,128)(2,1)S(1)}, f32[2,1280]{1,0:T(2,128)S(1)}) custom-call(bf16[1280,768]{1,0:T(8,128)(2,1)} %copy-done.4, bf16[1280,768]{1,0:T(8,128)(2,1)} %copy-done.4, bf16[1280,768]{1,0:T(8,128)(2,1)} %copy-done.4, ...), custom_call_target="tpu_custom_call" | custom-call | tf_op jit(solution)/shard_map/pallas_call | solution.py:941
  170.5 12.7 %collective-permute-start.32 = (bf16[2,160,256]{2,1,0:T(8,128)(2,1)S(1)}, bf16[2,160,256]{2,1,0:T(8,128)(2,1)S(1)}, u32[]{:S(2)}, u32[]{:S(2)}) collective-permute-start(bf16[2,160,256]{2,1,0:T(8,128)(2,1)S(1)} %get-tuple-element.244), channel_id=1, source_target_pairs={{0,2},{1,3},{2,4},{3,5},{4,6},{5,7},{6,0},{7,1},{8,10},{9,11},{10,... | collective-permute-start | bytes 491528 | tf_op jit(solution)/shard_map/ppermute | solution.py:100
  215.4 15.0 %collective-permute-done.34 = bf16[160,2048]{1,0:T(8,128)(2,1)S(1)} collective-permute-done((bf16[160,2048]{1,0:T(8,128)(2,1)S(1)}, bf16[160,2048]{1,0:T(8,128)(2,1)S(1)}, u32[]{:S(2)}, u32[]{:S(2)}) %collective-permute-start.34) | collective-permute-done | bytes 655392 | tf_op jit(solution)/shard_map/ppermute | solution.py:100
  230.5 13.1 %collective-permute-done.35 = bf16[160,2048]{1,0:T(8,128)(2,1)S(1)} collective-permute-done((bf16[160,2048]{1,0:T(8,128)(2,1)S(1)}, bf16[160,2048]{1,0:T(8,128)(2,1)S(1)}, u32[]{:S(2)}, u32[]{:S(2)}) %collective-permute-start.35) | collective-permute-done | bytes 655392 | tf_op jit(solution)/shard_map/ppermute | solution.py:100
  245.5 28.4 %collective-permute-done.38 = bf16[160,2048]{1,0:T(8,128)(2,1)S(1)} collective-permute-done((bf16[160,2048]{1,0:T(8,128)(2,1)S(1)}, bf16[160,2048]{1,0:T(8,128)(2,1)S(1)}, u32[]{:S(2)}, u32[]{:S(2)}) %collective-permute-start.38) | collective-permute-done | bytes 655392 | tf_op jit(solution)/shard_map/ppermute | solution.py:100
  282.9 14.6 %collective-permute-done.44 = bf16[160,2048]{1,0:T(8,128)(2,1)S(1)} collective-permute-done((bf16[160,2048]{1,0:T(8,128)(2,1)}, bf16[160,2048]{1,0:T(8,128)(2,1)S(1)}, u32[]{:S(2)}, u32[]{:S(2)}) %collective-permute-start.44) | collective-permute-done | bytes 655392 | tf_op jit(solution)/shard_map/ppermute | solution.py:100
  297.5 11.2 %collective-permute-done.45 = bf16[160,2048]{1,0:T(8,128)(2,1)S(1)} collective-permute-done((bf16[160,2048]{1,0:T(8,128)(2,1)}, bf16[160,2048]{1,0:T(8,128)(2,1)S(1)}, u32[]{:S(2)}, u32[]{:S(2)}) %collective-permute-start.45) | collective-permute-done | bytes 655392 | tf_op jit(solution)/shard_map/ppermute | solution.py:100
  398.0 19.5 %shard_map.231 = (bf16[4,64,2048]{2,1,0:T(8,128)(2,1)S(1)}, bf16[4,64,2048]{2,1,0:T(8,128)(2,1)}, bf16[4,64,2048]{2,1,0:T(8,128)(2,1)S(1)}, bf16[4,64,2048]{2,1,...) custom-call(s32[1]{0:T(128)} %bitcast.23.me_ref, ...), custom_call_target="tpu_custom_call" | custom-call | tf_op jit(solution)/shard_map/pallas_call | solution.py:723
  425.5 10.3 %shard_map.232 = (bf16[128,2048]{1,0:T(8,128)(2,1)S(1)}, bf16[128,2048]{1,0:T(8,128)(2,1)S(1)}, bf16[128,2048]{1,0:T(8,128)(2,1)S(1)}, bf16[128,2048]{1,0:T(8,12...) custom-call(s32[1]{0:T(128)} %bitcast.23.me_ref, ...), custom_call_target="tpu_custom_call" | custom-call | tf_op jit(solution)/shard_map/pallas_call | solution.py:759
  441.4 11.8 %collective-permute-done.54.refs_6_ = bf16[160,2048]{1,0:T(8,128)(2,1)S(1)} collective-permute-done((bf16[160,2048]{1,0:T(8,128)(2,1)S(1)}, bf16[160,2048]{1,0:T(8,128)(2,1)S(1)}, u32[]{:S(2)}, u32[]{:S(2)}) %collective-permute-start.54) | collective-permute-done | bytes 655392 | tf_op jit(solution)/shard_map/ppermute | solution.py:100
  456.3 21.2 %collective-permute-done.58 = bf16[4,64,2048]{2,1,0:T(8,128)(2,1)S(1)} collective-permute-done((bf16[4,64,2048]{2,1,0:T(8,128)(2,1)S(1)}, bf16[4,64,2048]{2,1,0:T(8,128)(2,1)S(1)}, u32[]{:S(2)}, u32[]{:S(2)}) %collective-permute-start.58) | collective-permute-done | bytes 1048608 | tf_op jit(solution)/shard_map/ppermute | solution.py:100
  489.8 13.9 %shard_map.233 = (f32[4,160,2048]{2,1,0:T(8,128)}, bf16[160,2048]{1,0:T(8,128)(2,1)S(1)}, f32[160,128]{1,0:T(8,128)S(1)}, f32[128,2048]{1,0:T(8,128)S(1)}, f32[8,128]{1,0:T(8,128)S(1)}) custom-call(f32[4,160,2048]{2,1,0:T(8,128)} %copy-done.13, f32[4,160,128]{2,1,0:T(8,128)S(1)} %copy-done.77, f32[4,128]{1,0:T(4,128)S(1)} %copy-done.134, ...), custom_call_target="tpu_custom_call" | custom-call | tf_op jit(solution)/shard_map/pallas_call | solution.py:643
  508.2 14.9 %collective-permute-done.60 = bf16[160,2048]{1,0:T(8,128)(2,1)S(1)} collective-permute-done((bf16[160,2048]{1,0:T(8,128)(2,1)S(1)}, bf16[160,2048]{1,0:T(8,128)(2,1)S(1)}, u32[]{:S(2)}, u32[]{:S(2)}) %collective-permute-start.60) | collective-permute-done | bytes 655392 | tf_op jit(solution)/shard_map/ppermute | solution.py:100
  523.1 9.8 %collective-permute-done.61 = bf16[160,2048]{1,0:T(8,128)(2,1)S(1)} collective-permute-done((bf16[160,2048]{1,0:T(8,128)(2,1)S(1)}, bf16[160,2048]{1,0:T(8,128)(2,1)S(1)}, u32[]{:S(2)}, u32[]{:S(2)}) %collective-permute-start.61) | collective-permute-done | bytes 655392 | tf_op jit(solution)/shard_map/ppermute | solution.py:100
  543.2 20.2 %collective-permute-done.64 = bf16[160,2048]{1,0:T(8,128)(2,1)S(1)} collective-permute-done((bf16[160,2048]{1,0:T(8,128)(2,1)S(1)}, bf16[160,2048]{1,0:T(8,128)(2,1)S(1)}, u32[]{:S(2)}, u32[]{:S(2)}) %collective-permute-start.64) | collective-permute-done | bytes 655392 | tf_op jit(solution)/shard_map/ppermute | solution.py:100
  596.3 17.3 %shard_map.237.y0.y1.a_ref = bf16[1280,768]{1,0:T(8,128)(2,1)} custom-call(bf16[1280,256]{1,0:T(8,128)(2,1)} %copy-done.84, bf16[1280,256]{1,0:T(8,128)(2,1)} %copy-done.85, bf16[1280,768]{1,0:T(8,128)(2,1)} %copy-done.4, bf16[1280,256]{1,0:T(8,128)(2,1)} %copy-done.35, f32[2,1280]{1,0:T(2,128)} %copy-done.137, f32[1280,128]{1,0:T(8,128)} %copy-done.14, ...), custom_call_target="tpu_custom_call" | custom-call | tf_op jit(solution)/shard_map/pallas_call | solution.py:982
  686.7 11.7 %collective-permute-done.85.refs_2_ = bf16[160,2048]{1,0:T(8,128)(2,1)S(1)} collective-permute-done((bf16[160,2048]{1,0:T(8,128)(2,1)S(1)}, bf16[160,2048]{1,0:T(8,128)(2,1)S(1)}, u32[]{:S(2)}, u32[]{:S(2)}) %collective-permute-start.85) | collective-permute-done | bytes 655392 | tf_op jit(solution)/shard_map/ppermute | solution.py:100
  712.8 20.2 %collective-permute-done.89.refs_3_ = bf16[160,2048]{1,0:T(8,128)(2,1)S(1)} collective-permute-done((bf16[160,2048]{1,0:T(8,128)(2,1)S(1)}, bf16[160,2048]{1,0:T(8,128)(2,1)S(1)}, u32[]{:S(2)}, u32[]{:S(2)}) %collective-permute-start.89) | collective-permute-done | bytes 655392 | tf_op jit(solution)/shard_map/ppermute | solution.py:100
  739.3 11.1 %collective-permute-done.95 = bf16[32,2048]{1,0:T(8,128)(2,1)S(1)} collective-permute-done((bf16[32,2048]{1,0:T(8,128)(2,1)S(1)}, bf16[32,2048]{1,0:T(8,128)(2,1)S(1)}, u32[]{:S(2)}, u32[]{:S(2)}) %collective-permute-start.95) | collective-permute-done | bytes 131104 | tf_op jit(solution)/shard_map/ppermute | solution.py:100
  763.5 12.3 %shard_map.242 = (f32[160,4,2048]{2,1,0:T(4,128)}, f32[128,2048]{1,0:T(8,128)S(1)}, f32[8,128]{1,0:T(8,128)S(1)}) custom-call(bf16[4,160,2048]{2,1,0:T(8,128)(2,1)S(1)} %copy-done.25, f32[4,160,128]{2,1,0:T(8,128)S(1)} %get-tuple-element.212.packed_ref.packed_first_ref, f32[4,128]{1,0:T(4,128)S(1)} %copy-done.130, f32[4,160,2048]{2,1,0:T(8,128)S(1)} %bitcast.139, ...), custom_call_target="tpu_custom_call" | custom-call | tf_op jit(solution)/shard_map/pallas_call | solution.py:643
  808.3 12.0 %shard_map.244 = (f32[256,8192]{1,0:T(8,128)}, f32[256,8192]{1,0:T(8,128)}) custom-call(s32[2]{0:T(128)} %copy-done.135, bf16[2,64,2048]{2,1,0:T(8,128)(2,1)} %pad_maximum_fusion.34.refs_0_, bf16[2,64,2048]{2,1,0:T(8,128)(2,1)} %get-tuple-element.381.refs_1_, bf16[2,64,2048]{2,1,0:T(8,128)(2,1)} %collective-permute-done.75.refs_2_, ...), custom_call_target="tpu_custom_call" | custom-call | tf_op jit(solution)/shard_map/pallas_call | solution.py:308
  (811 shorter events, 481.2 us)
Async XLA Ops:
  194.4 49.2 %collective-permute-start.36 = (bf16[4,64,2048]{2,1,0:T(8,128)(2,1)}, bf16[4,64,2048]{2,1,0:T(8,128)(2,1)S(1)}, u32[]{:S(2)}, u32[]{:S(2)}) collective-permute-start(bf16[4,64,2048]{2,1,0:T(8,128)(2,1)} %pad_maximum_fusion.4), channel_id=1, source_target_pairs={{0,8},{8,0},{16,24},{24,16},{1,9},{9,1},{17,25},{25,17},{2,10},{10... | collective-permute-start | bytes 3145736 | tf_op jit(solution)/shard_map/ppermute | solution.py:100
  195.5 48.0 %collective-permute-start.37 = (bf16[4,64,2048]{2,1,0:T(8,128)(2,1)S(1)}, bf16[4,64,2048]{2,1,0:T(8,128)(2,1)S(1)}, u32[]{:S(2)}, u32[]{:S(2)}) collective-permute-start(bf16[4,64,2048]{2,1,0:T(8,128)(2,1)S(1)} %pad_maximum_fusion.5), channel_id=1, source_target_pairs={{0,16},{8,24},{16,0},{24,8},{1,17},{9,25},{17,1},{25,9},{2,18},{10... | collective-permute-start | bytes 3145736 | tf_op jit(solution)/shard_map/ppermute | solution.py:100
  243.6 30.3 %collective-permute-start.38 = (bf16[160,2048]{1,0:T(8,128)(2,1)S(1)}, bf16[160,2048]{1,0:T(8,128)(2,1)S(1)}, u32[]{:S(2)}, u32[]{:S(2)}) collective-permute-start(bf16[160,2048]{1,0:T(8,128)(2,1)S(1)} %get-tuple-element.252), channel_id=1, source_target_pairs={{0,4},{1,5},{2,6},{3,7},{4,0},{5,1},{6,2},{7,3},{8,12},{9,13},{10,... | collective-permute-start | bytes 1966088 | tf_op jit(solution)/shard_map/ppermute | solution.py:100
  243.9 30.1 %collective-permute-start.39 = (bf16[2,64,2048]{2,1,0:T(8,128)(2,1)S(1)}, bf16[2,64,2048]{2,1,0:T(8,128)(2,1)S(1)}, u32[]{:S(2)}, u32[]{:S(2)}) collective-permute-start(bf16[2,64,2048]{2,1,0:T(8,128)(2,1)S(1)} %copy-done.65), channel_id=1, source_target_pairs={{0,16},{8,24},{16,0},{24,8},{1,17},{9,25},{17,1},{25,9},{2,18},{10... | collective-permute-start | bytes 1572872 | tf_op jit(solution)/shard_map/ppermute | solution.py:100
  274.0 34.7 %collective-permute-start.41 = (bf16[640,2048]{1,0:T(8,128)(2,1)S(1)}, bf16[640,2048]{1,0:T(8,128)(2,1)S(1)}, u32[]{:S(2)}, u32[]{:S(2)}) collective-permute-start(bf16[640,2048]{1,0:T(8,128)(2,1)S(1)} %constant_dynamic-update-slice_fusion.5.x_ref.x0), channel_id=1, source_target_pairs={{0,1},{1,0},{2,3},{3,2},{4,5},{5,4},{6,7},{7,6},{8,9},{9,8},{10,11... | collective-permute-start | bytes 7864328 | tf_op jit(solution)/shard_map/ppermute | solution.py:100
  274.3 34.4 %collective-permute-start.42 = (bf16[4,64,2048]{2,1,0:T(8,128)(2,1)S(1)}, bf16[4,64,2048]{2,1,0:T(8,128)(2,1)S(1)}, u32[]{:S(2)}, u32[]{:S(2)}) collective-permute-start(bf16[4,64,2048]{2,1,0:T(8,128)(2,1)S(1)} %pad_maximum_fusion.6), channel_id=1, source_target_pairs={{0,8},{8,0},{16,24},{24,16},{1,9},{9,1},{17,25},{25,17},{2,10},{10... | collective-permute-start | bytes 3145736 | tf_op jit(solution)/shard_map/ppermute | solution.py:100
  274.9 33.8 %collective-permute-start.43 = (bf16[4,64,2048]{2,1,0:T(8,128)(2,1)S(1)}, bf16[4,64,2048]{2,1,0:T(8,128)(2,1)S(1)}, u32[]{:S(2)}, u32[]{:S(2)}) collective-permute-start(bf16[4,64,2048]{2,1,0:T(8,128)(2,1)S(1)} %pad_maximum_fusion.7), channel_id=1, source_target_pairs={{0,16},{8,24},{16,0},{24,8},{1,17},{9,25},{17,1},{25,9},{2,18},{10... | collective-permute-start | bytes 3145736 | tf_op jit(solution)/shard_map/ppermute | solution.py:100
  277.9 30.8 %collective-permute-start.45 = (bf16[160,2048]{1,0:T(8,128)(2,1)}, bf16[160,2048]{1,0:T(8,128)(2,1)S(1)}, u32[]{:S(2)}, u32[]{:S(2)}) collective-permute-start(bf16[160,2048]{1,0:T(8,128)(2,1)} %get-tuple-element.264), channel_id=1, source_target_pairs={{0,6},{1,7},{2,0},{3,1},{4,2},{5,3},{6,4},{7,5},{8,14},{9,15},{10,... | collective-permute-start | bytes 1966088 | tf_op jit(solution)/shard_map/ppermute | solution.py:100
  308.8 30.9 %collective-permute-start.46 = (bf16[160,2048]{1,0:T(8,128)(2,1)}, bf16[160,2048]{1,0:T(8,128)(2,1)}, u32[]{:S(2)}, u32[]{:S(2)}) collective-permute-start(bf16[160,2048]{1,0:T(8,128)(2,1)} %get-tuple-element.264), channel_id=1, source_target_pairs={{0,4},{1,5},{2,6},{3,7},{4,0},{5,1},{6,2},{7,3},{8,12},{9,13},{10,... | collective-permute-start | bytes 1966088 | tf_op jit(solution)/shard_map/ppermute | solution.py:100
  353.3 30.9 %collective-permute-start.50 = (bf16[160,2048]{1,0:T(8,128)(2,1)S(1)}, bf16[160,2048]{1,0:T(8,128)(2,1)S(1)}, u32[]{:S(2)}, u32[]{:S(2)}) collective-permute-start(bf16[160,2048]{1,0:T(8,128)(2,1)S(1)} %get-tuple-element.268), channel_id=1, source_target_pairs={{0,6},{1,7},{2,0},{3,1},{4,2},{5,3},{6,4},{7,5},{8,14},{9,15},{10,... | collective-permute-start | bytes 1966088 | tf_op jit(solution)/shard_map/ppermute | solution.py:100
  385.0 32.6 %collective-permute-start.51 = (bf16[160,2048]{1,0:T(8,128)(2,1)}, bf16[160,2048]{1,0:T(8,128)(2,1)S(1)}, u32[]{:S(2)}, u32[]{:S(2)}) collective-permute-start(bf16[160,2048]{1,0:T(8,128)(2,1)} %get-tuple-element.271), channel_id=1, source_target_pairs={{0,4},{1,5},{2,6},{3,7},{4,0},{5,1},{6,2},{7,3},{8,12},{9,13},{10,... | collective-permute-start | bytes 1966088 | tf_op jit(solution)/shard_map/ppermute | solution.py:100
  417.6 35.6 %collective-permute-start.55 = (bf16[4,64,2048]{2,1,0:T(8,128)(2,1)}, bf16[4,64,2048]{2,1,0:T(8,128)(2,1)}, u32[]{:S(2)}, u32[]{:S(2)}) collective-permute-start(bf16[4,64,2048]{2,1,0:T(8,128)(2,1)} %get-tuple-element.277), channel_id=1, source_target_pairs={{0,8},{8,0},{16,24},{24,16},{1,9},{9,1},{17,25},{25,17},{2,10},{10... | collective-permute-start | bytes 3145736 | tf_op jit(solution)/shard_map/ppermute | solution.py:100
  418.7 34.4 %collective-permute-start.56 = (bf16[4,64,2048]{2,1,0:T(8,128)(2,1)}, bf16[4,64,2048]{2,1,0:T(8,128)(2,1)}, u32[]{:S(2)}, u32[]{:S(2)}) collective-permute-start(bf16[4,64,2048]{2,1,0:T(8,128)(2,1)} %get-tuple-element.279), channel_id=1, source_target_pairs={{0,16},{8,24},{16,0},{24,8},{1,17},{9,25},{17,1},{25,9},{2,18},{10... | collective-permute-start | bytes 3145736 | tf_op jit(solution)/shard_map/ppermute | solution.py:100
  423.2 30.0 %collective-permute-start.54 = (bf16[160,2048]{1,0:T(8,128)(2,1)S(1)}, bf16[160,2048]{1,0:T(8,128)(2,1)S(1)}, u32[]{:S(2)}, u32[]{:S(2)}) collective-permute-start(bf16[160,2048]{1,0:T(8,128)(2,1)S(1)} %get-tuple-element.274), channel_id=1, source_target_pairs={{0,6},{1,7},{2,0},{3,1},{4,2},{5,3},{6,4},{7,5},{8,14},{9,15},{10,... | collective-permute-start | bytes 1966088 | tf_op jit(solution)/shard_map/ppermute | solution.py:100
  453.8 31.3 %collective-permute-start.59 = (bf16[4,64,2048]{2,1,0:T(8,128)(2,1)}, bf16[4,64,2048]{2,1,0:T(8,128)(2,1)S(1)}, u32[]{:S(2)}, u32[]{:S(2)}) collective-permute-start(bf16[4,64,2048]{2,1,0:T(8,128)(2,1)} %get-tuple-element.289), channel_id=1, source_target_pairs={{0,16},{8,24},{16,0},{24,8},{1,17},{9,25},{17,1},{25,9},{2,18},{10... | collective-permute-start | bytes 3145736 | tf_op jit(solution)/shard_map/ppermute | solution.py:100
  454.7 30.4 %collective-permute-start.57 = (bf16[160,2048]{1,0:T(8,128)(2,1)}, bf16[160,2048]{1,0:T(8,128)(2,1)S(1)}, u32[]{:S(2)}, u32[]{:S(2)}) collective-permute-start(bf16[160,2048]{1,0:T(8,128)(2,1)} %get-tuple-element.284), channel_id=1, source_target_pairs={{0,4},{1,5},{2,6},{3,7},{4,0},{5,1},{6,2},{7,3},{8,12},{9,13},{10,... | collective-permute-start | bytes 1966088 | tf_op jit(solution)/shard_map/ppermute | solution.py:100
  485.1 47.8 %collective-permute-start.62 = (bf16[4,64,2048]{2,1,0:T(8,128)(2,1)}, bf16[4,64,2048]{2,1,0:T(8,128)(2,1)}, u32[]{:S(2)}, u32[]{:S(2)}) collective-permute-start(bf16[4,64,2048]{2,1,0:T(8,128)(2,1)} %add.227), channel_id=1, source_target_pairs={{0,16},{8,24},{16,0},{24,8},{1,17},{9,25},{17,1},{25,9},{2,18},{10... | collective-permute-start | bytes 3145736 | tf_op jit(solution)/shard_map/ppermute | solution.py:100
  487.6 45.3 %collective-permute-start.63 = (bf16[4,64,2048]{2,1,0:T(8,128)(2,1)}, bf16[4,64,2048]{2,1,0:T(8,128)(2,1)}, u32[]{:S(2)}, u32[]{:S(2)}) collective-permute-start(bf16[4,64,2048]{2,1,0:T(8,128)(2,1)} %add.228), channel_id=1, source_target_pairs={{0,8},{8,0},{16,24},{24,16},{1,9},{9,1},{17,25},{25,17},{2,10},{10... | collective-permute-start | bytes 3145736 | tf_op jit(solution)/shard_map/ppermute | solution.py:100
  532.9 30.5 %collective-permute-start.64 = (bf16[160,2048]{1,0:T(8,128)(2,1)S(1)}, bf16[160,2048]{1,0:T(8,128)(2,1)S(1)}, u32[]{:S(2)}, u32[]{:S(2)}) collective-permute-start(bf16[160,2048]{1,0:T(8,128)(2,1)S(1)} %get-tuple-element.299), channel_id=1, source_target_pairs={{0,4},{1,5},{2,6},{3,7},{4,0},{5,1},{6,2},{7,3},{8,12},{9,13},{10,... | collective-permute-start | bytes 1966088 | tf_op jit(solution)/shard_map/ppermute | solution.py:100
  585.6 34.6 %collective-permute-start.72 = (bf16[2,64,2048]{2,1,0:T(8,128)(2,1)}, bf16[2,64,2048]{2,1,0:T(8,128)(2,1)}, u32[]{:S(2)}, u32[]{:S(2)}) collective-permute-start(bf16[2,64,2048]{2,1,0:T(8,128)(2,1)} %pad_maximum_fusion.32), channel_id=1, source_target_pairs={{0,4},{1,5},{2,6},{3,7},{4,0},{5,1},{6,2},{7,3},{8,12},{9,13},{10,... | collective-permute-start | bytes 1572872 | tf_op jit(solution)/shard_map/ppermute | solution.py:100
  661.3 37.1 %collective-permute-start.86 = (bf16[8,64,768]{2,1,0:T(8,128)(2,1)S(1)}, bf16[8,64,768]{2,1,0:T(8,128)(2,1)S(1)}, u32[]{:S(2)}, u32[]{:S(2)}) collective-permute-start(bf16[8,64,768]{2,1,0:T(8,128)(2,1)S(1)} %pad_maximum_fusion.22), channel_id=1, source_target_pairs={{0,16},{8,24},{16,0},{24,8},{1,17},{9,25},{17,1},{25,9},{2,18},{10... | collective-permute-start | bytes 2359304 | tf_op jit(solution)/shard_map/ppermute | solution.py:100
  701.0 32.0 %collective-permute-start.90 = (bf16[4,64,2048]{2,1,0:T(8,128)(2,1)S(1)}, bf16[4,64,2048]{2,1,0:T(8,128)(2,1)S(1)}, u32[]{:S(2)}, u32[]{:S(2)}) collective-permute-start(bf16[4,64,2048]{2,1,0:T(8,128)(2,1)S(1)} %pad_maximum_fusion.13), channel_id=1, source_target_pairs={{0,8},{8,0},{16,24},{24,16},{1,9},{9,1},{17,25},{25,17},{2,10},{10... | collective-permute-start | bytes 3145736 | tf_op jit(solution)/shard_map/ppermute | solution.py:100
  701.7 31.3 %collective-permute-start.91 = (bf16[4,64,2048]{2,1,0:T(8,128)(2,1)S(1)}, bf16[4,64,2048]{2,1,0:T(8,128)(2,1)S(1)}, u32[]{:S(2)}, u32[]{:S(2)}) collective-permute-start(bf16[4,64,2048]{2,1,0:T(8,128)(2,1)S(1)} %pad_maximum_fusion.14), channel_id=1, source_target_pairs={{0,16},{8,24},{16,0},{24,8},{1,17},{9,25},{17,1},{25,9},{2,18},{10... | collective-permute-start | bytes 3145736 | tf_op jit(solution)/shard_map/ppermute | solution.py:100
  702.7 30.3 %collective-permute-start.89 = (bf16[160,2048]{1,0:T(8,128)(2,1)S(1)}, bf16[160,2048]{1,0:T(8,128)(2,1)S(1)}, u32[]{:S(2)}, u32[]{:S(2)}) collective-permute-start(bf16[160,2048]{1,0:T(8,128)(2,1)S(1)} %get-tuple-element.345), channel_id=1, source_target_pairs={{0,4},{1,5},{2,6},{3,7},{4,0},{5,1},{6,2},{7,3},{8,12},{9,13},{10,... | collective-permute-start | bytes 1966088 | tf_op jit(solution)/shard_map/ppermute | solution.py:100
  (283 other events, 4897.8 us)

commit v3 on v2

--- a/solution.py
+++ b/solution.py
@@ -225,21 +225,30 @@
     return [[came[u, m] for m in key] for u, key in enumerate(keys)]
 
 
-def chip_exchange(x, counts=(), out=None):
+def chip_exchange(x, counts=(), out=None, split=None):
     shards = lax.axis_size("shard")
     me = lax.axis_index("shard")
     pick = lambda k: lax.dynamic_index_in_dim(x, me ^ k, 0, keepdims=False)
     (came,) = yield [
         (sender("shard", [(i, i ^ 1) for i in range(shards)]), jnp.stack([pick(k) for k in range(1, shards, 2)]))
     ]
-    held = [jnp.stack([pick(2 * q), came[q]]) for q in range(shards // 2)]
     out, counts = [] if out is None else out, list(counts)
-    out += [held[0][0], held[0][1]]
-    while len(out) < shards:
-        q = len(out) // 2
-        step = range(q, min(shards // 2, q + (counts.pop(0) if counts else shards)))
-        came = yield [(sender("shard", [(i, i ^ (2 * q)) for i in range(shards)]), held[q]) for q in step]
-        out += [v[f] for v in came for f in range(2)]
+    blocks = {0: pick(0), 1: came[0]}
+    left = []
+    for q in range(1, shards // 2):
+        if split is None or q < split:
+            left.append(((2 * q, 2 * q + 1), jnp.stack([pick(2 * q), came[q]])))
+        else:
+            left += [((2 * q + 1,), came[q]), ((2 * q,), pick(2 * q))]
+    while left:
+        amount = counts.pop(0) if counts else len(left)
+        step, left = left[:amount], left[amount:]
+        arrived = yield [
+            (sender("shard", [(i, i ^ (keys[0] & ~1)) for i in range(shards)]), v) for keys, v in step
+        ]
+        for (keys, _), v in zip(step, arrived):
+            blocks |= {k: v[f] for f, k in enumerate(keys)} if len(keys) > 1 else {keys[0]: v}
+        out[:] = [blocks[k] for k in range(shards) if all(i in blocks for i in range(k + 1))]
     return out
 
 
@@ -852,14 +861,18 @@
     return pltpu.roll(values, values.shape[-1] // 2, 1)
 
 
-def allowed(place_ref, query_place, query_start):
-    keys = place_ref[...]
-    return (keys <= query_place) & (keys >= query_start)
+def allowed(places, query_place, query_start):
+    return (places <= query_place) & (places >= query_start)
+
+
+def key_chunks(tokens):
+    step = 128 if tokens % 128 == 0 else tokens
+    return [slice(i, i + step) for i in range(0, tokens, step)]
 
 
 def attend_kernel(
     heads, width, q_ref, k_ref, v_ref, cos_q, sin_q, cos_k, sin_k, key_place, query_place, query_start,
-    out_ref, rot_q_ref, rot_k_ref, log_ref, value_t,
+    out_ref, rot_q_ref, rot_k_ref, log_ref, value_t, scores, weights,
 ):
     scale = width ** (-0.5)
 
@@ -871,24 +884,37 @@
             rot_k_ref[:, cut] = (key * cos_k[...] + turn(key) * sin_k[...]).astype(BF16)
             value_t[cut, :] = v_ref[:, cut].T
 
-    mask = allowed(key_place, query_place[...], query_start[...])
+    chunks_here = key_chunks(k_ref.shape[0])
+    tops = []
     for h in range(heads):
         cut = slice(h * width, (h + 1) * width)
         query = q_ref[:, cut].astype(F32)
         query = (query * cos_q[...] + turn(query) * sin_q[...]).astype(BF16)
         rot_q_ref[:, cut] = query
-        scores = jnp.where(mask, dot(rot_k_ref[:, cut], query, NT), NEGATIVE)
-        top = jnp.max(scores, axis=0, keepdims=True)
-        weights = jnp.exp2((scores - top) * (scale * LOG2E))
-        total = jnp.sum(weights, axis=0, keepdims=True)
-        weights = (weights * (1.0 / total)).astype(BF16)
-        out_ref[:, cut] = dot(value_t[cut, :], weights).T.astype(BF16)
-        log_ref[h : h + 1] = top * (scale * LOG2E) + jnp.log2(total)
+        tops.append(jnp.full((8, query.shape[0]), NEGATIVE, F32))
+        scores[h] = dot(rot_k_ref[:, cut], query, NT)
+    for keys in chunks_here:
+        mask = allowed(key_place[keys, :], query_place[...], query_start[...])
+        for h in range(heads):
+            part = jnp.where(mask, scores[h, keys, :], NEGATIVE)
+            scores[h, keys, :] = part
+            tops[h] = jnp.maximum(tops[h], jnp.max(part.reshape(-1, 8, part.shape[1]), axis=0))
+    for h in range(heads):
+        cut = slice(h * width, (h + 1) * width)
+        top = jnp.max(tops[h], axis=0, keepdims=True) * (scale * LOG2E)
+        total = jnp.zeros((8, top.shape[1]), F32)
+        for keys in chunks_here:
+            part = jnp.exp2(scores[h, keys, :] * (scale * LOG2E) - top)
+            total = total + jnp.sum(part.reshape(-1, 8, part.shape[1]), axis=0)
+            weights[keys, :] = part.astype(BF16)
+        total = jnp.sum(total, axis=0, keepdims=True)
+        out_ref[:, cut] = (dot(value_t[cut, :], weights[...]) * (1.0 / total)).T.astype(BF16)
+        log_ref[h : h + 1] = top + jnp.log2(total)
 
 
 def attend_back_kernel(
-    heads, width, q_ref, k_ref, v_ref, grad_ref, log_ref, cos_q, sin_q, cos_k, sin_k, key_place, query_place,
-    query_start, out_ref, key_t, sum_k, sum_v,
+    heads, width, q_ref, k_ref, v_ref, out_rows_ref, grad_ref, log_ref, cos_q, sin_q, cos_k, sin_k, key_place,
+    query_place, query_start, out_ref, key_t, sum_k, sum_v, scores, grads, low_weights, low_grads,
 ):
     scale = width ** (-0.5)
     step = pl.program_id(0)
@@ -903,20 +929,22 @@
         sum_k[...] = jnp.zeros_like(sum_k)
         sum_v[...] = jnp.zeros_like(sum_v)
 
-    mask = allowed(key_place, query_place[...], query_start[...])
     for h in range(heads):
         cut = slice(h * width, (h + 1) * width)
-        query = q_ref[:, cut]
-        grad = grad_ref[:, cut]
-        scores = dot(k_ref[:, cut], query, NT) * (scale * LOG2E) - log_ref[h : h + 1]
-        weights = jnp.exp2(jnp.where(mask, scores, NEGATIVE))
-        grad_weights = dot(v_ref[:, cut], grad, NT)
-        centre = jnp.sum(weights * grad_weights, axis=0, keepdims=True)
-        grad_scores = (weights * (grad_weights - centre)).astype(BF16)
-        grad_query = (dot(key_t[cut, :], grad_scores) * scale).T
+        query, grad = q_ref[:, cut], grad_ref[:, cut]
+        centre = jnp.sum((grad.astype(F32) * out_rows_ref[:, cut].astype(F32)).T, axis=0, keepdims=True)
+        scores[...] = dot(k_ref[:, cut], query, NT)
+        grads[...] = dot(v_ref[:, cut], grad, NT)
+        for keys in key_chunks(k_ref.shape[0]):
+            mask = allowed(key_place[keys, :], query_place[...], query_start[...])
+            part = scores[keys, :] * (scale * LOG2E) - log_ref[h : h + 1]
+            weights = jnp.exp2(jnp.where(mask, part, NEGATIVE))
+            low_weights[keys, :] = weights.astype(BF16)
+            low_grads[keys, :] = (weights * (grads[keys, :] - centre)).astype(BF16)
+        sum_v[:, cut] += dot(low_weights[...], grad)
+        sum_k[:, cut] += dot(low_grads[...], query)
+        grad_query = (dot(key_t[cut, :], low_grads[...]) * scale).T
         out_ref[here, cut] = (grad_query * cos_q[...] - turn(grad_query) * sin_q[...]).astype(BF16)
-        sum_k[:, cut] += dot(grad_scores, query)
-        sum_v[:, cut] += dot(weights.astype(BF16), grad)
 
     @pl.when(step == pl.num_programs(0) - 1)
     def _():
@@ -965,13 +993,15 @@
             jax.ShapeDtypeStruct((tokens, width), BF16),
             jax.ShapeDtypeStruct((heads, tokens), F32),
         ],
-        scratch_shapes=[pltpu.VMEM((width, tokens), BF16)],
+        scratch_shapes=[pltpu.VMEM((width, tokens), BF16), pltpu.VMEM((heads, tokens, block), F32),
+            pltpu.VMEM((tokens, block), BF16),
+        ],
         compiler_params=params(48),
         cost_estimate=NO_COST,
     )(qkv, qkv, qkv, cosine, sine, cosine, sine, key_place, place[None], start[None])
 
 
-def attention_back(qkv, rot_q, rot_k, grad, logs, cosine, sine, place, start, heads):
+def attention_back(qkv, rot_q, rot_k, attended, grad, logs, cosine, sine, place, start, heads):
     tokens, width = rot_q.shape
     head_width = width // heads
     block = 256 if tokens % 256 == 0 else tokens
@@ -986,6 +1016,7 @@
             pl.BlockSpec((block, width), row),
             pl.BlockSpec((tokens, width), whole),
             pl.BlockSpec((tokens, width), lambda i: (0, 2)),
+            pl.BlockSpec((block, width), row),
             pl.BlockSpec((block, width), row),
             pl.BlockSpec((heads, block), along),
             pl.BlockSpec((block, head_width), row),
@@ -1002,10 +1033,14 @@
             pltpu.VMEM((width, tokens), BF16),
             pltpu.VMEM((tokens, width), F32),
             pltpu.VMEM((tokens, width), F32),
+            pltpu.VMEM((tokens, block), F32),
+            pltpu.VMEM((tokens, block), F32),
+            pltpu.VMEM((tokens, block), BF16),
+            pltpu.VMEM((tokens, block), BF16),
         ],
         compiler_params=params(56),
         cost_estimate=NO_COST,
-    )(rot_q, rot_k, qkv, grad, logs, cosine, sine, cosine, sine, key_place, place[None], start[None])
+    )(rot_q, rot_k, qkv, attended, grad, logs, cosine, sine, cosine, sine, key_place, place[None], start[None])
 
 
 def sequence_places(ordering, lengths):
@@ -1084,7 +1119,7 @@
     cosine, sine = rope_tables(place - start, head_width)
     w = tie(cotangent).transpose(1, 0, 2)
     gate_up_blocks = []
-    recut_gate_up = Task(chip_exchange(gate_up_piece, (line // 4, line // 4), gate_up_blocks))
+    recut_gate_up = Task(chip_exchange(gate_up_piece, (line // 4, line // 4, line // 4), gate_up_blocks, line - 1))
     run(gather_in, recut_gate_up)
     hold(cosine, sine, w)
     finish(gather_in, gather_qkv)
@@ -1105,11 +1140,12 @@
     gather_low = Task(rep_gather(stack_units(gate_up_blocks[: shards // 2], 2), True))
     tokens_out = Task(to_tokens(attended.reshape(2, line, tokens, local)))
     run(tokens_out, recut_gate_up, gather_low)
-    finish(recut_gate_up)
     output_mine = rows_in_order(gather_output.value)
     swap = Task(other_core(output_mine))
     run(tokens_out, swap)
     branch = dot(tokens_out.value[0], output_mine) + dot(tokens_out.value[1], swap.value)
+    hold(branch)
+    run(recut_gate_up)
 
     middle, entering_next, down_in, packed_next = token_call(
         middle_kernel, tokens,
@@ -1120,6 +1156,7 @@
         ],
     )
     finish(recut_gate_up)
+    hold(entering_next)
     gather_high = Task(rep_gather(stack_units(gate_up_blocks[shards // 2 :], 2), True))
     gather_ffn, gather_down = Task(direct_gather(entering_next, 2)), Task(direct_gather(down_in, 2))
     run(gather_ffn, gather_low)
@@ -1148,9 +1185,11 @@
     run(scatter_z)
     grad_both = ffn_backward(other_down, down_weight, by_gate, by_up, 1, (filled,))
     theirs = product((grad_both, 1), gate_up, NT)
-    hold(theirs)
+    down_blocks = rows_product([(active, 0), (active, 1)], [mine_down, other_down], 2)
+    hold(theirs, *down_blocks[0])
     swap = Task(other_core(theirs))
-    run(scatter_z, swap)
+    scatter_down = Task(rep_scatter(down_blocks, True))
+    run(scatter_z, swap, scatter_down)
     f_mine = product((grad_both, 0), gate_up, NT, add=swap.value)
     ready = after(grad_both, f_mine)
     gate_up_blocks = columns_product([mine_ffn, other_ffn], [(ready, 0), (ready, 1)], 2)
@@ -1158,8 +1197,6 @@
     scatter_f = Task(direct_scatter(f_mine, 2))
     scatter_gate_up = Task(rep_scatter(gate_up_blocks))
     run(scatter_f, (scatter_gate_up, 1))
-    down_blocks = rows_product([(active, 0), (active, 1)], [mine_down, other_down], 2)
-    hold(*down_blocks[0])
     run(scatter_f, scatter_gate_up)
     finish(scatter_f)
 
@@ -1183,34 +1220,34 @@
         out_kernel, tokens, [tie(middle), packed_next, static[1], *scatter_z.value],
         [shape((tokens, count, width), BF16)],
     )
-    scatter_down = Task(rep_scatter(down_blocks, True))
     run(gather_branch, scatter_down)
     hold(result)
     finish(gather_branch)
     mine_branch = gather_branch.value
     swap = Task(other_core(mine_branch))
     run(swap, recut_grad)
+    finish(scatter_down)
+    gather_down_rows = Task(rep_gather(scatter_down.value, True))
     grad_mine = product(mine_branch, output_weight, NT, into=0)
     other_branch = swap.value
-    run(recut_grad, scatter_down)
-    finish(scatter_down)
-    gather_down_rows = Task(rep_gather(scatter_down.value, True))
+    run(recut_grad, gather_down_rows)
     output_blocks = rows_product([(attended, 0), (attended, 1)], [mine_branch, other_branch], 2)
     hold(*output_blocks[0])
     grad_attended = product(other_branch, output_weight, NT, into=1, filled=(grad_mine,))
-    grad_qkv = attention_back(qkv, rot_q, rot_k, grad_attended, logs, cosine, sine, place, start, heads)
+    hold(grad_attended)
+    grad_qkv = attention_back(qkv, rot_q, rot_k, attended, grad_attended, logs, cosine, sine, place, start, heads)
     theirs = product((grad_qkv, 1), attention_weight, NT)
+    run(recut_grad, gather_down_rows)
+    hold(theirs)
     gather_low = Task(rep_gather(stack_units(low[: shards // 2], 2), True))
-    run(recut_grad, gather_down_rows, gather_low)
-    hold(theirs)
     scatter_output = Task(rep_scatter(output_blocks, True))
-    run(recut_grad, gather_down_rows)
+    run(recut_grad, gather_low, scatter_output)
     finish(recut_grad, gather_down_rows)
     qkv_blocks = columns_product([mine_in, other_in], [(grad_qkv, 0), (grad_qkv, 1)], 2)
     hold(*qkv_blocks[0])
     gather_high = Task(rep_gather(stack_units(low[shards // 2 :], 2), True))
     swap = Task(other_core(theirs))
-    run(swap, scatter_output)
+    run(swap)
     scatter_a = Task(direct_scatter(product((grad_qkv, 0), attention_weight, NT, add=swap.value), 2))
     scatter_qkv = Task(rep_scatter(qkv_blocks, True))
     run(scatter_a, scatter_qkv)

time: 844 us -> 817 us (0.968)
  starting transfers between devices: 148 us -> 138 us
    ppermute x117 -> x118, starting transfers between devices: 148 us -> 138 us  [sender(): return lambda x: lax.ppermute(x, axis, pairs)]
    unnamed x396 -> x394, local copies, waits for them, and re-layouts: 36.1 us -> 31.4 us
    ppermute x117 -> x118, waiting for transfers between devices: 341 us -> 341 us  [sender(): return lambda x: lax.ppermute(x, axis, pairs)]
  transfers between devices with their start and end apart: 117 -> 118, of which waited for: 55 -> 52; matrix products, arithmetic and copies ran while one was open for 10% -> 9% of each run, Pallas kernels for 27% -> 27%
where the time goes in v3:
time: 817 us; the launch traced here: 811 us
  waiting for transfers between devices  341 us (42%)
  Pallas kernels  224 us (27%)
  starting transfers between devices  138 us (17%)
  local copies, waits for them, and re-layouts  60.2 us (7%)
  other arithmetic  41.7 us (5%)
    ppermute x118, waiting for transfers between devices, sender(): return lambda x: lax.ppermute(x, axis, pairs)  341 us
    ppermute x118, starting transfers between devices, sender(): return lambda x: lax.ppermute(x, axis, pairs)  138 us
    pallas_call x6, Pallas kernels, token_call(): pl.pallas_call(kernel, grid=(tokens // block,), in_specs=[spec(o.shape) f...  55.3 us
    pallas_call x10, Pallas kernels, product(): pl.pallas_call(functools.partial(product_kernel, dims, add is not None),...  41.3 us
    unnamed x394, local copies, waits for them, and re-layouts  31.4 us
    pallas_call x2, Pallas kernels, columns_product(): pl.pallas_call(functools.partial(columns_product_kernel, units, reps), gr...  28.1 us
    pallas_call x6, Pallas kernels, join(): pl.pallas_call(functools.partial(columns_kernel, len(units), reps, parts)...  23.2 us
    pallas_call x2, Pallas kernels, ffn_forward(): pl.pallas_call(ffn_kernel, grid=(tiles,), in_specs=[pl.BlockSpec((rows, w...  17.3 us
  transfers between devices with their start and end apart: 118, of which 52 were waited for; matrix products, arithmetic and copies ran while one was open for 9% of the time, Pallas kernels for 27%

profile of v3, /device:TPU:0, one launch (start us, length us, event | category | flops | bytes accessed | tf_op | source)
XLA Modules:
  0.0 810.5 jit_solution(18401634381203196399)
XLA Ops:
  19.1 11.5 %shard_map.213 = (bf16[160,2048]{1,0:T(8,128)(2,1)S(1)}, f32[4,160,128]{2,1,0:T(8,128)S(1)}, bf16[4,160,2048]{2,1,0:T(8,128)(2,1)S(1)}) custom-call(bf16[160,4,2048]{2,1,0:T(4,128)(2,1)S(1)} %copy-done.49, bf16[128,2048]{1,0:T(8,128)(2,1)S(1)} %get-tuple-element.501.weight_ref.weight_rows_ref, f32[4,128]{1,0:T(4,128)S(1)} %get-tuple-element.576.static_ref.static_first_ref), custom_call_target="tpu_custom_call" | custom-call | tf_op jit(solution)/shard_map/pallas_call | solution.py:652
  68.7 9.7 %collective-permute-done.14 = bf16[8,64,768]{2,1,0:T(8,128)(2,1)S(1)} collective-permute-done((bf16[8,64,768]{2,1,0:T(8,128)(2,1)S(1)}, bf16[8,64,768]{2,1,0:T(8,128)(2,1)S(1)}, u32[]{:S(2)}, u32[]{:S(2)}) %collective-permute-start.14) | collective-permute-done | bytes 786464 | tf_op jit(solution)/shard_map/ppermute | solution.py:100
  91.6 12.6 %collective-permute-done.17.refs_5_ = bf16[224,2048]{1,0:T(8,128)(2,1)} collective-permute-done((bf16[224,2048]{1,0:T(8,128)(2,1)}, bf16[224,2048]{1,0:T(8,128)(2,1)}, u32[]{:S(2)}, u32[]{:S(2)}) %collective-permute-start.17) | collective-permute-done | bytes 917536 | tf_op jit(solution)/shard_map/ppermute | solution.py:100
  137.0 9.9 %shard_map.218 = (bf16[1280,256]{1,0:T(8,128)(2,1)S(1)}, bf16[1280,256]{1,0:T(8,128)(2,1)S(1)}, bf16[1280,256]{1,0:T(8,128)(2,1)S(1)}, f32[2,1280]{1,0:T(2,128)S(1)}) custom-call(bf16[1280,768]{1,0:T(8,128)(2,1)} %copy-done.5, bf16[1280,768]{1,0:T(8,128)(2,1)} %copy-done.5, bf16[1280,768]{1,0:T(8,128)(2,1)} %copy-done.5, ...), custom_call_target="tpu_custom_call" | custom-call | tf_op jit(solution)/shard_map/pallas_call | solution.py:969
  202.6 14.4 %collective-permute-done.35 = bf16[160,2048]{1,0:T(8,128)(2,1)S(1)} collective-permute-done((bf16[160,2048]{1,0:T(8,128)(2,1)S(1)}, bf16[160,2048]{1,0:T(8,128)(2,1)S(1)}, u32[]{:S(2)}, u32[]{:S(2)}) %collective-permute-start.35) | collective-permute-done | bytes 655392 | tf_op jit(solution)/shard_map/ppermute | solution.py:100
  217.0 16.9 %collective-permute-done.36 = bf16[160,2048]{1,0:T(8,128)(2,1)S(1)} collective-permute-done((bf16[160,2048]{1,0:T(8,128)(2,1)S(1)}, bf16[160,2048]{1,0:T(8,128)(2,1)S(1)}, u32[]{:S(2)}, u32[]{:S(2)}) %collective-permute-start.36) | collective-permute-done | bytes 655392 | tf_op jit(solution)/shard_map/ppermute | solution.py:100
  236.1 24.8 %collective-permute-done.39 = bf16[160,2048]{1,0:T(8,128)(2,1)S(1)} collective-permute-done((bf16[160,2048]{1,0:T(8,128)(2,1)S(1)}, bf16[160,2048]{1,0:T(8,128)(2,1)S(1)}, u32[]{:S(2)}, u32[]{:S(2)}) %collective-permute-start.39) | collective-permute-done | bytes 655392 | tf_op jit(solution)/shard_map/ppermute | solution.py:100
  270.7 14.6 %collective-permute-done.45 = bf16[160,2048]{1,0:T(8,128)(2,1)S(1)} collective-permute-done((bf16[160,2048]{1,0:T(8,128)(2,1)}, bf16[160,2048]{1,0:T(8,128)(2,1)S(1)}, u32[]{:S(2)}, u32[]{:S(2)}) %collective-permute-start.45) | collective-permute-done | bytes 655392 | tf_op jit(solution)/shard_map/ppermute | solution.py:100
  285.2 11.2 %collective-permute-done.46 = bf16[160,2048]{1,0:T(8,128)(2,1)S(1)} collective-permute-done((bf16[160,2048]{1,0:T(8,128)(2,1)}, bf16[160,2048]{1,0:T(8,128)(2,1)S(1)}, u32[]{:S(2)}, u32[]{:S(2)}) %collective-permute-start.46) | collective-permute-done | bytes 655392 | tf_op jit(solution)/shard_map/ppermute | solution.py:100
  369.1 10.5 %shard_map.230 = (bf16[128,2048]{1,0:T(8,128)(2,1)S(1)}, bf16[128,2048]{1,0:T(8,128)(2,1)S(1)}, bf16[128,2048]{1,0:T(8,128)(2,1)S(1)}, bf16[128,2048]{1,0:T(8,12...) custom-call(s32[1]{0:T(128)} %bitcast.23.me_ref, ...), custom_call_target="tpu_custom_call" | custom-call | tf_op jit(solution)/shard_map/pallas_call | solution.py:768
  392.9 19.3 %shard_map.232 = (bf16[4,64,2048]{2,1,0:T(8,128)(2,1)S(1)}, bf16[4,64,2048]{2,1,0:T(8,128)(2,1)S(1)}, bf16[4,64,2048]{2,1,0:T(8,128)(2,1)S(1)}, bf16[4,64,2048]{...) custom-call(s32[1]{0:T(128)} %bitcast.23.me_ref, ...), custom_call_target="tpu_custom_call" | custom-call | tf_op jit(solution)/shard_map/pallas_call | solution.py:732
  420.0 15.6 %collective-permute-done.56.refs_5_ = bf16[160,2048]{1,0:T(8,128)(2,1)S(1)} collective-permute-done((bf16[160,2048]{1,0:T(8,128)(2,1)S(1)}, bf16[160,2048]{1,0:T(8,128)(2,1)S(1)}, u32[]{:S(2)}, u32[]{:S(2)}) %collective-permute-start.56) | collective-permute-done | bytes 655392 | tf_op jit(solution)/shard_map/ppermute | solution.py:100
  435.7 10.7 %collective-permute-done.57.refs_6_ = bf16[160,2048]{1,0:T(8,128)(2,1)S(1)} collective-permute-done((bf16[160,2048]{1,0:T(8,128)(2,1)S(1)}, bf16[160,2048]{1,0:T(8,128)(2,1)S(1)}, u32[]{:S(2)}, u32[]{:S(2)}) %collective-permute-start.57) | collective-permute-done | bytes 655392 | tf_op jit(solution)/shard_map/ppermute | solution.py:100
  451.1 19.0 %collective-permute-done.61 = bf16[4,64,2048]{2,1,0:T(8,128)(2,1)S(1)} collective-permute-done((bf16[4,64,2048]{2,1,0:T(8,128)(2,1)S(1)}, bf16[4,64,2048]{2,1,0:T(8,128)(2,1)S(1)}, u32[]{:S(2)}, u32[]{:S(2)}) %collective-permute-start.61) | collective-permute-done | bytes 1048608 | tf_op jit(solution)/shard_map/ppermute | solution.py:100
  481.2 14.0 %shard_map.233 = (f32[4,160,2048]{2,1,0:T(8,128)}, bf16[160,2048]{1,0:T(8,128)(2,1)S(1)}, f32[160,128]{1,0:T(8,128)S(1)}, f32[128,2048]{1,0:T(8,128)S(1)}, f32[8,128]{1,0:T(8,128)S(1)}) custom-call(f32[4,160,2048]{2,1,0:T(8,128)} %copy-done.14, f32[4,160,128]{2,1,0:T(8,128)S(1)} %copy-done.77, f32[4,128]{1,0:T(4,128)S(1)} %copy-done.120, ...), custom_call_target="tpu_custom_call" | custom-call | tf_op jit(solution)/shard_map/pallas_call | solution.py:652
  500.2 14.5 %collective-permute-done.63 = bf16[160,2048]{1,0:T(8,128)(2,1)S(1)} collective-permute-done((bf16[160,2048]{1,0:T(8,128)(2,1)S(1)}, bf16[160,2048]{1,0:T(8,128)(2,1)S(1)}, u32[]{:S(2)}, u32[]{:S(2)}) %collective-permute-start.63) | collective-permute-done | bytes 655392 | tf_op jit(solution)/shard_map/ppermute | solution.py:100
  514.7 10.0 %collective-permute-done.64 = bf16[160,2048]{1,0:T(8,128)(2,1)S(1)} collective-permute-done((bf16[160,2048]{1,0:T(8,128)(2,1)S(1)}, bf16[160,2048]{1,0:T(8,128)(2,1)S(1)}, u32[]{:S(2)}, u32[]{:S(2)}) %collective-permute-start.64) | collective-permute-done | bytes 655392 | tf_op jit(solution)/shard_map/ppermute | solution.py:100
  537.4 17.1 %collective-permute-done.67 = bf16[160,2048]{1,0:T(8,128)(2,1)S(1)} collective-permute-done((bf16[160,2048]{1,0:T(8,128)(2,1)S(1)}, bf16[160,2048]{1,0:T(8,128)(2,1)S(1)}, u32[]{:S(2)}, u32[]{:S(2)}) %collective-permute-start.67) | collective-permute-done | bytes 655392 | tf_op jit(solution)/shard_map/ppermute | solution.py:100
  586.4 15.2 %shard_map.237.y0.y1.a_ref = bf16[1280,768]{1,0:T(8,128)(2,1)} custom-call(bf16[1280,256]{1,0:T(8,128)(2,1)} %copy-done.84, bf16[1280,256]{1,0:T(8,128)(2,1)} %copy-done.85, bf16[1280,768]{1,0:T(8,128)(2,1)} %copy-done.5, bf16[1280,256]{1,0:T(8,128)(2,1)} %copy-done.24, bf16[1280,256]{1,0:T(8,128)(2,1)} %copy-done.36, f32[2,1280]{1,0:T(2,128)} %copy-done.123, ...), custom_call_target="tpu_custom_call" | custom-call | tf_op jit(solution)/shard_map/pallas_call | solution.py:1012
  663.4 12.6 %collective-permute-done.86.refs_2_ = bf16[160,2048]{1,0:T(8,128)(2,1)S(1)} collective-permute-done((bf16[160,2048]{1,0:T(8,128)(2,1)S(1)}, bf16[160,2048]{1,0:T(8,128)(2,1)S(1)}, u32[]{:S(2)}, u32[]{:S(2)}) %collective-permute-start.86) | collective-permute-done | bytes 655392 | tf_op jit(solution)/shard_map/ppermute | solution.py:100
  690.5 20.2 %collective-permute-done.90.refs_3_ = bf16[160,2048]{1,0:T(8,128)(2,1)S(1)} collective-permute-done((bf16[160,2048]{1,0:T(8,128)(2,1)S(1)}, bf16[160,2048]{1,0:T(8,128)(2,1)S(1)}, u32[]{:S(2)}, u32[]{:S(2)}) %collective-permute-start.90) | collective-permute-done | bytes 655392 | tf_op jit(solution)/shard_map/ppermute | solution.py:100
  717.0 10.9 %collective-permute-done.96 = bf16[32,2048]{1,0:T(8,128)(2,1)S(1)} collective-permute-done((bf16[32,2048]{1,0:T(8,128)(2,1)S(1)}, bf16[32,2048]{1,0:T(8,128)(2,1)S(1)}, u32[]{:S(2)}, u32[]{:S(2)}) %collective-permute-start.96) | collective-permute-done | bytes 131104 | tf_op jit(solution)/shard_map/ppermute | solution.py:100
  739.9 12.3 %shard_map.242 = (f32[160,4,2048]{2,1,0:T(4,128)}, f32[128,2048]{1,0:T(8,128)S(1)}, f32[8,128]{1,0:T(8,128)S(1)}) custom-call(bf16[4,160,2048]{2,1,0:T(8,128)(2,1)S(1)} %copy-done.28, f32[4,160,128]{2,1,0:T(8,128)S(1)} %get-tuple-element.213.packed_ref.packed_first_ref, f32[4,128]{1,0:T(4,128)S(1)} %copy-done.116, f32[4,160,2048]{2,1,0:T(8,128)S(1)} %bitcast.145, ...), custom_call_target="tpu_custom_call" | custom-call | tf_op jit(solution)/shard_map/pallas_call | solution.py:652
  784.1 12.0 %shard_map.244 = (f32[256,8192]{1,0:T(8,128)}, f32[256,8192]{1,0:T(8,128)}) custom-call(s32[2]{0:T(128)} %copy-done.121, bf16[2,64,2048]{2,1,0:T(8,128)(2,1)} %copy-done.139, bf16[2,64,2048]{2,1,0:T(8,128)(2,1)} %get-tuple-element.383.refs_1_, bf16[2,64,2048]{2,1,0:T(8,128)(2,1)} %copy-done.147, bf16[2,64,2048]{2,1,0:T(8,128)(2,1)} %get-tuple-element.385.refs_3_, ...), custom_call_target="tpu_custom_call" | custom-call | tf_op jit(solution)/shard_map/pallas_call | solution.py:317
  (811 shorter events, 466.5 us)
Async XLA Ops:
  195.6 38.2 %collective-permute-start.37 = (bf16[4,64,2048]{2,1,0:T(8,128)(2,1)S(1)}, bf16[4,64,2048]{2,1,0:T(8,128)(2,1)S(1)}, u32[]{:S(2)}, u32[]{:S(2)}) collective-permute-start(bf16[4,64,2048]{2,1,0:T(8,128)(2,1)S(1)} %pad_maximum_fusion.4), channel_id=1, source_target_pairs={{0,8},{8,0},{16,24},{24,16},{1,9},{9,1},{17,25},{25,17},{2,10},{10... | collective-permute-start | bytes 3145736 | tf_op jit(solution)/shard_map/ppermute | solution.py:100
  197.1 36.7 %collective-permute-start.38 = (bf16[4,64,2048]{2,1,0:T(8,128)(2,1)S(1)}, bf16[4,64,2048]{2,1,0:T(8,128)(2,1)S(1)}, u32[]{:S(2)}, u32[]{:S(2)}) collective-permute-start(bf16[4,64,2048]{2,1,0:T(8,128)(2,1)S(1)} %pad_maximum_fusion.5), channel_id=1, source_target_pairs={{0,16},{8,24},{16,0},{24,8},{1,17},{9,25},{17,1},{25,9},{2,18},{10... | collective-permute-start | bytes 3145736 | tf_op jit(solution)/shard_map/ppermute | solution.py:100
  199.6 34.2 %collective-permute-start.36 = (bf16[160,2048]{1,0:T(8,128)(2,1)S(1)}, bf16[160,2048]{1,0:T(8,128)(2,1)S(1)}, u32[]{:S(2)}, u32[]{:S(2)}) collective-permute-start(bf16[160,2048]{1,0:T(8,128)(2,1)S(1)} %get-tuple-element.254), channel_id=1, source_target_pairs={{0,2},{1,3},{2,4},{3,5},{4,6},{5,7},{6,0},{7,1},{8,10},{9,11},{10,... | collective-permute-start | bytes 1966088 | tf_op jit(solution)/shard_map/ppermute | solution.py:100
  261.1 35.3 %collective-permute-start.42 = (bf16[640,2048]{1,0:T(8,128)(2,1)S(1)}, bf16[640,2048]{1,0:T(8,128)(2,1)S(1)}, u32[]{:S(2)}, u32[]{:S(2)}) collective-permute-start(bf16[640,2048]{1,0:T(8,128)(2,1)S(1)} %constant_dynamic-update-slice_fusion.5.x_ref.x0), channel_id=1, source_target_pairs={{0,1},{1,0},{2,3},{3,2},{4,5},{5,4},{6,7},{7,6},{8,9},{9,8},{10,11... | collective-permute-start | bytes 7864328 | tf_op jit(solution)/shard_map/ppermute | solution.py:100
  261.4 35.0 %collective-permute-start.43 = (bf16[4,64,2048]{2,1,0:T(8,128)(2,1)S(1)}, bf16[4,64,2048]{2,1,0:T(8,128)(2,1)S(1)}, u32[]{:S(2)}, u32[]{:S(2)}) collective-permute-start(bf16[4,64,2048]{2,1,0:T(8,128)(2,1)S(1)} %pad_maximum_fusion.6), channel_id=1, source_target_pairs={{0,8},{8,0},{16,24},{24,16},{1,9},{9,1},{17,25},{25,17},{2,10},{10... | collective-permute-start | bytes 3145736 | tf_op jit(solution)/shard_map/ppermute | solution.py:100
  262.5 34.0 %collective-permute-start.44 = (bf16[4,64,2048]{2,1,0:T(8,128)(2,1)S(1)}, bf16[4,64,2048]{2,1,0:T(8,128)(2,1)S(1)}, u32[]{:S(2)}, u32[]{:S(2)}) collective-permute-start(bf16[4,64,2048]{2,1,0:T(8,128)(2,1)S(1)} %pad_maximum_fusion.7), channel_id=1, source_target_pairs={{0,16},{8,24},{16,0},{24,8},{1,17},{9,25},{17,1},{25,9},{2,18},{10... | collective-permute-start | bytes 3145736 | tf_op jit(solution)/shard_map/ppermute | solution.py:100
  265.6 30.8 %collective-permute-start.46 = (bf16[160,2048]{1,0:T(8,128)(2,1)}, bf16[160,2048]{1,0:T(8,128)(2,1)S(1)}, u32[]{:S(2)}, u32[]{:S(2)}) collective-permute-start(bf16[160,2048]{1,0:T(8,128)(2,1)} %get-tuple-element.266), channel_id=1, source_target_pairs={{0,6},{1,7},{2,0},{3,1},{4,2},{5,3},{6,4},{7,5},{8,14},{9,15},{10,... | collective-permute-start | bytes 1966088 | tf_op jit(solution)/shard_map/ppermute | solution.py:100
  296.5 31.0 %collective-permute-start.47 = (bf16[160,2048]{1,0:T(8,128)(2,1)}, bf16[160,2048]{1,0:T(8,128)(2,1)}, u32[]{:S(2)}, u32[]{:S(2)}) collective-permute-start(bf16[160,2048]{1,0:T(8,128)(2,1)} %get-tuple-element.266), channel_id=1, source_target_pairs={{0,4},{1,5},{2,6},{3,7},{4,0},{5,1},{6,2},{7,3},{8,12},{9,13},{10,... | collective-permute-start | bytes 1966088 | tf_op jit(solution)/shard_map/ppermute | solution.py:100
  341.4 38.2 %collective-permute-start.50 = (bf16[160,2048]{1,0:T(8,128)(2,1)}, bf16[160,2048]{1,0:T(8,128)(2,1)}, u32[]{:S(2)}, u32[]{:S(2)}) collective-permute-start(bf16[160,2048]{1,0:T(8,128)(2,1)} %get-tuple-element.269), channel_id=1, source_target_pairs={{0,2},{1,3},{2,4},{3,5},{4,6},{5,7},{6,0},{7,1},{8,10},{9,11},{10,... | collective-permute-start | bytes 1966088 | tf_op jit(solution)/shard_map/ppermute | solution.py:100
  341.5 38.2 %collective-permute-start.51 = (bf16[160,2048]{1,0:T(8,128)(2,1)}, bf16[160,2048]{1,0:T(8,128)(2,1)}, u32[]{:S(2)}, u32[]{:S(2)}) collective-permute-start(bf16[160,2048]{1,0:T(8,128)(2,1)} %get-tuple-element.270), channel_id=1, source_target_pairs={{0,6},{1,7},{2,0},{3,1},{4,2},{5,3},{6,4},{7,5},{8,14},{9,15},{10,... | collective-permute-start | bytes 1966088 | tf_op jit(solution)/shard_map/ppermute | solution.py:100
  382.3 31.5 %collective-permute-start.54 = (bf16[256,2048]{1,0:T(8,128)(2,1)}, bf16[256,2048]{1,0:T(8,128)(2,1)}, u32[]{:S(2)}, u32[]{:S(2)}) collective-permute-start(bf16[256,2048]{1,0:T(8,128)(2,1)} %pad_maximum_fusion.8), channel_id=1, source_target_pairs={{0,8},{8,0},{16,24},{24,16},{1,9},{9,1},{17,25},{25,17},{2,10},{10... | collective-permute-start | bytes 3145736 | tf_op jit(solution)/shard_map/ppermute | solution.py:100
  383.8 30.0 %collective-permute-start.55 = (bf16[256,2048]{1,0:T(8,128)(2,1)}, bf16[256,2048]{1,0:T(8,128)(2,1)}, u32[]{:S(2)}, u32[]{:S(2)}) collective-permute-start(bf16[256,2048]{1,0:T(8,128)(2,1)} %pad_maximum_fusion.9), channel_id=1, source_target_pairs={{0,16},{8,24},{16,0},{24,8},{1,17},{9,25},{17,1},{25,9},{2,18},{10... | collective-permute-start | bytes 3145736 | tf_op jit(solution)/shard_map/ppermute | solution.py:100
  413.7 32.7 %collective-permute-start.58 = (bf16[4,64,2048]{2,1,0:T(8,128)(2,1)S(1)}, bf16[4,64,2048]{2,1,0:T(8,128)(2,1)S(1)}, u32[]{:S(2)}, u32[]{:S(2)}) collective-permute-start(bf16[4,64,2048]{2,1,0:T(8,128)(2,1)S(1)} %get-tuple-element.287), channel_id=1, source_target_pairs={{0,8},{8,0},{16,24},{24,16},{1,9},{9,1},{17,25},{25,17},{2,10},{10... | collective-permute-start | bytes 3145736 | tf_op jit(solution)/shard_map/ppermute | solution.py:100
  414.7 31.7 %collective-permute-start.59 = (bf16[4,64,2048]{2,1,0:T(8,128)(2,1)}, bf16[4,64,2048]{2,1,0:T(8,128)(2,1)S(1)}, u32[]{:S(2)}, u32[]{:S(2)}) collective-permute-start(bf16[4,64,2048]{2,1,0:T(8,128)(2,1)} %get-tuple-element.289), channel_id=1, source_target_pairs={{0,16},{8,24},{16,0},{24,8},{1,17},{9,25},{17,1},{25,9},{2,18},{10... | collective-permute-start | bytes 3145736 | tf_op jit(solution)/shard_map/ppermute | solution.py:100
  416.2 30.2 %collective-permute-start.57 = (bf16[160,2048]{1,0:T(8,128)(2,1)S(1)}, bf16[160,2048]{1,0:T(8,128)(2,1)S(1)}, u32[]{:S(2)}, u32[]{:S(2)}) collective-permute-start(bf16[160,2048]{1,0:T(8,128)(2,1)S(1)} %get-tuple-element.284), channel_id=1, source_target_pairs={{0,6},{1,7},{2,0},{3,1},{4,2},{5,3},{6,4},{7,5},{8,14},{9,15},{10,... | collective-permute-start | bytes 1966088 | tf_op jit(solution)/shard_map/ppermute | solution.py:100
  448.0 30.1 %collective-permute-start.62 = (bf16[4,64,2048]{2,1,0:T(8,128)(2,1)S(1)}, bf16[4,64,2048]{2,1,0:T(8,128)(2,1)S(1)}, u32[]{:S(2)}, u32[]{:S(2)}) collective-permute-start(bf16[4,64,2048]{2,1,0:T(8,128)(2,1)S(1)} %copy-done.183), channel_id=1, source_target_pairs={{0,16},{8,24},{16,0},{24,8},{1,17},{9,25},{17,1},{25,9},{2,18},{10... | collective-permute-start | bytes 3145736 | tf_op jit(solution)/shard_map/ppermute | solution.py:100
  478.0 46.7 %collective-permute-start.65 = (bf16[4,64,2048]{2,1,0:T(8,128)(2,1)S(1)}, bf16[4,64,2048]{2,1,0:T(8,128)(2,1)}, u32[]{:S(2)}, u32[]{:S(2)}) collective-permute-start(bf16[4,64,2048]{2,1,0:T(8,128)(2,1)S(1)} %add.227), channel_id=1, source_target_pairs={{0,16},{8,24},{16,0},{24,8},{1,17},{9,25},{17,1},{25,9},{2,18},{10... | collective-permute-start | bytes 3145736 | tf_op jit(solution)/shard_map/ppermute | solution.py:100
  480.0 44.7 %collective-permute-start.66 = (bf16[4,64,2048]{2,1,0:T(8,128)(2,1)S(1)}, bf16[4,64,2048]{2,1,0:T(8,128)(2,1)}, u32[]{:S(2)}, u32[]{:S(2)}) collective-permute-start(bf16[4,64,2048]{2,1,0:T(8,128)(2,1)S(1)} %add.228), channel_id=1, source_target_pairs={{0,8},{8,0},{16,24},{24,16},{1,9},{9,1},{17,25},{25,17},{2,10},{10... | collective-permute-start | bytes 3145736 | tf_op jit(solution)/shard_map/ppermute | solution.py:100
  524.7 29.8 %collective-permute-start.67 = (bf16[160,2048]{1,0:T(8,128)(2,1)S(1)}, bf16[160,2048]{1,0:T(8,128)(2,1)S(1)}, u32[]{:S(2)}, u32[]{:S(2)}) collective-permute-start(bf16[160,2048]{1,0:T(8,128)(2,1)S(1)} %get-tuple-element.305), channel_id=1, source_target_pairs={{0,4},{1,5},{2,6},{3,7},{4,0},{5,1},{6,2},{7,3},{8,12},{9,13},{10,... | collective-permute-start | bytes 1966088 | tf_op jit(solution)/shard_map/ppermute | solution.py:100
  638.3 37.8 %collective-permute-start.87 = (bf16[8,64,768]{2,1,0:T(8,128)(2,1)S(1)}, bf16[8,64,768]{2,1,0:T(8,128)(2,1)S(1)}, u32[]{:S(2)}, u32[]{:S(2)}) collective-permute-start(bf16[8,64,768]{2,1,0:T(8,128)(2,1)S(1)} %pad_maximum_fusion.22), channel_id=1, source_target_pairs={{0,16},{8,24},{16,0},{24,8},{1,17},{9,25},{17,1},{25,9},{2,18},{10... | collective-permute-start | bytes 2359304 | tf_op jit(solution)/shard_map/ppermute | solution.py:100
  646.5 29.6 %collective-permute-start.86 = (bf16[160,2048]{1,0:T(8,128)(2,1)S(1)}, bf16[160,2048]{1,0:T(8,128)(2,1)S(1)}, u32[]{:S(2)}, u32[]{:S(2)}) collective-permute-start(bf16[160,2048]{1,0:T(8,128)(2,1)S(1)} %get-tuple-element.339), channel_id=1, source_target_pairs={{0,6},{1,7},{2,0},{3,1},{4,2},{5,3},{6,4},{7,5},{8,14},{9,15},{10,... | collective-permute-start | bytes 1966088 | tf_op jit(solution)/shard_map/ppermute | solution.py:100
  678.6 32.1 %collective-permute-start.91 = (bf16[4,64,2048]{2,1,0:T(8,128)(2,1)S(1)}, bf16[4,64,2048]{2,1,0:T(8,128)(2,1)S(1)}, u32[]{:S(2)}, u32[]{:S(2)}) collective-permute-start(bf16[4,64,2048]{2,1,0:T(8,128)(2,1)S(1)} %pad_maximum_fusion.13), channel_id=1, source_target_pairs={{0,8},{8,0},{16,24},{24,16},{1,9},{9,1},{17,25},{25,17},{2,10},{10... | collective-permute-start | bytes 3145736 | tf_op jit(solution)/shard_map/ppermute | solution.py:100
  679.4 31.3 %collective-permute-start.92 = (bf16[4,64,2048]{2,1,0:T(8,128)(2,1)S(1)}, bf16[4,64,2048]{2,1,0:T(8,128)(2,1)S(1)}, u32[]{:S(2)}, u32[]{:S(2)}) collective-permute-start(bf16[4,64,2048]{2,1,0:T(8,128)(2,1)S(1)} %pad_maximum_fusion.14), channel_id=1, source_target_pairs={{0,16},{8,24},{16,0},{24,8},{1,17},{9,25},{17,1},{25,9},{2,18},{10... | collective-permute-start | bytes 3145736 | tf_op jit(solution)/shard_map/ppermute | solution.py:100
  680.2 30.5 %collective-permute-start.90 = (bf16[160,2048]{1,0:T(8,128)(2,1)S(1)}, bf16[160,2048]{1,0:T(8,128)(2,1)S(1)}, u32[]{:S(2)}, u32[]{:S(2)}) collective-permute-start(bf16[160,2048]{1,0:T(8,128)(2,1)S(1)} %get-tuple-element.347), channel_id=1, source_target_pairs={{0,4},{1,5},{2,6},{3,7},{4,0},{5,1},{6,2},{7,3},{8,12},{9,13},{10,... | collective-permute-start | bytes 1966088 | tf_op jit(solution)/shard_map/ppermute | solution.py:100
  (283 other events, 4683.3 us)

commit v4 on v3

--- a/solution.py
+++ b/solution.py
@@ -913,7 +913,7 @@
 
 
 def attend_back_kernel(
-    heads, width, q_ref, k_ref, v_ref, out_rows_ref, grad_ref, log_ref, cos_q, sin_q, cos_k, sin_k, key_place,
+    heads, width, q_ref, k_ref, v_ref, grad_ref, log_ref, cos_q, sin_q, cos_k, sin_k, key_place,
     query_place, query_start, out_ref, key_t, sum_k, sum_v, scores, grads, low_weights, low_grads,
 ):
     scale = width ** (-0.5)
@@ -932,15 +932,19 @@
     for h in range(heads):
         cut = slice(h * width, (h + 1) * width)
         query, grad = q_ref[:, cut], grad_ref[:, cut]
-        centre = jnp.sum((grad.astype(F32) * out_rows_ref[:, cut].astype(F32)).T, axis=0, keepdims=True)
+        centre = jnp.zeros((8, block), F32)
         scores[...] = dot(k_ref[:, cut], query, NT)
         grads[...] = dot(v_ref[:, cut], grad, NT)
         for keys in key_chunks(k_ref.shape[0]):
             mask = allowed(key_place[keys, :], query_place[...], query_start[...])
             part = scores[keys, :] * (scale * LOG2E) - log_ref[h : h + 1]
             weights = jnp.exp2(jnp.where(mask, part, NEGATIVE))
+            scores[keys, :] = weights
             low_weights[keys, :] = weights.astype(BF16)
-            low_grads[keys, :] = (weights * (grads[keys, :] - centre)).astype(BF16)
+            centre = centre + jnp.sum((weights * grads[keys, :]).reshape(-1, 8, block), axis=0)
+        centre = jnp.sum(centre, axis=0, keepdims=True)
+        for keys in key_chunks(k_ref.shape[0]):
+            low_grads[keys, :] = (scores[keys, :] * (grads[keys, :] - centre)).astype(BF16)
         sum_v[:, cut] += dot(low_weights[...], grad)
         sum_k[:, cut] += dot(low_grads[...], query)
         grad_query = (dot(key_t[cut, :], low_grads[...]) * scale).T
@@ -1001,7 +1005,7 @@
     )(qkv, qkv, qkv, cosine, sine, cosine, sine, key_place, place[None], start[None])
 
 
-def attention_back(qkv, rot_q, rot_k, attended, grad, logs, cosine, sine, place, start, heads):
+def attention_back(qkv, rot_q, rot_k, grad, logs, cosine, sine, place, start, heads):
     tokens, width = rot_q.shape
     head_width = width // heads
     block = 256 if tokens % 256 == 0 else tokens
@@ -1016,7 +1020,6 @@
             pl.BlockSpec((block, width), row),
             pl.BlockSpec((tokens, width), whole),
             pl.BlockSpec((tokens, width), lambda i: (0, 2)),
-            pl.BlockSpec((block, width), row),
             pl.BlockSpec((block, width), row),
             pl.BlockSpec((heads, block), along),
             pl.BlockSpec((block, head_width), row),
@@ -1040,7 +1043,7 @@
         ],
         compiler_params=params(56),
         cost_estimate=NO_COST,
-    )(rot_q, rot_k, qkv, attended, grad, logs, cosine, sine, cosine, sine, key_place, place[None], start[None])
+    )(rot_q, rot_k, qkv, grad, logs, cosine, sine, cosine, sine, key_place, place[None], start[None])
 
 
 def sequence_places(ordering, lengths):
@@ -1235,7 +1238,7 @@
     hold(*output_blocks[0])
     grad_attended = product(other_branch, output_weight, NT, into=1, filled=(grad_mine,))
     hold(grad_attended)
-    grad_qkv = attention_back(qkv, rot_q, rot_k, attended, grad_attended, logs, cosine, sine, place, start, heads)
+    grad_qkv = attention_back(qkv, rot_q, rot_k, grad_attended, logs, cosine, sine, place, start, heads)
     theirs = product((grad_qkv, 1), attention_weight, NT)
     run(recut_grad, gather_down_rows)
     hold(theirs)

time: 817 us -> 816 us (level)
    unnamed x394 -> x392, local copies, waits for them, and re-layouts: 31.4 us -> 31.4 us
  transfers between devices with their start and end apart: 118 -> 118, of which waited for: 52 -> 52; matrix products, arithmetic and copies ran while one was open for 9% -> 9% of each run, Pallas kernels for 27% -> 28%
where the time goes in v4:
time: 816 us; the launch traced here: 810 us
  waiting for transfers between devices  340 us (42%)
  Pallas kernels  226 us (28%)
  starting transfers between devices  137 us (17%)
  local copies, waits for them, and re-layouts  59.4 us (7%)
  other arithmetic  41.6 us (5%)
    ppermute x118, waiting for transfers between devices, sender(): return lambda x: lax.ppermute(x, axis, pairs)  340 us
    ppermute x118, starting transfers between devices, sender(): return lambda x: lax.ppermute(x, axis, pairs)  137 us
    pallas_call x6, Pallas kernels, token_call(): pl.pallas_call(kernel, grid=(tokens // block,), in_specs=[spec(o.shape) f...  55.1 us
    pallas_call x10, Pallas kernels, product(): pl.pallas_call(functools.partial(product_kernel, dims, add is not None),...  41.5 us
    unnamed x392, local copies, waits for them, and re-layouts  31.4 us
    pallas_call x2, Pallas kernels, columns_product(): pl.pallas_call(functools.partial(columns_product_kernel, units, reps), gr...  28.1 us
    pallas_call x6, Pallas kernels, join(): pl.pallas_call(functools.partial(columns_kernel, len(units), reps, parts)...  23.2 us
    pallas_call x2, Pallas kernels, ffn_forward(): pl.pallas_call(ffn_kernel, grid=(tiles,), in_specs=[pl.BlockSpec((rows, w...  17.3 us
  transfers between devices with their start and end apart: 118, of which 52 were waited for; matrix products, arithmetic and copies ran while one was open for 9% of the time, Pallas kernels for 28%

profile of v4, /device:TPU:0, one launch (start us, length us, event | category | flops | bytes accessed | tf_op | source)
XLA Modules:
  0.0 809.8 jit_solution(17393879969567997586)
XLA Ops:
  19.0 11.5 %shard_map.213 = (bf16[160,2048]{1,0:T(8,128)(2,1)S(1)}, f32[4,160,128]{2,1,0:T(8,128)S(1)}, bf16[4,160,2048]{2,1,0:T(8,128)(2,1)S(1)}) custom-call(bf16[160,4,2048]{2,1,0:T(4,128)(2,1)S(1)} %copy-done.49, bf16[128,2048]{1,0:T(8,128)(2,1)S(1)} %get-tuple-element.501.weight_ref.weight_rows_ref, f32[4,128]{1,0:T(4,128)S(1)} %get-tuple-element.576.static_ref.static_first_ref), custom_call_target="tpu_custom_call" | custom-call | tf_op jit(solution)/shard_map/pallas_call | solution.py:652
  68.7 9.7 %collective-permute-done.14 = bf16[8,64,768]{2,1,0:T(8,128)(2,1)S(1)} collective-permute-done((bf16[8,64,768]{2,1,0:T(8,128)(2,1)S(1)}, bf16[8,64,768]{2,1,0:T(8,128)(2,1)S(1)}, u32[]{:S(2)}, u32[]{:S(2)}) %collective-permute-start.14) | collective-permute-done | bytes 786464 | tf_op jit(solution)/shard_map/ppermute | solution.py:100
  91.5 12.6 %collective-permute-done.17.refs_5_ = bf16[224,2048]{1,0:T(8,128)(2,1)} collective-permute-done((bf16[224,2048]{1,0:T(8,128)(2,1)}, bf16[224,2048]{1,0:T(8,128)(2,1)}, u32[]{:S(2)}, u32[]{:S(2)}) %collective-permute-start.17) | collective-permute-done | bytes 917536 | tf_op jit(solution)/shard_map/ppermute | solution.py:100
  137.0 9.9 %shard_map.218 = (bf16[1280,256]{1,0:T(8,128)(2,1)S(1)}, bf16[1280,256]{1,0:T(8,128)(2,1)S(1)}, bf16[1280,256]{1,0:T(8,128)(2,1)S(1)}, f32[2,1280]{1,0:T(2,128)S(1)}) custom-call(bf16[1280,768]{1,0:T(8,128)(2,1)} %copy-done.5, bf16[1280,768]{1,0:T(8,128)(2,1)} %copy-done.5, bf16[1280,768]{1,0:T(8,128)(2,1)} %copy-done.5, ...), custom_call_target="tpu_custom_call" | custom-call | tf_op jit(solution)/shard_map/pallas_call | solution.py:973
  202.6 14.4 %collective-permute-done.35 = bf16[160,2048]{1,0:T(8,128)(2,1)S(1)} collective-permute-done((bf16[160,2048]{1,0:T(8,128)(2,1)S(1)}, bf16[160,2048]{1,0:T(8,128)(2,1)S(1)}, u32[]{:S(2)}, u32[]{:S(2)}) %collective-permute-start.35) | collective-permute-done | bytes 655392 | tf_op jit(solution)/shard_map/ppermute | solution.py:100
  216.9 16.9 %collective-permute-done.36 = bf16[160,2048]{1,0:T(8,128)(2,1)S(1)} collective-permute-done((bf16[160,2048]{1,0:T(8,128)(2,1)S(1)}, bf16[160,2048]{1,0:T(8,128)(2,1)S(1)}, u32[]{:S(2)}, u32[]{:S(2)}) %collective-permute-start.36) | collective-permute-done | bytes 655392 | tf_op jit(solution)/shard_map/ppermute | solution.py:100
  236.1 24.8 %collective-permute-done.39 = bf16[160,2048]{1,0:T(8,128)(2,1)S(1)} collective-permute-done((bf16[160,2048]{1,0:T(8,128)(2,1)S(1)}, bf16[160,2048]{1,0:T(8,128)(2,1)S(1)}, u32[]{:S(2)}, u32[]{:S(2)}) %collective-permute-start.39) | collective-permute-done | bytes 655392 | tf_op jit(solution)/shard_map/ppermute | solution.py:100
  270.7 14.6 %collective-permute-done.45 = bf16[160,2048]{1,0:T(8,128)(2,1)S(1)} collective-permute-done((bf16[160,2048]{1,0:T(8,128)(2,1)}, bf16[160,2048]{1,0:T(8,128)(2,1)S(1)}, u32[]{:S(2)}, u32[]{:S(2)}) %collective-permute-start.45) | collective-permute-done | bytes 655392 | tf_op jit(solution)/shard_map/ppermute | solution.py:100
  285.2 11.2 %collective-permute-done.46 = bf16[160,2048]{1,0:T(8,128)(2,1)S(1)} collective-permute-done((bf16[160,2048]{1,0:T(8,128)(2,1)}, bf16[160,2048]{1,0:T(8,128)(2,1)S(1)}, u32[]{:S(2)}, u32[]{:S(2)}) %collective-permute-start.46) | collective-permute-done | bytes 655392 | tf_op jit(solution)/shard_map/ppermute | solution.py:100
  369.1 10.5 %shard_map.230 = (bf16[128,2048]{1,0:T(8,128)(2,1)S(1)}, bf16[128,2048]{1,0:T(8,128)(2,1)S(1)}, bf16[128,2048]{1,0:T(8,128)(2,1)S(1)}, bf16[128,2048]{1,0:T(8,12...) custom-call(s32[1]{0:T(128)} %bitcast.23.me_ref, ...), custom_call_target="tpu_custom_call" | custom-call | tf_op jit(solution)/shard_map/pallas_call | solution.py:768
  392.8 19.3 %shard_map.232 = (bf16[4,64,2048]{2,1,0:T(8,128)(2,1)S(1)}, bf16[4,64,2048]{2,1,0:T(8,128)(2,1)S(1)}, bf16[4,64,2048]{2,1,0:T(8,128)(2,1)S(1)}, bf16[4,64,2048]{...) custom-call(s32[1]{0:T(128)} %bitcast.23.me_ref, ...), custom_call_target="tpu_custom_call" | custom-call | tf_op jit(solution)/shard_map/pallas_call | solution.py:732
  420.0 15.6 %collective-permute-done.56.refs_5_ = bf16[160,2048]{1,0:T(8,128)(2,1)S(1)} collective-permute-done((bf16[160,2048]{1,0:T(8,128)(2,1)S(1)}, bf16[160,2048]{1,0:T(8,128)(2,1)S(1)}, u32[]{:S(2)}, u32[]{:S(2)}) %collective-permute-start.56) | collective-permute-done | bytes 655392 | tf_op jit(solution)/shard_map/ppermute | solution.py:100
  435.6 10.7 %collective-permute-done.57.refs_6_ = bf16[160,2048]{1,0:T(8,128)(2,1)S(1)} collective-permute-done((bf16[160,2048]{1,0:T(8,128)(2,1)S(1)}, bf16[160,2048]{1,0:T(8,128)(2,1)S(1)}, u32[]{:S(2)}, u32[]{:S(2)}) %collective-permute-start.57) | collective-permute-done | bytes 655392 | tf_op jit(solution)/shard_map/ppermute | solution.py:100
  451.0 19.0 %collective-permute-done.61 = bf16[4,64,2048]{2,1,0:T(8,128)(2,1)S(1)} collective-permute-done((bf16[4,64,2048]{2,1,0:T(8,128)(2,1)S(1)}, bf16[4,64,2048]{2,1,0:T(8,128)(2,1)S(1)}, u32[]{:S(2)}, u32[]{:S(2)}) %collective-permute-start.61) | collective-permute-done | bytes 1048608 | tf_op jit(solution)/shard_map/ppermute | solution.py:100
  481.1 14.0 %shard_map.233 = (f32[4,160,2048]{2,1,0:T(8,128)}, bf16[160,2048]{1,0:T(8,128)(2,1)S(1)}, f32[160,128]{1,0:T(8,128)S(1)}, f32[128,2048]{1,0:T(8,128)S(1)}, f32[8,128]{1,0:T(8,128)S(1)}) custom-call(f32[4,160,2048]{2,1,0:T(8,128)} %copy-done.14, f32[4,160,128]{2,1,0:T(8,128)S(1)} %copy-done.77, f32[4,128]{1,0:T(4,128)S(1)} %copy-done.120, ...), custom_call_target="tpu_custom_call" | custom-call | tf_op jit(solution)/shard_map/pallas_call | solution.py:652
  500.3 14.4 %collective-permute-done.63 = bf16[160,2048]{1,0:T(8,128)(2,1)S(1)} collective-permute-done((bf16[160,2048]{1,0:T(8,128)(2,1)S(1)}, bf16[160,2048]{1,0:T(8,128)(2,1)S(1)}, u32[]{:S(2)}, u32[]{:S(2)}) %collective-permute-start.63) | collective-permute-done | bytes 655392 | tf_op jit(solution)/shard_map/ppermute | solution.py:100
  514.6 10.2 %collective-permute-done.64 = bf16[160,2048]{1,0:T(8,128)(2,1)S(1)} collective-permute-done((bf16[160,2048]{1,0:T(8,128)(2,1)S(1)}, bf16[160,2048]{1,0:T(8,128)(2,1)S(1)}, u32[]{:S(2)}, u32[]{:S(2)}) %collective-permute-start.64) | collective-permute-done | bytes 655392 | tf_op jit(solution)/shard_map/ppermute | solution.py:100
  537.1 17.7 %collective-permute-done.67 = bf16[160,2048]{1,0:T(8,128)(2,1)S(1)} collective-permute-done((bf16[160,2048]{1,0:T(8,128)(2,1)S(1)}, bf16[160,2048]{1,0:T(8,128)(2,1)S(1)}, u32[]{:S(2)}, u32[]{:S(2)}) %collective-permute-start.67) | collective-permute-done | bytes 655392 | tf_op jit(solution)/shard_map/ppermute | solution.py:100
  585.6 16.7 %shard_map.237.y0.y1.a_ref = bf16[1280,768]{1,0:T(8,128)(2,1)} custom-call(bf16[1280,256]{1,0:T(8,128)(2,1)} %copy-done.84, bf16[1280,256]{1,0:T(8,128)(2,1)} %copy-done.85, bf16[1280,768]{1,0:T(8,128)(2,1)} %copy-done.5, bf16[1280,256]{1,0:T(8,128)(2,1)} %copy-done.36, f32[2,1280]{1,0:T(2,128)} %copy-done.123, f32[1280,128]{1,0:T(8,128)} %copy-done.15, ...), custom_call_target="tpu_custom_call" | custom-call | tf_op jit(solution)/shard_map/pallas_call | solution.py:1016
  662.8 12.6 %collective-permute-done.86.refs_2_ = bf16[160,2048]{1,0:T(8,128)(2,1)S(1)} collective-permute-done((bf16[160,2048]{1,0:T(8,128)(2,1)S(1)}, bf16[160,2048]{1,0:T(8,128)(2,1)S(1)}, u32[]{:S(2)}, u32[]{:S(2)}) %collective-permute-start.86) | collective-permute-done | bytes 655392 | tf_op jit(solution)/shard_map/ppermute | solution.py:100
  689.7 20.4 %collective-permute-done.90.refs_3_ = bf16[160,2048]{1,0:T(8,128)(2,1)S(1)} collective-permute-done((bf16[160,2048]{1,0:T(8,128)(2,1)S(1)}, bf16[160,2048]{1,0:T(8,128)(2,1)S(1)}, u32[]{:S(2)}, u32[]{:S(2)}) %collective-permute-start.90) | collective-permute-done | bytes 655392 | tf_op jit(solution)/shard_map/ppermute | solution.py:100
  716.4 10.9 %collective-permute-done.96 = bf16[32,2048]{1,0:T(8,128)(2,1)S(1)} collective-permute-done((bf16[32,2048]{1,0:T(8,128)(2,1)S(1)}, bf16[32,2048]{1,0:T(8,128)(2,1)S(1)}, u32[]{:S(2)}, u32[]{:S(2)}) %collective-permute-start.96) | collective-permute-done | bytes 131104 | tf_op jit(solution)/shard_map/ppermute | solution.py:100
  739.1 12.3 %shard_map.242 = (f32[160,4,2048]{2,1,0:T(4,128)}, f32[128,2048]{1,0:T(8,128)S(1)}, f32[8,128]{1,0:T(8,128)S(1)}) custom-call(bf16[4,160,2048]{2,1,0:T(8,128)(2,1)S(1)} %copy-done.26, f32[4,160,128]{2,1,0:T(8,128)S(1)} %get-tuple-element.213.packed_ref.packed_first_ref, f32[4,128]{1,0:T(4,128)S(1)} %copy-done.116, f32[4,160,2048]{2,1,0:T(8,128)S(1)} %bitcast.145, ...), custom_call_target="tpu_custom_call" | custom-call | tf_op jit(solution)/shard_map/pallas_call | solution.py:652
  783.3 12.0 %shard_map.244 = (f32[256,8192]{1,0:T(8,128)}, f32[256,8192]{1,0:T(8,128)}) custom-call(s32[2]{0:T(128)} %copy-done.121, bf16[2,64,2048]{2,1,0:T(8,128)(2,1)} %copy-done.139, bf16[2,64,2048]{2,1,0:T(8,128)(2,1)} %get-tuple-element.383.refs_1_, bf16[2,64,2048]{2,1,0:T(8,128)(2,1)} %copy-done.147, bf16[2,64,2048]{2,1,0:T(8,128)(2,1)} %get-tuple-element.385.refs_3_, ...), custom_call_target="tpu_custom_call" | custom-call | tf_op jit(solution)/shard_map/pallas_call | solution.py:317
  (809 shorter events, 463.4 us)
Async XLA Ops:
  195.6 38.2 %collective-permute-start.37 = (bf16[4,64,2048]{2,1,0:T(8,128)(2,1)S(1)}, bf16[4,64,2048]{2,1,0:T(8,128)(2,1)S(1)}, u32[]{:S(2)}, u32[]{:S(2)}) collective-permute-start(bf16[4,64,2048]{2,1,0:T(8,128)(2,1)S(1)} %pad_maximum_fusion.4), channel_id=1, source_target_pairs={{0,8},{8,0},{16,24},{24,16},{1,9},{9,1},{17,25},{25,17},{2,10},{10... | collective-permute-start | bytes 3145736 | tf_op jit(solution)/shard_map/ppermute | solution.py:100
  197.1 36.7 %collective-permute-start.38 = (bf16[4,64,2048]{2,1,0:T(8,128)(2,1)S(1)}, bf16[4,64,2048]{2,1,0:T(8,128)(2,1)S(1)}, u32[]{:S(2)}, u32[]{:S(2)}) collective-permute-start(bf16[4,64,2048]{2,1,0:T(8,128)(2,1)S(1)} %pad_maximum_fusion.5), channel_id=1, source_target_pairs={{0,16},{8,24},{16,0},{24,8},{1,17},{9,25},{17,1},{25,9},{2,18},{10... | collective-permute-start | bytes 3145736 | tf_op jit(solution)/shard_map/ppermute | solution.py:100
  199.6 34.2 %collective-permute-start.36 = (bf16[160,2048]{1,0:T(8,128)(2,1)S(1)}, bf16[160,2048]{1,0:T(8,128)(2,1)S(1)}, u32[]{:S(2)}, u32[]{:S(2)}) collective-permute-start(bf16[160,2048]{1,0:T(8,128)(2,1)S(1)} %get-tuple-element.254), channel_id=1, source_target_pairs={{0,2},{1,3},{2,4},{3,5},{4,6},{5,7},{6,0},{7,1},{8,10},{9,11},{10,... | collective-permute-start | bytes 1966088 | tf_op jit(solution)/shard_map/ppermute | solution.py:100
  261.1 35.3 %collective-permute-start.42 = (bf16[640,2048]{1,0:T(8,128)(2,1)S(1)}, bf16[640,2048]{1,0:T(8,128)(2,1)S(1)}, u32[]{:S(2)}, u32[]{:S(2)}) collective-permute-start(bf16[640,2048]{1,0:T(8,128)(2,1)S(1)} %constant_dynamic-update-slice_fusion.5.x_ref.x0), channel_id=1, source_target_pairs={{0,1},{1,0},{2,3},{3,2},{4,5},{5,4},{6,7},{7,6},{8,9},{9,8},{10,11... | collective-permute-start | bytes 7864328 | tf_op jit(solution)/shard_map/ppermute | solution.py:100
  261.4 35.0 %collective-permute-start.43 = (bf16[4,64,2048]{2,1,0:T(8,128)(2,1)S(1)}, bf16[4,64,2048]{2,1,0:T(8,128)(2,1)S(1)}, u32[]{:S(2)}, u32[]{:S(2)}) collective-permute-start(bf16[4,64,2048]{2,1,0:T(8,128)(2,1)S(1)} %pad_maximum_fusion.6), channel_id=1, source_target_pairs={{0,8},{8,0},{16,24},{24,16},{1,9},{9,1},{17,25},{25,17},{2,10},{10... | collective-permute-start | bytes 3145736 | tf_op jit(solution)/shard_map/ppermute | solution.py:100
  262.4 34.0 %collective-permute-start.44 = (bf16[4,64,2048]{2,1,0:T(8,128)(2,1)S(1)}, bf16[4,64,2048]{2,1,0:T(8,128)(2,1)S(1)}, u32[]{:S(2)}, u32[]{:S(2)}) collective-permute-start(bf16[4,64,2048]{2,1,0:T(8,128)(2,1)S(1)} %pad_maximum_fusion.7), channel_id=1, source_target_pairs={{0,16},{8,24},{16,0},{24,8},{1,17},{9,25},{17,1},{25,9},{2,18},{10... | collective-permute-start | bytes 3145736 | tf_op jit(solution)/shard_map/ppermute | solution.py:100
  265.6 30.8 %collective-permute-start.46 = (bf16[160,2048]{1,0:T(8,128)(2,1)}, bf16[160,2048]{1,0:T(8,128)(2,1)S(1)}, u32[]{:S(2)}, u32[]{:S(2)}) collective-permute-start(bf16[160,2048]{1,0:T(8,128)(2,1)} %get-tuple-element.266), channel_id=1, source_target_pairs={{0,6},{1,7},{2,0},{3,1},{4,2},{5,3},{6,4},{7,5},{8,14},{9,15},{10,... | collective-permute-start | bytes 1966088 | tf_op jit(solution)/shard_map/ppermute | solution.py:100
  296.5 31.0 %collective-permute-start.47 = (bf16[160,2048]{1,0:T(8,128)(2,1)}, bf16[160,2048]{1,0:T(8,128)(2,1)}, u32[]{:S(2)}, u32[]{:S(2)}) collective-permute-start(bf16[160,2048]{1,0:T(8,128)(2,1)} %get-tuple-element.266), channel_id=1, source_target_pairs={{0,4},{1,5},{2,6},{3,7},{4,0},{5,1},{6,2},{7,3},{8,12},{9,13},{10,... | collective-permute-start | bytes 1966088 | tf_op jit(solution)/shard_map/ppermute | solution.py:100
  341.4 38.2 %collective-permute-start.50 = (bf16[160,2048]{1,0:T(8,128)(2,1)}, bf16[160,2048]{1,0:T(8,128)(2,1)}, u32[]{:S(2)}, u32[]{:S(2)}) collective-permute-start(bf16[160,2048]{1,0:T(8,128)(2,1)} %get-tuple-element.269), channel_id=1, source_target_pairs={{0,2},{1,3},{2,4},{3,5},{4,6},{5,7},{6,0},{7,1},{8,10},{9,11},{10,... | collective-permute-start | bytes 1966088 | tf_op jit(solution)/shard_map/ppermute | solution.py:100
  341.4 38.2 %collective-permute-start.51 = (bf16[160,2048]{1,0:T(8,128)(2,1)}, bf16[160,2048]{1,0:T(8,128)(2,1)}, u32[]{:S(2)}, u32[]{:S(2)}) collective-permute-start(bf16[160,2048]{1,0:T(8,128)(2,1)} %get-tuple-element.270), channel_id=1, source_target_pairs={{0,6},{1,7},{2,0},{3,1},{4,2},{5,3},{6,4},{7,5},{8,14},{9,15},{10,... | collective-permute-start | bytes 1966088 | tf_op jit(solution)/shard_map/ppermute | solution.py:100
  382.2 31.5 %collective-permute-start.54 = (bf16[256,2048]{1,0:T(8,128)(2,1)}, bf16[256,2048]{1,0:T(8,128)(2,1)}, u32[]{:S(2)}, u32[]{:S(2)}) collective-permute-start(bf16[256,2048]{1,0:T(8,128)(2,1)} %pad_maximum_fusion.8), channel_id=1, source_target_pairs={{0,8},{8,0},{16,24},{24,16},{1,9},{9,1},{17,25},{25,17},{2,10},{10... | collective-permute-start | bytes 3145736 | tf_op jit(solution)/shard_map/ppermute | solution.py:100
  383.7 30.0 %collective-permute-start.55 = (bf16[256,2048]{1,0:T(8,128)(2,1)}, bf16[256,2048]{1,0:T(8,128)(2,1)}, u32[]{:S(2)}, u32[]{:S(2)}) collective-permute-start(bf16[256,2048]{1,0:T(8,128)(2,1)} %pad_maximum_fusion.9), channel_id=1, source_target_pairs={{0,16},{8,24},{16,0},{24,8},{1,17},{9,25},{17,1},{25,9},{2,18},{10... | collective-permute-start | bytes 3145736 | tf_op jit(solution)/shard_map/ppermute | solution.py:100
  413.7 32.7 %collective-permute-start.58 = (bf16[4,64,2048]{2,1,0:T(8,128)(2,1)S(1)}, bf16[4,64,2048]{2,1,0:T(8,128)(2,1)S(1)}, u32[]{:S(2)}, u32[]{:S(2)}) collective-permute-start(bf16[4,64,2048]{2,1,0:T(8,128)(2,1)S(1)} %get-tuple-element.287), channel_id=1, source_target_pairs={{0,8},{8,0},{16,24},{24,16},{1,9},{9,1},{17,25},{25,17},{2,10},{10... | collective-permute-start | bytes 3145736 | tf_op jit(solution)/shard_map/ppermute | solution.py:100
  414.6 31.7 %collective-permute-start.59 = (bf16[4,64,2048]{2,1,0:T(8,128)(2,1)}, bf16[4,64,2048]{2,1,0:T(8,128)(2,1)S(1)}, u32[]{:S(2)}, u32[]{:S(2)}) collective-permute-start(bf16[4,64,2048]{2,1,0:T(8,128)(2,1)} %get-tuple-element.289), channel_id=1, source_target_pairs={{0,16},{8,24},{16,0},{24,8},{1,17},{9,25},{17,1},{25,9},{2,18},{10... | collective-permute-start | bytes 3145736 | tf_op jit(solution)/shard_map/ppermute | solution.py:100
  416.2 30.2 %collective-permute-start.57 = (bf16[160,2048]{1,0:T(8,128)(2,1)S(1)}, bf16[160,2048]{1,0:T(8,128)(2,1)S(1)}, u32[]{:S(2)}, u32[]{:S(2)}) collective-permute-start(bf16[160,2048]{1,0:T(8,128)(2,1)S(1)} %get-tuple-element.284), channel_id=1, source_target_pairs={{0,6},{1,7},{2,0},{3,1},{4,2},{5,3},{6,4},{7,5},{8,14},{9,15},{10,... | collective-permute-start | bytes 1966088 | tf_op jit(solution)/shard_map/ppermute | solution.py:100
  447.9 30.1 %collective-permute-start.62 = (bf16[4,64,2048]{2,1,0:T(8,128)(2,1)S(1)}, bf16[4,64,2048]{2,1,0:T(8,128)(2,1)S(1)}, u32[]{:S(2)}, u32[]{:S(2)}) collective-permute-start(bf16[4,64,2048]{2,1,0:T(8,128)(2,1)S(1)} %copy-done.182), channel_id=1, source_target_pairs={{0,16},{8,24},{16,0},{24,8},{1,17},{9,25},{17,1},{25,9},{2,18},{10... | collective-permute-start | bytes 3145736 | tf_op jit(solution)/shard_map/ppermute | solution.py:100
  478.0 46.8 %collective-permute-start.65 = (bf16[4,64,2048]{2,1,0:T(8,128)(2,1)S(1)}, bf16[4,64,2048]{2,1,0:T(8,128)(2,1)}, u32[]{:S(2)}, u32[]{:S(2)}) collective-permute-start(bf16[4,64,2048]{2,1,0:T(8,128)(2,1)S(1)} %add.227), channel_id=1, source_target_pairs={{0,16},{8,24},{16,0},{24,8},{1,17},{9,25},{17,1},{25,9},{2,18},{10... | collective-permute-start | bytes 3145736 | tf_op jit(solution)/shard_map/ppermute | solution.py:100
  479.9 44.9 %collective-permute-start.66 = (bf16[4,64,2048]{2,1,0:T(8,128)(2,1)S(1)}, bf16[4,64,2048]{2,1,0:T(8,128)(2,1)}, u32[]{:S(2)}, u32[]{:S(2)}) collective-permute-start(bf16[4,64,2048]{2,1,0:T(8,128)(2,1)S(1)} %add.228), channel_id=1, source_target_pairs={{0,8},{8,0},{16,24},{24,16},{1,9},{9,1},{17,25},{25,17},{2,10},{10... | collective-permute-start | bytes 3145736 | tf_op jit(solution)/shard_map/ppermute | solution.py:100
  524.8 30.0 %collective-permute-start.67 = (bf16[160,2048]{1,0:T(8,128)(2,1)S(1)}, bf16[160,2048]{1,0:T(8,128)(2,1)S(1)}, u32[]{:S(2)}, u32[]{:S(2)}) collective-permute-start(bf16[160,2048]{1,0:T(8,128)(2,1)S(1)} %get-tuple-element.305), channel_id=1, source_target_pairs={{0,4},{1,5},{2,6},{3,7},{4,0},{5,1},{6,2},{7,3},{8,12},{9,13},{10,... | collective-permute-start | bytes 1966088 | tf_op jit(solution)/shard_map/ppermute | solution.py:100
  637.2 38.3 %collective-permute-start.87 = (bf16[8,64,768]{2,1,0:T(8,128)(2,1)S(1)}, bf16[8,64,768]{2,1,0:T(8,128)(2,1)S(1)}, u32[]{:S(2)}, u32[]{:S(2)}) collective-permute-start(bf16[8,64,768]{2,1,0:T(8,128)(2,1)S(1)} %pad_maximum_fusion.22), channel_id=1, source_target_pairs={{0,16},{8,24},{16,0},{24,8},{1,17},{9,25},{17,1},{25,9},{2,18},{10... | collective-permute-start | bytes 2359304 | tf_op jit(solution)/shard_map/ppermute | solution.py:100
  645.6 29.8 %collective-permute-start.86 = (bf16[160,2048]{1,0:T(8,128)(2,1)S(1)}, bf16[160,2048]{1,0:T(8,128)(2,1)S(1)}, u32[]{:S(2)}, u32[]{:S(2)}) collective-permute-start(bf16[160,2048]{1,0:T(8,128)(2,1)S(1)} %get-tuple-element.339), channel_id=1, source_target_pairs={{0,6},{1,7},{2,0},{3,1},{4,2},{5,3},{6,4},{7,5},{8,14},{9,15},{10,... | collective-permute-start | bytes 1966088 | tf_op jit(solution)/shard_map/ppermute | solution.py:100
  677.7 32.5 %collective-permute-start.91 = (bf16[4,64,2048]{2,1,0:T(8,128)(2,1)S(1)}, bf16[4,64,2048]{2,1,0:T(8,128)(2,1)S(1)}, u32[]{:S(2)}, u32[]{:S(2)}) collective-permute-start(bf16[4,64,2048]{2,1,0:T(8,128)(2,1)S(1)} %pad_maximum_fusion.13), channel_id=1, source_target_pairs={{0,8},{8,0},{16,24},{24,16},{1,9},{9,1},{17,25},{25,17},{2,10},{10... | collective-permute-start | bytes 3145736 | tf_op jit(solution)/shard_map/ppermute | solution.py:100
  678.6 31.6 %collective-permute-start.92 = (bf16[4,64,2048]{2,1,0:T(8,128)(2,1)S(1)}, bf16[4,64,2048]{2,1,0:T(8,128)(2,1)S(1)}, u32[]{:S(2)}, u32[]{:S(2)}) collective-permute-start(bf16[4,64,2048]{2,1,0:T(8,128)(2,1)S(1)} %pad_maximum_fusion.14), channel_id=1, source_target_pairs={{0,16},{8,24},{16,0},{24,8},{1,17},{9,25},{17,1},{25,9},{2,18},{10... | collective-permute-start | bytes 3145736 | tf_op jit(solution)/shard_map/ppermute | solution.py:100
  679.6 30.5 %collective-permute-start.90 = (bf16[160,2048]{1,0:T(8,128)(2,1)S(1)}, bf16[160,2048]{1,0:T(8,128)(2,1)S(1)}, u32[]{:S(2)}, u32[]{:S(2)}) collective-permute-start(bf16[160,2048]{1,0:T(8,128)(2,1)S(1)} %get-tuple-element.347), channel_id=1, source_target_pairs={{0,4},{1,5},{2,6},{3,7},{4,0},{5,1},{6,2},{7,3},{8,12},{9,13},{10,... | collective-permute-start | bytes 1966088 | tf_op jit(solution)/shard_map/ppermute | solution.py:100
  (282 other events, 4668.2 us)
